TPU v7x, 32 devices: a whole 2x2x4 slice. The times are simulated.
32 devices in a mesh: seq: 8 (over y, x, core), mp: 4 (over z).
Axes of the slice: x: 2, y: 2, z: 4, core: 2. Of those that a mesh axis runs over, the one named last changes fastest.
Arguments:
- tokens: float32 [8192, 2, 2048], P(('seq', 'mp')), may hold values from -6 to 6
- norm1_gain: float32 [2048], replicated, may hold values from 0.5 to 1.5
- w_mix_in: bfloat16 [2048, 4, 2048], P(None, None, 'mp'), may hold values from -0.125 to 0.125
- forget_gap: float32 [16, 128], P('mp'), may hold values from 0.00012207031 to 0.1
- group_gain: float32 [16, 128], P('mp'), may hold values from 0.5 to 1.5
- w_mix_out: bfloat16 [16, 128, 2048], replicated, may hold values from -0.125 to 0.125
- norm2_gain: float32 [2048], replicated, may hold values from 0.5 to 1.5
- w_gate_up: bfloat16 [2048, 2, 5632], P(None, None, 'mp'), may hold values from -0.125 to 0.125
- w_down: bfloat16 [5632, 2048], P('mp'), may hold values from -0.078125 to 0.078125
- doc_lengths: int32 [2, 4], replicated, may hold values from 1 to 7169, 8192 in all within a row
- out_cotangent: float32 [8192, 2, 2048], P('seq'), may hold values from -6 to 6
Outputs:
- layer_out: float32 [8192, 2, 2048], P(('seq', 'mp'))
- tokens_grad: float32 [8192, 2, 2048], P(('seq', 'mp'))
- norm1_gain_grad: float32 [2048], P(('seq', 'mp'))
- w_mix_in_grad: float32 [2048, 4, 2048], P('seq', None, 'mp')
- forget_gap_grad: float32 [16, 128], P('mp', 'seq')
- group_gain_grad: float32 [16, 128], P('mp', 'seq')
- w_mix_out_grad: float32 [16, 128, 2048], P('mp', 'seq')
- norm2_gain_grad: float32 [2048], P(('seq', 'mp'))
- w_gate_up_grad: float32 [2048, 2, 5632], P('seq', None, 'mp')
- w_down_grad: float32 [5632, 2048], P('mp', 'seq')
Inputs may be any that keep to these rules, and one draw needn't show every extreme that they name: `doc_lengths`: in each pack the 4 lengths add up to 8192, and the longest is exactly 7169.
All inputs are finite; a program needn't handle non-finite values.
Results may differ from a plain program's by a relative error of at most 0.025.
The roundings to bfloat16 on the way count: a program that leaves them out, or rounds other values in their place, can miss the bound.
Values may be sent and summed in bfloat16 or wider, within the bound.
A program may use at most 384 MiB of HBM per device.

v0:
```python
import jax
import jax.numpy as jnp
from jax import lax
from jax.sharding import PartitionSpec as P

BLOCK = 128


EPSILON = 1e-06
PRECISE = lax.Precision.HIGHEST


def entering(x, axis, combine, identity, reverse):
    length, index = (lax.axis_size(axis), lax.axis_index(axis))
    everything = jax.tree.map(
        lambda part, kind: lax.all_gather(part.astype(kind), axis), x, (jnp.bfloat16, jnp.bfloat16)
    )
    start = jax.tree.map(
        lambda part, zero: jnp.broadcast_to(jnp.asarray(zero, part.dtype), part.shape), x, identity
    )

    def turn(k, before):
        at = length - 1 - k if reverse else k
        reached = at > index if reverse else at < index
        new = combine(
            before, jax.tree.map(lambda part, own: part[at].astype(own.dtype), everything, x)
        )
        return jax.tree.map(lambda a, b: jnp.where(reached, a, b), new, before)

    return lax.fori_loop(0, length, turn, start)


def rounded(signal):
    return lax.optimization_barrier(signal.astype(jnp.bfloat16)).astype(jnp.float32)


def rms_scale(signal):
    return lax.rsqrt(jnp.mean(signal * signal, axis=-1, keepdims=True) + EPSILON)


def rms_back(gradient, signal, scaling, gain_vec):
    weighted = gradient * gain_vec
    inner_sum = jnp.mean(weighted * signal, axis=-1, keepdims=True)
    return scaling * weighted - signal * (scaling * scaling * scaling) * inner_sum


def silu_slope(signal):
    sigma_val = jax.nn.sigmoid(signal)
    return sigma_val * (1.0 + signal * (1.0 - sigma_val))


def doc_index(doc_lengths, positions):
    doc_ends = jnp.cumsum(doc_lengths, axis=1)
    return jnp.sum((positions[:, None, None] >= doc_ends[None, :, :]).astype(jnp.int32), axis=2)


def chain_combine(earlier, later_part):
    return (earlier[0] * later_part[0], later_part[0][..., None] * earlier[1] + later_part[1])


def block_tables(log_forget, doc_ids, previous):
    length = log_forget.shape[1]
    row_index = lax.broadcasted_iota(jnp.int32, (length, length), 0)
    col_index = lax.broadcasted_iota(jnp.int32, (length, length), 1)
    lower_ones = (row_index >= col_index).astype(jnp.float32)
    cumulated = jnp.einsum("ij,njshk->nishk", lower_ones, log_forget, precision=PRECISE)
    last_sum = cumulated[:, -1]
    same_doc = doc_ids[:, :, None, :] == doc_ids[:, None, :, :]
    visible = jnp.transpose(same_doc & (row_index >= col_index)[None, :, :, None], (0, 3, 1, 2))[
        :, :, None
    ]
    enters = (doc_ids == previous[:, None, :]).astype(jnp.float32)[..., None, None]
    at_end = (doc_ids == doc_ids[:, -1:, :]).astype(jnp.float32)[..., None, None]
    alive_end = (doc_ids[:, -1] == previous).astype(jnp.float32)[..., None, None]
    decays = jnp.exp(last_sum) * alive_end
    return (lower_ones, cumulated, last_sum, visible, enters, at_end, decays)


def block_factors(queries, key_vec, cumulated, last_sum, at_end):
    q_tilde = queries * jnp.exp(cumulated)
    k_tilde = key_vec * jnp.exp(-cumulated)
    k_hat = key_vec * jnp.exp(last_sum[:, None] - cumulated) * at_end
    return (q_tilde, k_tilde, k_hat)


def recur_forward(queries, key_vec, values_in, log_forget, doc_ids, previous):
    lower_ones, cumulated, last_sum, visible, enters, at_end, decays = block_tables(
        log_forget, doc_ids, previous
    )
    q_tilde, k_tilde, k_hat = block_factors(queries, key_vec, cumulated, last_sum, at_end)
    scores = jnp.einsum("nishk,njshk->nshij", q_tilde, k_tilde, precision=PRECISE)
    mixing = jnp.where(visible, scores, 0.0)
    inside = jnp.einsum("nshij,njshv->nishv", mixing, values_in, precision=PRECISE)
    local_sum = jnp.einsum("njshk,njshv->nshkv", k_hat, values_in, precision=PRECISE)

    def advance(carried, element):
        state_now, product = carried
        factor, addend = element
        return ((factor[..., None] * state_now + addend, product * factor), (state_now, product))

    zero_state = jnp.zeros(local_sum.shape[1:], jnp.float32)
    unit_decay = jnp.ones(decays.shape[1:], jnp.float32)
    (run_state, run_decay), (prefix_state, prefix_decay) = lax.scan(
        advance, (zero_state, unit_decay), (decays, local_sum)
    )
    incoming = entering(
        (run_decay, run_state), "seq", chain_combine, (unit_decay, zero_state), False
    )[1]
    start_state = prefix_state + prefix_decay[..., None] * incoming[None]
    carried_in = jnp.einsum("nishk,nshkv->nishv", q_tilde * enters, start_state, precision=PRECISE)
    return (inside + carried_in, start_state)


def recur_backward(
    queries, key_vec, values_in, log_forget, doc_ids, previous, start_state, grad_out
):
    lower_ones, cumulated, last_sum, visible, enters, at_end, decays = block_tables(
        log_forget, doc_ids, previous
    )
    q_tilde, k_tilde, k_hat = block_factors(queries, key_vec, cumulated, last_sum, at_end)
    scores = jnp.einsum("nishk,njshk->nshij", q_tilde, k_tilde, precision=PRECISE)
    mixing = jnp.where(visible, scores, 0.0)
    own_term = jnp.einsum("nishk,nishv->nshkv", q_tilde * enters, grad_out, precision=PRECISE)

    def retreat(carried, element):
        running, product = carried
        factor, addend = element
        return ((addend + factor[..., None] * running, product * factor), (running, product))

    zero_state = jnp.zeros(own_term.shape[1:], jnp.float32)
    unit_decay = jnp.ones(decays.shape[1:], jnp.float32)
    (run_grad, run_decay), (after_sum, after_decay) = lax.scan(
        retreat, (zero_state, unit_decay), (decays, own_term), reverse=True
    )
    outgoing = entering(
        (run_decay, run_grad), "seq", chain_combine, (unit_decay, zero_state), True
    )[1]
    next_grad = after_sum + after_decay[..., None] * outgoing[None]
    grad_mixing = jnp.where(
        visible, jnp.einsum("nishv,njshv->nshij", grad_out, values_in, precision=PRECISE), 0.0
    )
    grad_qt = jnp.einsum("nshij,njshk->nishk", grad_mixing, k_tilde, precision=PRECISE)
    grad_qt = grad_qt + jnp.einsum(
        "nishv,nshkv->nishk", grad_out * enters, start_state, precision=PRECISE
    )
    grad_kt = jnp.einsum("nshij,nishk->njshk", grad_mixing, q_tilde, precision=PRECISE)
    grad_values = jnp.einsum("nshij,nishv->njshv", mixing, grad_out, precision=PRECISE)
    grad_values = grad_values + jnp.einsum(
        "njshk,nshkv->njshv", k_hat, next_grad, precision=PRECISE
    )
    grad_khat = jnp.einsum("njshv,nshkv->njshk", values_in, next_grad, precision=PRECISE) * at_end
    grad_decay = jnp.sum(next_grad * start_state, axis=-1)
    grad_queries = grad_qt * jnp.exp(cumulated)
    grad_keys = grad_kt * jnp.exp(-cumulated) + grad_khat * jnp.exp(last_sum[:, None] - cumulated)
    grad_cum = grad_qt * q_tilde - grad_kt * k_tilde - grad_khat * k_hat
    grad_last = jnp.sum(grad_khat * k_hat, axis=1) + grad_decay * decays
    grad_log = (
        jnp.einsum("it,nishk->ntshk", lower_ones, grad_cum, precision=PRECISE) + grad_last[:, None]
    )
    return (grad_queries, grad_keys, grad_values, grad_log)


def on_device(
    tokens,
    norm1_gain,
    w_mix_in,
    forget_gap,
    group_gain,
    w_mix_out,
    norm2_gain,
    w_gate_up,
    w_down,
    doc_lengths,
    out_cotangent,
):
    mp_count = lax.axis_size("mp")
    rows_dev, pack_count, model_width = tokens.shape
    run_length = rows_dev * mp_count
    blocks = run_length // BLOCK
    local_heads, head_size = forget_gap.shape
    local_chans = local_heads * head_size
    local_ff = w_gate_up.shape[2]
    mp_index = lax.axis_index("mp")
    run_start = lax.axis_index("seq") * run_length
    positions = run_start - 1 + jnp.arange(run_length + 1, dtype=jnp.int32)
    all_ids = doc_index(doc_lengths, positions)
    doc_ids = all_ids[1:].reshape(blocks, BLOCK, pack_count)
    previous = all_ids[0:run_length:BLOCK]
    shape_blocks = (blocks, BLOCK, pack_count, local_heads, head_size)
    shape_heads = (run_length, pack_count, local_heads, head_size)
    shape_flat = (run_length, pack_count, local_chans)
    scale_one = rms_scale(tokens)
    normed = (tokens * scale_one * norm1_gain).astype(jnp.bfloat16)
    in_flat = w_mix_in.reshape(model_width, 4 * local_chans)
    shard_rows = lax.all_gather(normed, "mp", axis=0, tiled=True)
    normed_all = shard_rows
    projected = jnp.einsum("tsd,dc->tsc", shard_rows, in_flat, preferred_element_type=jnp.float32)
    pre_query = projected[..., :local_chans]
    pre_forget = projected[..., local_chans : 2 * local_chans]
    pre_value = projected[..., 2 * local_chans : 3 * local_chans]
    pre_gate = projected[..., 3 * local_chans :]
    open_gate = jax.nn.sigmoid(-pre_forget)
    gap_gate = forget_gap.reshape(local_chans) * open_gate
    queries = rounded(pre_query).reshape(shape_blocks)
    key_vec = rounded(gap_gate).reshape(shape_blocks)
    values_in = rounded(pre_value).reshape(shape_blocks)
    log_forget = jnp.log1p(-gap_gate).reshape(shape_blocks)
    mixed, start_state = recur_forward(queries, key_vec, values_in, log_forget, doc_ids, previous)
    mixed = mixed.reshape(shape_flat)
    gate_act = jax.nn.silu(pre_gate)
    gated_four = (mixed * gate_act).reshape(shape_heads)
    scale_group = rms_scale(gated_four)
    heads_out = (gated_four * scale_group * group_gain).astype(jnp.bfloat16).reshape(shape_flat)
    heads_tok = lax.all_to_all(heads_out, "mp", split_axis=0, concat_axis=2, tiled=True)
    out_flat = w_mix_out.reshape(-1, model_width)
    hidden = tokens + jnp.einsum(
        "tsc,cd->tsd", heads_tok, out_flat, preferred_element_type=jnp.float32
    )
    scale_two = rms_scale(hidden)
    normed_two = (hidden * scale_two * norm2_gain).astype(jnp.bfloat16)
    ffn_flat = w_gate_up.reshape(model_width, 2 * local_ff)
    shard_rows = lax.all_gather(normed_two, "mp", axis=0, tiled=True)
    gate_up = jnp.einsum("tsd,dc->tsc", shard_rows, ffn_flat, preferred_element_type=jnp.float32)
    pre_gate_two = gate_up[..., :local_ff]
    pre_up = gate_up[..., local_ff:]
    silu_two = jax.nn.silu(pre_gate_two)
    activation = (silu_two * pre_up).astype(jnp.bfloat16)
    partial_value = activation
    ffn_sum = lax.psum_scatter(
        jnp.einsum("tsf,fd->tsd", partial_value, w_down, preferred_element_type=jnp.float32).astype(
            jnp.bfloat16
        ),
        "mp",
        scatter_dimension=0,
        tiled=True,
    ).astype(jnp.float32)
    layer_out = hidden + ffn_sum
    cot_low = out_cotangent.astype(jnp.bfloat16)
    cot_own = lax.dynamic_slice_in_dim(out_cotangent, mp_index * rows_dev, rows_dev, 0)
    down_part = jnp.einsum("tsf,tsd->fd", activation, cot_low, preferred_element_type=jnp.float32)
    grad_act = jnp.einsum("tsd,fd->tsf", cot_low, w_down, preferred_element_type=jnp.float32)
    grad_gate_two = grad_act * pre_up * silu_slope(pre_gate_two)
    grad_up = grad_act * silu_two
    grad_gate_up = jnp.concatenate([grad_gate_two, grad_up], axis=-1).astype(jnp.bfloat16)
    gate_up_part = jnp.einsum(
        "tsd,tsc->dc", shard_rows, grad_gate_up, preferred_element_type=jnp.float32
    )
    gate_up_part = gate_up_part.reshape(model_width, 2, local_ff)
    partial_value = grad_gate_up
    grad_normed_two = lax.psum_scatter(
        jnp.einsum(
            "tsc,dc->tsd", partial_value, ffn_flat, preferred_element_type=jnp.float32
        ).astype(jnp.bfloat16),
        "mp",
        scatter_dimension=0,
        tiled=True,
    ).astype(jnp.float32)
    norm2_part = jnp.sum(grad_normed_two * hidden * scale_two, axis=(0, 1))
    grad_hidden = cot_own + rms_back(grad_normed_two, hidden, scale_two, norm2_gain)
    grad_mix = grad_hidden.astype(jnp.bfloat16)
    out_part = jnp.einsum("tsc,tsd->cd", heads_tok, grad_mix, preferred_element_type=jnp.float32)
    grad_tok = jnp.einsum(
        "tsd,cd->tsc", grad_mix, out_flat, preferred_element_type=jnp.float32
    ).astype(jnp.bfloat16)
    grad_heads = lax.all_to_all(grad_tok, "mp", split_axis=2, concat_axis=0, tiled=True).astype(
        jnp.float32
    )
    grad_four = grad_heads.reshape(shape_heads)
    group_part = jnp.sum(grad_four * gated_four * scale_group, axis=(0, 1))
    grad_gated = rms_back(grad_four, gated_four, scale_group, group_gain).reshape(shape_flat)
    grad_mixed = grad_gated * gate_act
    grad_gate_in = grad_gated * mixed * silu_slope(pre_gate)
    grad_queries, grad_keys, grad_values, grad_log = recur_backward(
        queries,
        key_vec,
        values_in,
        log_forget,
        doc_ids,
        previous,
        start_state,
        grad_mixed.reshape(shape_blocks),
    )
    grad_gap = grad_keys.reshape(shape_flat) - grad_log.reshape(shape_flat) / (1.0 - gap_gate)
    gap_part = jnp.sum(grad_gap * open_gate, axis=(0, 1)).reshape(local_heads, head_size)
    grad_forget_in = -grad_gap * gap_gate * (1.0 - open_gate)
    grad_projected = jnp.concatenate(
        [
            grad_queries.reshape(shape_flat),
            grad_forget_in,
            grad_values.reshape(shape_flat),
            grad_gate_in,
        ],
        axis=-1,
    ).astype(jnp.bfloat16)
    mix_in_part = jnp.einsum(
        "tsd,tsc->dc", normed_all, grad_projected, preferred_element_type=jnp.float32
    )
    mix_in_part = mix_in_part.reshape(model_width, 4, local_chans)
    partial_value = grad_projected
    grad_normed = lax.psum_scatter(
        jnp.einsum(
            "tsc,dc->tsd", partial_value, in_flat, preferred_element_type=jnp.float32
        ).astype(jnp.bfloat16),
        "mp",
        scatter_dimension=0,
        tiled=True,
    ).astype(jnp.float32)
    norm1_part = jnp.sum(grad_normed * tokens * scale_one, axis=(0, 1))
    tokens_grad = grad_hidden + rms_back(grad_normed, tokens, scale_one, norm1_gain)
    seq_count = lax.axis_size("seq")
    arranged = out_part.reshape(
        mp_count, local_heads, seq_count, head_size // seq_count, model_width
    )
    arranged = jnp.transpose(arranged, (2, 0, 1, 3, 4)).reshape(
        seq_count * mp_count * local_heads, head_size // seq_count, model_width
    )
    mix_in_grad, gate_up_grad, down_grad, group_grad, gap_grad = (
        lax.psum_scatter(
            mix_in_part.astype(jnp.bfloat16), "seq", scatter_dimension=0, tiled=True
        ).astype(jnp.float32),
        lax.psum_scatter(
            gate_up_part.astype(jnp.bfloat16), "seq", scatter_dimension=0, tiled=True
        ).astype(jnp.float32),
        lax.psum_scatter(
            down_part.astype(jnp.bfloat16), "seq", scatter_dimension=1, tiled=True
        ).astype(jnp.float32),
        lax.psum_scatter(
            group_part.astype(jnp.bfloat16), "seq", scatter_dimension=1, tiled=True
        ).astype(jnp.float32),
        lax.psum_scatter(
            gap_part.astype(jnp.bfloat16), "seq", scatter_dimension=1, tiled=True
        ).astype(jnp.float32),
    )
    mix_out_grad, norm1_grad, norm2_grad = (
        lax.psum_scatter(arranged, ("seq", "mp"), scatter_dimension=0, tiled=True),
        lax.psum_scatter(norm1_part, ("seq", "mp"), scatter_dimension=0, tiled=True),
        lax.psum_scatter(norm2_part, ("seq", "mp"), scatter_dimension=0, tiled=True),
    )
    return (
        layer_out,
        tokens_grad,
        norm1_grad,
        mix_in_grad,
        gap_grad,
        group_grad,
        mix_out_grad,
        norm2_grad,
        gate_up_grad,
        down_grad,
    )


def solution(mesh):
    placed = (
        P(("seq", "mp"), None, None),
        P(),
        P(None, None, "mp"),
        P("mp", None),
        P("mp", None),
        P(),
        P(),
        P(None, None, "mp"),
        P("mp", None),
        P(),
        P("seq", None, None),
    )
    return jax.shard_map(
        on_device,
        mesh=mesh,
        in_specs=placed,
        out_specs=(
            P(("seq", "mp"), None, None),
            P(("seq", "mp"), None, None),
            P(("seq", "mp")),
            P("seq", None, "mp"),
            P("mp", "seq"),
            P("mp", "seq"),
            P("mp", "seq", None),
            P(("seq", "mp")),
            P("seq", None, "mp"),
            P("mp", "seq"),
        ),
        check_vma=False,
    )
```

profile of v0, /device:TPU:0, one launch (start us, length us, event | category | flops | bytes accessed | tf_op | source)
XLA Modules:
  0.0 2169.8 jit_solution(9496402910027111081)
XLA Ops:
  19.8 14.6 reshape.272
  34.7 136.2 %all-gather.9.cloned.1.call-done = bf16[1024,2,2048]{2,0,1:T(8,128)(2,1)} async-done(((bf16[256,2,2048]{2,0,1:T(8,128)(2,1)}), bf16[1024,2,2048]{2,0,1:T(8,128)(2,1)}) %all-gather.9.cloned.1.call-update) | async-done | bytes 8388624 | tf_op jit(solution)/shard_map/all_gather | solution.py:195
  170.9 23.8 %fusion.122 = (bf16[1024,2,2048]{2,0,1:T(8,128)(2,1)}, f32[1024,2,2048]{2,0,1:T(8,128)S(1)}) fusion(bf16[1024,2,2048]{2,0,1:T(8,128)(2,1)} %all-gather.9.cloned.1.call-done, bf16[2048,2048,1]{1,0,2:T(8,128)(2,1)} %reshape.272), kind=kOutput, calls=%fused_computation.199 | convolution fusion | flops 17184063488 | bytes 41943040 | tf_op jit(solution)/shard_map/tsd,dc->tsc/dot_general | solution.py:197
  244.6 17.9 while.68
  272.6 15.3 fusion.119
  300.7 11.7 fusion.52
  362.8 53.0 %all_to_all.27 = bf16[1024,2,512]{2,1,0:T(2,128)(2,1)S(1)} all-to-all(bf16[1024,2,512]{2,1,0:T(2,128)(2,1)S(1)} %copy.404), channel_id=1, replica_groups=mesh['seq'=8,'mp'=4] {'mp'}, dimensions={0} | all-to-all | bytes 4194304 | tf_op jit(solution)/shard_map/all_to_all | solution.py:214
  422.1 12.0 multiply_reduce_fusion.3
  437.8 25.3 %reshape.275 = bf16[2048,2816,1]{1,0,2:T(8,128)(2,1)} reshape(bf16[2048,2,1408]{2,1,0:T(2,128)(2,1)} %param.26) | data formatting | bytes 23068672 | tf_op jit(solution)/shard_map/reshape | solution.py:221
  472.7 113.0 %all-gather.11.cloned.1.call-done = bf16[1024,2,2048]{2,0,1:T(8,128)(2,1)} async-done(((bf16[256,2,2048]{2,0,1:T(8,128)(2,1)}), bf16[1024,2,2048]{2,0,1:T(8,128)(2,1)}) %all-gather.11.cloned.1.call-update) | async-done | bytes 8388624 | tf_op jit(solution)/shard_map/all_gather | solution.py:222
  585.7 31.9 %fusion.123 = f32[1024,2,2816]{2,0,1:T(8,128)} fusion(bf16[1024,2,2048]{2,0,1:T(8,128)(2,1)} %all-gather.11.cloned.1.call-done, bf16[2048,2816,1]{1,0,2:T(8,128)(2,1)} %reshape.275), kind=kOutput, calls=%fused_computation.200 | convolution fusion | flops 23622320128 | bytes 42991616 | tf_op jit(solution)/shard_map/tsd,dc->tsc/dot_general | solution.py:223
  617.6 30.3 %multiply_convert_fusion.1 = (bf16[1024,2,1408]{2,0,1:T(8,128)(2,1)}, bf16[1024,2,1408]{2,0,1:T(8,128)(2,1)}, bf16[1024,2,1408]{2,0,1:T(8,128)(2,1)}) fusion(f32[1024,2,2816]{2,0,1:T(8,128)} %fusion.123, bf16[1408,2048]{1,0:T(8,128)(2,1)} %param.27, bf16[1024,2,2048]{2,1,0:T(2,128)(2,1)} %convert_element_type.218), kind=kOutput, calls=%fused_computation.21 | convolution fusion | flops 11854413824 | bytes 54525952 | tf_op jit(solution)/shard_map/tsd,fd->tsf/dot_general | solution.py:241
  647.8 31.2 %fusion.13 = bf16[1024,2,2048]{2,0,1:T(8,128)(2,1)} fusion(bf16[2048,2816,1]{1,0,2:T(8,128)(2,1)} %reshape.275, bf16[1024,2,1408]{2,0,1:T(8,128)(2,1)} %get-tuple-element.647, bf16[1024,2,1408]{2,0,1:T(8,128)(2,1)} %get-tuple-element.646), kind=kOutput, calls=%fused_computation.35 | convolution fusion | flops 23649583104 | bytes 31457280 | tf_op jit(solution)/shard_map/tsc,dc->tsd/dot_general | solution.py:251
  679.1 18.6 fusion.10
  703.9 117.9 %reduce-scatter.14.cloned.1.call-done = bf16[256,2,2048]{2,0,1:T(8,128)(2,1)} async-done(((bf16[1024,2,2048]{2,0,1:T(8,128)(2,1)}), bf16[256,2,2048]{2,0,1:T(8,128)(2,1)}) %reduce-scatter.14.cloned.1.call-update) | async-done | bytes 2097168 | tf_op jit(solution)/shard_map/reduce_scatter | solution.py:250
  826.7 142.6 %reduce-scatter.12.cloned.1.call-done = bf16[256,2,2048]{2,0,1:T(8,128)(2,1)} async-done(((bf16[1024,2,2048]{2,0,1:T(8,128)(2,1)}), bf16[256,2,2048]{2,0,1:T(8,128)(2,1)}) %reduce-scatter.12.cloned.1.call-update) | async-done | bytes 2097168 | tf_op jit(solution)/shard_map/reduce_scatter | solution.py:229
  1007.6 36.2 %all-to-all-done.1 = bf16[256,2,2048]{0,1,2:T(2,128)(2,1)S(1)} async-done(((bf16[256,2,2048]{0,1,2:T(2,128)(2,1)}), bf16[256,2,2048]{0,1,2:T(2,128)(2,1)S(1)}, u32[]{:S(2)}, u32[]{:S(2)}) %all-to-all-start.1) | async-done | bytes 2097184 | tf_op jit(solution)/shard_map/all_to_all | solution.py:265
  1069.1 13.0 fusion.106
  1087.6 12.7 fusion.50
  1102.7 23.2 %while.70 = (s32[]{:T(128)}, f32[2,4,128,128]{3,2,1,0:T(8,128)S(1)}, f32[2,4,128]{2,1,0:T(4,128)S(1)}, f32[8,2,4,128,128]{4,3,2,1,0:T(8,128)}, f32[8,2,4,128]{3,...) while((s32[]{:T(128)}, ...), condition=%wide.region_14.15_spmd.clone, body=%wide.region_13.14_spmd.clone.sunk | while | flops 527364 | bytes 2650254 | solution.py:132
  1126.8 19.0 bitcast_convert_fusion.4
  1145.8 31.6 %bitcast_convert_fusion.2 = bf16[2048,2816]{1,0:T(8,128)(2,1)} fusion(bf16[1024,2,2048]{2,0,1:T(8,128)(2,1)} %all-gather.11.cloned.1.call-done, bf16[1024,2,1408]{2,0,1:T(8,128)(2,1)} %get-tuple-element.647, bf16[1024,2,1408]{2,0,1:T(8,128)(2,1)} %get-tuple-element.646), kind=kOutput, calls=%fused_computation.16 | convolution fusion | flops 23651155968 | bytes 31457280 | tf_op jit(solution)/shard_map/tsd,tsc->dc/dot_general | solution.py:245
  1177.4 22.8 %convert_element_type.243 = bf16[2048,2,1408]{2,1,0:T(2,128)(2,1)} reshape(bf16[2048,2816]{1,0:T(8,128)(2,1)} %bitcast_convert_fusion.2) | data formatting | bytes 23068672 | tf_op jit(solution)/shard_map/convert_element_type | solution.py:322
  1269.5 12.7 fusion.97
  1315.9 12.7 multiply_reduce_fusion
  1355.2 26.3 %bitcast_convert_fusion.3 = bf16[2048,2048]{0,1:T(8,128)(2,1)} fusion(bf16[1024,2,2048]{2,0,1:T(8,128)(2,1)} %all-gather.9.cloned.1.call-done, bf16[1024,2,512]{2,0,1:T(8,128)(2,1)} %get-tuple-element.653, bf16[1024,2,512]{2,0,1:T(8,128)(2,1)} %reshape.250, bf16[1024,2,512]{2,0,1:T(8,128)(2,1)S(1)} %copy-done.29, bf16[1024,2,512]{2,0,1:T(8,128)(2,1)} %reshape.247), kind=kOutput, calls=%fused_computation.17 | convolution fusion | flops 17217617920 | bytes 25165824 | tf_op jit(solution)/shard_map/tsd,tsc->dc/dot_general | solution.py:295
  1381.5 14.6 copy.437
  1396.1 24.7 %convolution_convert_fusion = bf16[1024,2,2048]{2,0,1:T(8,128)(2,1)} fusion(bf16[2048,2048,1]{1,0,2:T(8,128)(2,1)} %reshape.272, bf16[1024,2,512]{2,0,1:T(8,128)(2,1)} %get-tuple-element.653, bf16[1024,2,512]{2,0,1:T(8,128)(2,1)} %reshape.250, bf16[1024,2,512]{2,0,1:T(8,128)(2,1)S(1)} %copy-done.29, bf16[1024,2,512]{2,0,1:T(8,128)(2,1)} %reshape.247), kind=kOutput, calls=%fused_computation.34 | convolution fusion | flops 17217617920 | bytes 25165824 | tf_op jit(solution)/shard_map/tsc,dc->tsd/dot_general | solution.py:301
  1453.5 193.6 %all-reduce.8.cloned.1.call-done = (bf16[2048,4,512]{2,1,0:T(4,128)(2,1)}, bf16[2048,2,1408]{2,1,0:T(2,128)(2,1)}) async-done(((bf16[2048,4,512]{2,1,0:T(4,128)(2,1)}, bf16[2048,2,1408]{2,1,0:T(2,128)(2,1)}), (bf16[2048,4,512]{2,1,0:T(4,128)(2,1)}, bf16[2048,2,1408]{2,1,0:T(2,128)(2,1)})) %all-reduce.8.cloned.1.call-update) | async-done | bytes 19922960
  1653.8 140.2 %reduce-scatter.16.cloned.1.call-done = bf16[256,2,2048]{2,0,1:T(8,128)(2,1)} async-done(((bf16[1024,2,2048]{2,0,1:T(8,128)(2,1)}), bf16[256,2,2048]{2,0,1:T(8,128)(2,1)}) %reduce-scatter.16.cloned.1.call-update) | async-done | bytes 2097168 | tf_op jit(solution)/shard_map/reduce_scatter | solution.py:300
  1801.0 44.9 %all-reduce.4 = (f32[2048]{0:T(1024)S(1)}, f32[2048]{0:T(1024)S(1)}) all-reduce(f32[2048]{0:T(1024)S(1)} %get-tuple-element.586, f32[2048]{0:T(1024)S(1)} %copy-done.50), channel_id=9, replica_groups=mesh['seq'=8,'mp'=4] {'seq','mp'}, use_global_device_ids=true, to_apply=%region_22.23.clone | all-reduce | flops 4096 | bytes 32768
  1858.2 304.5 %reduce-scatter.18.cloned.1.call-done = f32[4,16,2048]{2,1,0:T(8,128)} async-done(((f32[128,16,2048]{2,1,0:T(8,128)}), f32[4,16,2048]{2,1,0:T(8,128)}) %reduce-scatter.18.cloned.1.call-update) | async-done | bytes 524304 | tf_op jit(solution)/shard_map/reduce_scatter | solution.py:335
  (364 shorter events, 487.6 us)
Async XLA Ops:
  7.2 163.7 %all-gather.9.cloned.1.call-start = ((), (), s32[]{:S(2)}) async-start(), calls=%async_computation.9 | async-start | bytes 10485760 | tf_op jit(solution)/shard_map/all_gather | solution.py:195
  18.4 271.1 %all-gather.13.cloned.1.call-start = ((), (), s32[]{:S(2)}) async-start(), calls=%async_computation.16 | async-start | bytes 2359296 | tf_op jit(solution)/shard_map/all_gather | solution.py:16
  34.6 194.6 %copy-start.44 = (f32[8,2]{1,0:T(8,128)}, f32[8,2]{1,0:T(8,128)S(1)}, u32[]{:S(2)}) copy-start(f32[8,2]{1,0:T(8,128)S(1)} %copy.392) | copy-start | bytes 196
  34.7 194.6 %copy-start.38 = (f32[8,128,2]{1,2,0:T(2,128)}, f32[8,128,2]{1,2,0:T(2,128)S(1)}, u32[]{:S(2)}) copy-start(f32[8,128,2]{1,2,0:T(2,128)S(1)} %get-tuple-element.667) | copy-start | bytes 24580
  34.7 266.0 %copy-start.36 = (f32[8,128,2]{1,2,0:T(2,128)}, f32[8,128,2]{1,2,0:T(2,128)S(1)}, u32[]{:S(2)}) copy-start(f32[8,128,2]{1,2,0:T(2,128)S(1)} %get-tuple-element.666) | copy-start | bytes 24580
  34.7 165.8 %copy-start.55 = (f32[4,128]{1,0:T(4,128)S(1)}, f32[4,128]{1,0:T(4,128)}, u32[]{:S(2)}) copy-start(f32[4,128]{1,0:T(4,128)} %param.22) | copy-start | bytes 6148
  229.1 83.3 %copy-start.12 = (bf16[8,128,2,4,128]{4,3,1,0,2:T(4,128)(2,1)}, bf16[8,128,2,4,128]{4,3,1,0,2:T(4,128)(2,1)S(1)}, u32[]{:S(2)}) copy-start(bf16[8,128,2,4,128]{4,3,1,0,2:T(4,128)(2,1)S(1)} %reshape.236) | copy-start | bytes 6291460
  262.5 38.1 %copy-start.30 = (f32[8,2,4,128]{3,2,1,0:T(4,128)}, f32[8,2,4,128]{3,2,1,0:T(4,128)S(1)}, u32[]{:S(2)}) copy-start(f32[8,2,4,128]{3,2,1,0:T(4,128)S(1)} %get-tuple-element.421) | copy-start | bytes 98308
  263.3 322.4 %all-gather.11.cloned.1.call-start = ((), (), s32[]{:S(2)}) async-start(), calls=%async_computation.10 | async-start | bytes 10485760 | tf_op jit(solution)/shard_map/all_gather | solution.py:222
  263.8 48.6 %copy-start.27 = (pred[8,2,128,128]{3,2,1,0:T(8,128)(4,1)}, pred[8,2,128,128]{3,2,1,0:T(8,128)(4,1)S(1)}, u32[]{:S(2)}) copy-start(pred[8,2,128,128]{3,2,1,0:T(8,128)(4,1)S(1)} %compare_and_fusion) | copy-start | bytes 786436
  422.0 14.0 copy-start.40
  437.8 384.1 %reduce-scatter.14.cloned.1.call-start = ((), (), s32[]{:S(2)}) async-start(), calls=%async_computation.12 | async-start | bytes 10485760 | tf_op jit(solution)/shard_map/reduce_scatter | solution.py:250
  679.1 290.2 %reduce-scatter.12.cloned.1.call-start = ((), (), s32[]{:S(2)}) async-start(), calls=%async_computation.11 | async-start | bytes 10485760 | tf_op jit(solution)/shard_map/reduce_scatter | solution.py:229
  697.7 124.2 %copy-start.41 = (f32[2048]{0:T(1024)S(1)}, f32[2048]{0:T(1024)}, u32[]{:S(2)}) copy-start(f32[2048]{0:T(1024)} %param.25) | copy-start | bytes 24580
  697.7 124.2 %copy-start.49 = (f32[256,2]{0,1:T(2,128)S(1)}, f32[256,2]{0,1:T(2,128)}, u32[]{:S(2)}) copy-start(f32[256,2]{0,1:T(2,128)} %copy-done.48) | copy-start | bytes 6148
  703.9 265.4 %copy-start.54 = (f32[256,2]{0,1:T(2,128)S(1)}, f32[256,2]{0,1:T(2,128)}, u32[]{:S(2)}) copy-start(f32[256,2]{0,1:T(2,128)} %get-tuple-element.672) | copy-start | bytes 6148
  821.9 147.4 %copy-start.26 = (bf16[256,2,2048]{2,0,1:T(8,128)(2,1)S(1)}, bf16[256,2,2048]{2,0,1:T(8,128)(2,1)}, u32[]{:S(2)}) copy-start(bf16[256,2,2048]{2,0,1:T(8,128)(2,1)} %reduce-scatter.14.cloned.1.call-done) | copy-start | bytes 6291460
  991.1 52.7 %all-to-all-start.1 = ((bf16[256,2,2048]{0,1,2:T(2,128)(2,1)}), bf16[256,2,2048]{0,1,2:T(2,128)(2,1)S(1)}, u32[]{:S(2)}, u32[]{:S(2)}) async-start(bf16[256,2,2048]{0,1,2:T(2,128)(2,1)} %copy.409), calls=%async_computation.3 | async-start | bytes 4194304 | tf_op jit(solution)/shard_map/all_to_all | solution.py:265
  995.5 256.4 %all-gather.15.cloned.1.call-start = ((), (), s32[]{:S(2)}) async-start(), calls=%async_computation.17 | async-start | bytes 2359296 | tf_op jit(solution)/shard_map/all_gather | solution.py:16
  1126.7 314.1 %reduce-scatter.20.cloned.1.call-start = ((), (), s32[]{:S(2)}) async-start(), calls=%async_computation.15 | async-start | bytes 6488064 | tf_op jit(solution)/shard_map/reduce_scatter | solution.py:324
  1145.7 305.0 %reduce-scatter.24.cloned.1.call-start = ((), (), s32[]{:S(2)}) async-start(), calls=%async_computation.19 | async-start | bytes 36864
  1177.4 32.4 %copy-start.13 = (bf16[8,128,2,4,128]{4,3,1,0,2:T(4,128)(2,1)S(1)}, bf16[8,128,2,4,128]{4,3,1,0,2:T(4,128)(2,1)}, u32[]{:S(2)}) copy-start(bf16[8,128,2,4,128]{4,3,1,0,2:T(4,128)(2,1)} %copy-done.12) | copy-start | bytes 6291460
  1251.9 200.2 %reduce-scatter.22.cloned.1.call-start = ((), (), s32[]{:S(2)}) async-start(), calls=%async_computation.18 | async-start | bytes 36864
  1315.9 13.4 copy-start.20
  1355.1 291.9 %all-reduce.8.cloned.1.call-start = ((), (), s32[]{:S(2)}) async-start(), calls=%async_computation.20 | async-start | bytes 39845888
  1396.1 397.9 %reduce-scatter.16.cloned.1.call-start = ((), (), s32[]{:S(2)}) async-start(), calls=%async_computation.13 | async-start | bytes 10485760 | tf_op jit(solution)/shard_map/reduce_scatter | solution.py:300
  1420.9 741.8 %reduce-scatter.18.cloned.1.call-start = ((), (), s32[]{:S(2)}) async-start(), calls=%async_computation.14 | async-start | bytes 17301504 | tf_op jit(solution)/shard_map/reduce_scatter | solution.py:335
  1450.7 343.3 %copy-start.43 = (f32[2048]{0:T(1024)S(1)}, f32[2048]{0:T(1024)}, u32[]{:S(2)}) copy-start(f32[2048]{0:T(1024)} %param.20) | copy-start | bytes 24580
  1450.7 343.3 %copy-start.47 = (f32[256,2]{0,1:T(2,128)S(1)}, f32[256,2]{0,1:T(2,128)}, u32[]{:S(2)}) copy-start(f32[256,2]{0,1:T(2,128)} %copy-done.46) | copy-start | bytes 6148
  1653.8 147.2 %copy-start.50 = (f32[2048]{0:T(1024)S(1)}, f32[2048]{0:T(1024)}, u32[]{:S(2)}) copy-start(f32[2048]{0:T(1024)} %get-tuple-element.584) | copy-start | bytes 24580
  1653.8 193.3 %copy-start.53 = (f32[256,2]{0,1:T(2,128)S(1)}, f32[256,2]{0,1:T(2,128)}, u32[]{:S(2)}) copy-start(f32[256,2]{0,1:T(2,128)} %get-tuple-element.670) | copy-start | bytes 6148
  1794.0 53.1 %copy-start.25 = (bf16[256,2,2048]{2,0,1:T(8,128)(2,1)S(1)}, bf16[256,2,2048]{2,0,1:T(8,128)(2,1)}, u32[]{:S(2)}) copy-start(bf16[256,2,2048]{2,0,1:T(8,128)(2,1)} %reduce-scatter.16.cloned.1.call-done) | copy-start | bytes 6291460
  (40 other events, 283.0 us)
Sparse Core Ops, SparseCore 0:
  18.5 152.3 all-gather.8
  263.4 26.0 all-gather.12
  437.9 147.7 all-gather.10
  679.2 142.6 reduce-scatter.13
  824.1 145.1 reduce-scatter.11
  1126.8 26.9 all-gather.14
  1157.2 59.1 reduce-scatter.19
  1252.0 29.6 reduce-scatter.23
  1355.2 29.6 reduce-scatter.21
  1396.2 250.7 all-reduce.7
  1649.5 144.4 reduce-scatter.15
  1796.8 365.8 reduce-scatter.17
where the time goes:
time: 2180 us; the launch traced here: 2170 us
  waiting for transfers between devices  1190 us (55%)
  matrix products  395 us (18%)
  local copies, waits for them, and re-layouts  262 us (12%)
  other arithmetic  188 us (9%)
  blocking collectives  116 us (5%)
    reduce_scatter x1, waiting for transfers between devices, on_device(): lax.psum_scatter(arranged, ('seq', 'mp'), scatter_dimension=0, tiled=True)  305 us
    unnamed x15, waiting for transfers between devices  194 us
    reduce_scatter x1, waiting for transfers between devices, on_device(): lax.psum_scatter(jnp.einsum('tsf,fd->tsd', partial_value, w_down, preferr...  143 us
    reduce_scatter x1, waiting for transfers between devices, on_device(): lax.psum_scatter(jnp.einsum('tsc,dc->tsd', partial_value, in_flat, prefer...  140 us
    all_gather x1, waiting for transfers between devices, on_device(): shard_rows = lax.all_gather(normed, 'mp', axis=0, tiled=True)  136 us
    reduce_scatter x1, waiting for transfers between devices, on_device(): lax.psum_scatter(jnp.einsum('tsc,dc->tsd', partial_value, ffn_flat, prefe...  118 us
    all_gather x1, waiting for transfers between devices, on_device(): shard_rows = lax.all_gather(normed_two, 'mp', axis=0, tiled=True)  113 us
    all_to_all x1, blocking collectives, on_device(): lax.all_to_all(heads_out, 'mp', split_axis=0, concat_axis=2, tiled=True)  53 us
  transfers between devices with their start and end apart: 13, of which 9 were waited for; matrix products, arithmetic and copies ran while one was open for 21% of the time, Pallas kernels for 0%

commit v1 on v0

--- a/solution.py
+++ b/solution.py
@@ -1,6 +1,10 @@
+import functools
+
 import jax
 import jax.numpy as jnp
 from jax import lax
+from jax.experimental import pallas as pl
+from jax.experimental.pallas import tpu as pltpu
 from jax.sharding import PartitionSpec as P
 
 BLOCK = 128
@@ -50,7 +54,9 @@
 
 
 def doc_index(doc_lengths, positions):
-    doc_ends = jnp.cumsum(doc_lengths, axis=1)
+    doc_ends = jnp.stack(
+        [jnp.sum(doc_lengths[:, : k + 1], axis=1) for k in range(doc_lengths.shape[1])], axis=1
+    )
     return jnp.sum((positions[:, None, None] >= doc_ends[None, :, :]).astype(jnp.int32), axis=2)
 
 
@@ -160,7 +166,7 @@
     return (grad_queries, grad_keys, grad_values, grad_log)
 
 
-def on_device(
+def generic_device(
     tokens,
     norm1_gain,
     w_mix_in,
@@ -350,7 +356,611 @@
     )
 
 
+F32 = jnp.float32
+BF16 = jnp.bfloat16
+
+
+def mm(a, b, dims=((1,), (0,))):
+    return lax.dot_general(a, b, (dims, ((), ())), preferred_element_type=F32)
+
+
+NN, NT, TN = ((1,), (0,)), ((1,), (1,)), ((0,), (0,))
+
+
+def split_two(value):
+    high = value.astype(BF16)
+    return high, (value - high.astype(F32)).astype(BF16)
+
+
+def triangle(length, upper):
+    row = lax.broadcasted_iota(jnp.int32, (length, length), 0)
+    col = lax.broadcasted_iota(jnp.int32, (length, length), 1)
+    return jnp.where((row <= col) if upper else (row >= col), 1.0, 0.0).astype(BF16)
+
+
+def ids_of(lens, pack, positions):
+    total, ids = 0, jnp.zeros_like(positions)
+    for k in range(lens.shape[1]):
+        total = total + lens[pack, k]
+        ids = ids + jnp.where(positions >= total, 1, 0)
+    return ids
+
+
+def block_docs(lens, pack, base, length):
+    col = ids_of(lens, pack, base + lax.broadcasted_iota(jnp.int32, (length, 1), 0))
+    row = ids_of(lens, pack, base + lax.broadcasted_iota(jnp.int32, (1, length), 1))
+    last = ids_of(lens, pack, base + length - 1 + jnp.zeros((1, 1), jnp.int32))
+    before = ids_of(lens, pack, base - 1 + jnp.zeros((1, 1), jnp.int32))
+    return col, row, last, before
+
+
+def gates(pre_forget, gap):
+    open_gate = jax.nn.sigmoid(-pre_forget)
+    gap_gate = gap * open_gate
+    return open_gate, gap_gate, gap_gate.astype(BF16).astype(F32), jnp.log1p(-gap_gate)
+
+
+def mm_split(a, b, dims=((1,), (0,))):
+    (a_high, a_low), (b_high, b_low) = split_two(a), split_two(b)
+    return mm(a_high, b_high, dims) + mm(a_high, b_low, dims) + mm(a_low, b_high, dims)
+
+
+def running_sum(ones, value):
+    high, low = split_two(value)
+    return mm(ones, high) + mm(ones, low)
+
+
+def states_kernel(lens, start, gap, pf, pv, state_out, decay_out):
+    step = pl.program_id(0)
+    length = pf.shape[2]
+    heads = state_out.shape[1]
+
+    @pl.when(step == 0)
+    def _():
+        state_out[...] = jnp.zeros_like(state_out)
+        decay_out[...] = jnp.ones_like(decay_out)
+
+    base = start[0] + step * length
+    ones = triangle(length, False)
+    for p in range(pf.shape[1]):
+        col, _, last_id, before = block_docs(lens, p, base, length)
+        _, _, key, log_forget = gates(pf[0, p], gap[...])
+        cum = running_sum(ones, log_forget)
+        last = cum[length - 1 :]
+        khat = (key * jnp.where(col == last_id, jnp.exp(last - cum), 0.0)).astype(BF16)
+        decay = jnp.where(last_id == before, jnp.exp(last), 0.0)
+        decay_out[p] = decay_out[p] * decay
+        for h in range(heads):
+            at = slice(h * 128, h * 128 + 128)
+            values = pv[0, p, :, at].astype(BF16)
+            state_out[p, h] = state_out[p, h] * decay[:, at] + mm(values, khat[:, at], TN)
+
+
+def entering_state(where_ref, states, decays, place, reverse):
+    count = states.shape[0]
+    for p in range(states.shape[1]):
+        for h in range(states.shape[2]):
+            at = slice(h * 128, h * 128 + 128)
+            now = jnp.zeros(states.shape[3:], F32)
+            for k in range(count):
+                s = count - 1 - k if reverse else k
+                reached = (s > place) if reverse else (s < place)
+                new = decays[s, p, :, at] * now + states[s, p, h].astype(F32)
+                now = jnp.where(reached, new, now)
+            where_ref[p, h] = now
+
+
+def forward_kernel(
+    lens, start, gap, gain, proj, states, decays, heads_out, mixed_out, kept, state
+):
+    step = pl.program_id(0)
+    length = proj.shape[2]
+    heads = state.shape[1]
+    width = heads * 128
+
+    @pl.when(step == 0)
+    def _():
+        entering_state(state, states, decays, start[1], False)
+
+    base = start[0] + step * length
+    ones = triangle(length, False)
+    row_index = lax.broadcasted_iota(jnp.int32, (length, length), 0)
+    col_index = lax.broadcasted_iota(jnp.int32, (length, length), 1)
+    for p in range(proj.shape[1]):
+        col, row, last_id, before = block_docs(lens, p, base, length)
+        _, _, key, log_forget = gates(proj[0, p, :, width : 2 * width], gap[...])
+        cum = running_sum(ones, log_forget)
+        last = cum[length - 1 :]
+        khat = (key * jnp.where(col == last_id, jnp.exp(last - cum), 0.0)).astype(BF16)
+        decay = jnp.where(last_id == before, jnp.exp(last), 0.0)
+        qt = proj[0, p, :, :width].astype(BF16).astype(F32) * jnp.exp(cum)
+        qe = jnp.where(col == before, qt, 0.0)
+        kt = key * jnp.exp(-cum)
+        visible = (col == row) & (row_index >= col_index)
+        for h in range(heads):
+            at = slice(h * 128, h * 128 + 128)
+            values = proj[0, p, :, 2 * width + h * 128 : 2 * width + h * 128 + 128].astype(BF16)
+            gate = proj[0, p, :, 3 * width + h * 128 : 3 * width + h * 128 + 128]
+            now = state[p, h]
+            kept[0, p, h] = now
+            mixing = jnp.where(visible, mm_split(qt[:, at], kt[:, at], NT), 0.0).astype(BF16)
+            mixed = mm(mixing, values) + mm_split(qe[:, at], now, NT)
+            state[p, h] = now * decay[:, at] + mm(values, khat[:, at], TN)
+            mixed_out[0, p, :, at] = mixed
+            gated = mixed * (gate * jax.nn.sigmoid(gate))
+            scale = lax.rsqrt(jnp.mean(gated * gated, axis=-1, keepdims=True) + EPSILON)
+            heads_out[0, p, :, at] = (gated * scale * gain[:, at]).astype(BF16)
+
+
+def gate_back_kernel(
+    lens, start, gap, gain, proj, mixed_in, grad_heads, grad_out, grad_gate, group_part, state
+):
+    step = pl.program_id(0)
+    length = proj.shape[2]
+    heads = state.shape[1]
+    width = heads * 128
+
+    @pl.when(step == 0)
+    def _():
+        state[...] = jnp.zeros_like(state)
+        group_part[...] = jnp.zeros_like(group_part)
+
+    base = start[0] + (pl.num_programs(0) - 1 - step) * length
+    ones = triangle(length, False)
+    for p in range(proj.shape[1]):
+        col, _, last_id, before = block_docs(lens, p, base, length)
+        _, _, _, log_forget = gates(proj[0, p, :, width : 2 * width], gap[...])
+        cum = running_sum(ones, log_forget)
+        decay = jnp.where(last_id == before, jnp.exp(cum[length - 1 :]), 0.0)
+        qt = proj[0, p, :, :width].astype(BF16).astype(F32) * jnp.exp(cum)
+        qe = jnp.where(col == before, qt, 0.0).astype(BF16)
+        for h in range(heads):
+            at = slice(h * 128, h * 128 + 128)
+            gate = proj[0, p, :, 3 * width + h * 128 : 3 * width + h * 128 + 128]
+            mixed = mixed_in[0, p, :, at]
+            incoming = grad_heads[0, p, :, at].astype(F32)
+            sigma = jax.nn.sigmoid(gate)
+            act = gate * sigma
+            gated = mixed * act
+            scale = lax.rsqrt(jnp.mean(gated * gated, axis=-1, keepdims=True) + EPSILON)
+            group_part[:, at] += jnp.sum(incoming * gated * scale, axis=0, keepdims=True)
+            weighted = incoming * gain[:, at]
+            inner = jnp.mean(weighted * gated, axis=-1, keepdims=True)
+            grad_gated = scale * weighted - gated * (scale * scale * scale) * inner
+            grad = grad_gated * act
+            grad_out[0, p, :, at] = grad
+            slope = sigma * (1.0 + gate * (1.0 - sigma))
+            grad_gate[0, p, :, at] = (grad_gated * mixed * slope).astype(BF16)
+            high, low = split_two(grad)
+            own = mm(high, qe[:, at], TN) + mm(low, qe[:, at], TN)
+            state[p, h] = state[p, h] * decay[:, at] + own
+
+
+def backward_kernel(
+    lens, start, gap, proj, grad_out, grad_gate, kept, states, decays, grad_proj, gap_part, state
+):
+    step = pl.program_id(0)
+    length = proj.shape[2]
+    heads = state.shape[1]
+    width = heads * 128
+
+    @pl.when(step == 0)
+    def _():
+        entering_state(state, states, decays, start[1], True)
+        gap_part[...] = jnp.zeros_like(gap_part)
+
+    base = start[0] + (pl.num_programs(0) - 1 - step) * length
+    ones = triangle(length, False)
+    ones_up = triangle(length, True)
+    row_index = lax.broadcasted_iota(jnp.int32, (length, length), 0)
+    col_index = lax.broadcasted_iota(jnp.int32, (length, length), 1)
+    for p in range(proj.shape[1]):
+        col, row, last_id, before = block_docs(lens, p, base, length)
+        open_gate, gap_gate, key, log_forget = gates(proj[0, p, :, width : 2 * width], gap[...])
+        cum = running_sum(ones, log_forget)
+        last = cum[length - 1 :]
+        ecum = jnp.exp(cum)
+        encum = jnp.exp(-cum)
+        tail = jnp.where(col == last_id, jnp.exp(last - cum), 0.0)
+        khat = (key * tail).astype(BF16)
+        decay = jnp.where(last_id == before, jnp.exp(last), 0.0)
+        qt = proj[0, p, :, :width].astype(BF16).astype(F32) * ecum
+        enters = col == before
+        qe = jnp.where(enters, qt, 0.0).astype(BF16)
+        qt = qt.astype(BF16)
+        kt = (key * encum).astype(BF16)
+        visible = (col == row) & (row_index >= col_index)
+        for h in range(heads):
+            at = slice(h * 128, h * 128 + 128)
+            values = proj[0, p, :, 2 * width + h * 128 : 2 * width + h * 128 + 128].astype(BF16)
+            grad = grad_out[0, p, :, at]
+            grad_enter = jnp.where(enters, grad, 0.0)
+            grad, grad_low = split_two(grad)
+            after = state[p, h]
+            after_high, after_low = split_two(after)
+            now = kept[0, p, h]
+            mixing = jnp.where(visible, mm(qt[:, at], kt[:, at], NT), 0.0).astype(BF16)
+            grad_mixing = mm(grad, values, NT) + mm(grad_low, values, NT)
+            grad_mixing = jnp.where(visible, grad_mixing, 0.0).astype(BF16)
+            grad_qt = mm(grad_mixing, kt[:, at]) + mm_split(grad_enter, now)
+            grad_kt = mm(grad_mixing, qt[:, at], TN)
+            grad_values = mm(mixing, grad, TN) + mm(khat[:, at], after_high, NT)
+            grad_khat = mm(values, after_high) + mm(values, after_low)
+            grad_decay = jnp.sum(after * now, axis=0, keepdims=True)
+            own = mm(grad, qe[:, at], TN) + mm(grad_low, qe[:, at], TN)
+            state[p, h] = after * decay[:, at] + own
+            through = grad_khat * khat[:, at].astype(F32)
+            grad_cum = (
+                grad_qt * qt[:, at].astype(F32) - grad_kt * kt[:, at].astype(F32) - through
+            )
+            grad_last = jnp.sum(through, axis=0, keepdims=True) + grad_decay * decay[:, at]
+            grad_log = running_sum(ones_up, grad_cum) + grad_last
+            grad_keys = grad_kt * encum[:, at] + grad_khat * tail[:, at]
+            grad_gap = grad_keys - grad_log / (1.0 - gap_gate[:, at])
+            gap_part[:, at] += jnp.sum(grad_gap * open_gate[:, at], axis=0, keepdims=True)
+            grad_forget = -grad_gap * gap_gate[:, at] * (1.0 - open_gate[:, at])
+            grad_proj[0, p, :, at] = (grad_qt * ecum[:, at]).astype(BF16)
+            grad_proj[0, p, :, width + h * 128 : width + h * 128 + 128] = grad_forget.astype(BF16)
+            grad_proj[0, p, :, 2 * width + h * 128 : 2 * width + h * 128 + 128] = (
+                grad_values.astype(BF16)
+            )
+        grad_proj[0, p, :, 3 * width :] = grad_gate[0, p]
+
+
+def recur_call(kernel, steps, half, reverse, ins, outs, scratch, flops, name):
+    def index(kind):
+        def rows(j):
+            b = steps - 1 - j if reverse else j
+            return (b // half, 0, b % half, kind if isinstance(kind, int) else 0)
+
+        def block(j):
+            return (steps - 1 - j if reverse else j, 0, 0, 0, 0)
+
+        return rows if isinstance(kind, int) else block
+
+    in_specs, arrays = [], []
+    for array, kind, shape in ins:
+        arrays.append(array)
+        if kind == "smem":
+            in_specs.append(pl.BlockSpec(memory_space=pltpu.SMEM))
+        elif kind == "whole":
+            in_specs.append(pl.BlockSpec(array.shape, lambda j, n=array.ndim: (0,) * n))
+        else:
+            in_specs.append(pl.BlockSpec(shape, index(kind)))
+    out_specs, out_shapes = [], []
+    for shape, dtype, kind, block in outs:
+        out_shapes.append(jax.ShapeDtypeStruct(shape, dtype))
+        if kind == "whole":
+            out_specs.append(pl.BlockSpec(shape, lambda j, n=len(shape): (0,) * n))
+        else:
+            out_specs.append(pl.BlockSpec(block, index(kind)))
+    moved = sum(a.size * a.dtype.itemsize for a in arrays)
+    return pl.pallas_call(
+        kernel,
+        grid=(steps,),
+        in_specs=in_specs,
+        out_specs=out_specs,
+        out_shape=out_shapes,
+        scratch_shapes=scratch,
+        compiler_params=pltpu.CompilerParams(
+            dimension_semantics=("arbitrary",), vmem_limit_bytes=48 << 20
+        ),
+        cost_estimate=pl.CostEstimate(flops=flops, bytes_accessed=moved, transcendentals=0),
+        name=name,
+    )(*arrays)
+
+
+def swap(value, across):
+    return lax.ppermute(value, "seq", [(i, i ^ across) for i in range(lax.axis_size("seq"))])
+
+
+CORE, XLINK, YLINK = 1, 2, 4
+TILE = 128
+
+
+def plane_gather(own):
+    half = own.shape[0] // 2
+    got = {0: own, XLINK: swap(own, XLINK), YLINK: swap(own, YLINK), CORE: swap(own, CORE)}
+    first = swap(got[YLINK][:half], XLINK)
+    second = swap(got[XLINK][half:], YLINK)
+    got[XLINK + CORE] = swap(got[XLINK], CORE)
+    got[YLINK + CORE] = swap(got[YLINK], CORE)
+    got[XLINK + YLINK] = jnp.concatenate([first, second])
+    got[XLINK + YLINK + CORE] = jnp.concatenate([swap(first, CORE), swap(second, CORE)])
+    return got
+
+
+def add_low(a, b):
+    return (a.astype(F32) + b.astype(F32)).astype(BF16)
+
+
+def plane_scatter(parts):
+    half = parts[0].shape[0] // 2
+    chip = {}
+    for a in (6, 2, 4, 0):
+        chip[a] = add_low(parts[a], swap(parts[a ^ CORE], CORE))
+    from_x = swap(chip[6][:half], XLINK)
+    from_y = swap(chip[6][half:], YLINK)
+    mine_x = swap(chip[2][:half], XLINK)
+    mine_y = swap(chip[4][half:], YLINK)
+    last_y = swap(add_low(chip[4][:half], from_x), YLINK)
+    last_x = swap(add_low(chip[2][half:], from_y), XLINK)
+    low = chip[0][:half].astype(F32) + mine_x.astype(F32) + last_y.astype(F32)
+    high = chip[0][half:].astype(F32) + mine_y.astype(F32) + last_x.astype(F32)
+    return jnp.concatenate([low, high])
+
+
+def pick(array, index, axis):
+    return lax.dynamic_index_in_dim(array, index, axis, keepdims=False)
+
+
+def plane_device(
+    tokens,
+    norm1_gain,
+    w_mix_in,
+    forget_gap,
+    group_gain,
+    w_mix_out,
+    norm2_gain,
+    w_gate_up,
+    w_down,
+    doc_lengths,
+    out_cotangent,
+):
+    seq_count, mp_count = lax.axis_size("seq"), lax.axis_size("mp")
+    seq_index, mp_index = lax.axis_index("seq"), lax.axis_index("mp")
+    core, chip = seq_index % 2, seq_index // 2
+    chips = seq_count // 2
+    span, packs, width = tokens.shape
+    rows = span * packs
+    run = span * mp_count
+    heads, head_size = forget_gap.shape
+    chans = heads * head_size
+    hidden_units = w_gate_up.shape[2]
+    slice_d = width // seq_count
+
+    def pack_major(array):
+        return jnp.transpose(array, (1, 0, 2)).reshape(rows, width)
+
+    def token_major(array):
+        return jnp.transpose(array.reshape(packs, span, width), (1, 0, 2))
+
+    own = pack_major(tokens)
+    scale_one = rms_scale(own)
+    normed = (own * scale_one * norm1_gain).astype(BF16)
+    in_flat = w_mix_in.reshape(width, 4 * chans)
+    normed_all = lax.all_gather(normed, "mp", axis=0, tiled=True)
+
+    cot_own = pack_major(lax.dynamic_slice_in_dim(out_cotangent, mp_index * span, span, 0))
+    cot = plane_gather(cot_own.astype(BF16))
+
+    share = -(-hidden_units // (chips * TILE)) * TILE
+    local_ff = 2 * share
+    spare = share * chips - hidden_units
+    begin = jnp.minimum(chip * share, hidden_units - share)
+    gu_part = lax.dynamic_slice_in_dim(pick(w_gate_up, core, 1), begin, share, 1)
+    dn_part = lax.dynamic_slice_in_dim(w_down, begin, share, 0)
+    fresh = lax.broadcasted_iota(jnp.int32, (share, 1), 0) >= chip * share - begin
+    dn_part = jnp.where(fresh, dn_part, jnp.zeros_like(dn_part))
+    dn_part = lax.dynamic_slice_in_dim(dn_part, core * (share // 2), share // 2, 0)
+
+    def collect(part):
+        pairs = lax.all_gather(part, "mp", axis=0).reshape((2, 2) + part.shape)
+        mine = pick(pairs, core, 0)
+        other = swap(pick(pairs, 1 - core, 0), CORE)
+        return jnp.where(core == 0, mine, other), jnp.where(core == 0, other, mine)
+
+    normed_all, in_flat, gu_part, dn_part, cot = lax.optimization_barrier(
+        (normed_all, in_flat, gu_part, dn_part, cot)
+    )
+    w_gate, w_up = collect(gu_part)
+    w_gu = jnp.concatenate([w_gate[0], w_gate[1], w_up[0], w_up[1]], axis=1)
+    w_dn = jnp.concatenate(collect(dn_part), axis=1).reshape(local_ff, width)
+
+    projected = mm(normed_all, in_flat).reshape(mp_count, packs, span, 4 * chans)
+
+    start = jnp.stack([seq_index * run, seq_index]).astype(jnp.int32)
+    gap_row = forget_gap.reshape(1, chans)
+    gain_row = group_gain.reshape(1, chans)
+    steps, half = run // BLOCK, span // BLOCK
+    block = (1, packs, BLOCK, chans)
+    wide = (1, packs, BLOCK, 4 * chans)
+    state_shape = (packs, heads, head_size, head_size)
+    unit = 2 * BLOCK * head_size * head_size * packs * heads * steps
+    common = [(doc_lengths, "smem", None), (start, "smem", None), (gap_row, "whole", None)]
+    run_state, run_decay = recur_call(
+        states_kernel,
+        steps,
+        half,
+        False,
+        common + [(projected, 1, block), (projected, 2, block)],
+        [(state_shape, F32, "whole", None), ((packs, 1, chans), F32, "whole", None)],
+        [],
+        3 * unit,
+        "run_states",
+    )
+    all_states = lax.all_gather(run_state.astype(BF16), "seq")
+    all_decays = lax.all_gather(run_decay, "seq")
+    row_shape = (mp_count, packs, span, chans)
+    heads_out, mixed, kept = recur_call(
+        forward_kernel,
+        steps,
+        half,
+        False,
+        common
+        + [
+            (gain_row, "whole", None),
+            (projected, 0, wide),
+            (all_states, "whole", None),
+            (all_decays, "whole", None),
+        ],
+        [
+            (row_shape, BF16, 0, block),
+            (row_shape, F32, 0, block),
+            ((steps,) + state_shape, F32, "block", (1,) + state_shape),
+        ],
+        [pltpu.VMEM(state_shape, F32)],
+        6 * unit,
+        "mix_forward",
+    )
+    heads_tok = lax.all_to_all(
+        heads_out.reshape(mp_count, rows, chans), "mp", split_axis=0, concat_axis=0, tiled=True
+    )
+    heads_tok = jnp.transpose(heads_tok, (1, 0, 2)).reshape(rows, mp_count * chans)
+    out_flat = w_mix_out.reshape(-1, width)
+    hidden = own + mm(heads_tok, out_flat)
+    scale_two = rms_scale(hidden)
+    normed_two = (hidden * scale_two * norm2_gain).astype(BF16)
+
+    two = plane_gather(normed_two)
+    groups = ((6, 7), (2, 3, 4, 5), (0, 1))
+    act_of, pre_of, two_of, cot_of = {}, {}, {}, {}
+    down_parts = {}
+    for group in reversed(groups):
+        two_of[group] = jnp.concatenate([two[a] for a in group])
+        cot_of[group] = jnp.concatenate([cot[a] for a in group])
+        pre = mm(two_of[group], w_gu)
+        pre_of[group] = pre
+        act_of[group] = (jax.nn.silu(pre[:, :local_ff]) * pre[:, local_ff:]).astype(BF16)
+    for group in groups:
+        made = mm(act_of[group], w_dn).astype(BF16)
+        for k, a in enumerate(group):
+            down_parts[a] = made[k * rows : k * rows + rows]
+    back_parts, grad_of = {}, {}
+    for group in groups:
+        pre_gate, pre_up = pre_of[group][:, :local_ff], pre_of[group][:, local_ff:]
+        grad_act = mm(cot_of[group], w_dn, NT)
+        grad_of[group] = jnp.concatenate(
+            [grad_act * pre_up * silu_slope(pre_gate), grad_act * jax.nn.silu(pre_gate)], axis=1
+        ).astype(BF16)
+        made = mm(grad_of[group], w_gu, NT).astype(BF16)
+        for k, a in enumerate(group):
+            back_parts[a] = made[k * rows : k * rows + rows]
+    grad_normed_two = plane_scatter(back_parts)
+    gu_grad = sum(mm(two_of[g], grad_of[g], TN) for g in groups).astype(BF16)
+    dn_grad = sum(mm(act_of[g], cot_of[g], TN) for g in groups).astype(BF16)
+    grad_normed_two, gu_grad, dn_grad, down_parts = lax.optimization_barrier(
+        (grad_normed_two, gu_grad, dn_grad, down_parts)
+    )
+    layer_out = token_major(hidden + plane_scatter(down_parts))
+
+    norm2_part = jnp.sum(grad_normed_two * hidden * scale_two, axis=0)
+    grad_hidden = cot_own + rms_back(grad_normed_two, hidden, scale_two, norm2_gain)
+    grad_mix = grad_hidden.astype(BF16)
+    grad_tok = mm(grad_mix, out_flat, NT).astype(BF16)
+    grad_tok = jnp.transpose(grad_tok.reshape(rows, mp_count, chans), (1, 0, 2))
+    grad_heads = lax.all_to_all(grad_tok, "mp", split_axis=0, concat_axis=0, tiled=True)
+    grad_heads = grad_heads.reshape(row_shape)
+
+    def deliver(parts):
+        mine = pick(parts, core, 0)
+        other = swap(pick(parts, 1 - core, 0), CORE)
+        low = jnp.where(core == 0, mine, other)
+        high = jnp.where(core == 0, other, mine)
+        return lax.psum_scatter(
+            jnp.concatenate([low, high]), "mp", scatter_dimension=0, tiled=True
+        )[0]
+
+    def hand_round(piece):
+        got = [pick(piece, chip, 0)]
+        got += [swap(pick(piece, chip ^ a, 0), 2 * a) for a in range(1, chips)]
+        got = jnp.stack(got)
+        return [pick(got, chip ^ c, 0) for c in range(chips)]
+
+    gu_grad = gu_grad.reshape(chips, 2, slice_d, 2, 2, share)
+    gu_grad = jnp.transpose(gu_grad, (1, 4, 3, 0, 2, 5))
+    got = [q.astype(F32) for q in hand_round(jnp.transpose(deliver(gu_grad), (1, 0, 2, 3)))]
+    got[-1] = got[-1][:, :, spare:]
+    gate_up_grad = jnp.transpose(jnp.concatenate(got, axis=-1), (1, 0, 2))
+    dn_grad = dn_grad.reshape(2, share, chips, 2, slice_d)
+    got = hand_round(deliver(jnp.transpose(dn_grad, (3, 0, 2, 1, 4))))
+    got[-1] = got[-1][spare:]
+    down_grad = jnp.concatenate(got, axis=0).astype(F32)
+
+    out_grad = mm(heads_tok, grad_mix, TN).astype(BF16)
+    out_grad = out_grad.reshape(mp_count * heads, seq_count, head_size // seq_count, width)
+    out_grad = plane_scatter(
+        {a: pick(out_grad, seq_index ^ a, 1) for a in range(seq_count)}
+    ).astype(BF16)
+    mix_out_grad = lax.psum_scatter(out_grad, "mp", scatter_dimension=0, tiled=True).astype(F32)
+
+    grad_out, grad_gate, group_part, run_grad = recur_call(
+        gate_back_kernel,
+        steps,
+        half,
+        True,
+        common
+        + [
+            (gain_row, "whole", None),
+            (projected, 0, wide),
+            (mixed, 0, block),
+            (grad_heads, 0, block),
+        ],
+        [
+            (row_shape, F32, 0, block),
+            (row_shape, BF16, 0, block),
+            ((1, chans), F32, "whole", None),
+            (state_shape, F32, "whole", None),
+        ],
+        [],
+        3 * unit,
+        "gate_back",
+    )
+    all_grads = lax.all_gather(run_grad.astype(BF16), "seq")
+    grad_projected, gap_part = recur_call(
+        backward_kernel,
+        steps,
+        half,
+        True,
+        common
+        + [
+            (projected, 0, wide),
+            (grad_out, 0, block),
+            (grad_gate, 0, block),
+            (kept, "block", (1,) + state_shape),
+            (all_grads, "whole", None),
+            (all_decays, "whole", None),
+        ],
+        [((mp_count, packs, span, 4 * chans), BF16, 0, wide), ((1, chans), F32, "whole", None)],
+        [pltpu.VMEM(state_shape, F32)],
+        12 * unit,
+        "mix_backward",
+    )
+    grad_flat = grad_projected.reshape(mp_count * rows, 4 * chans)
+    back_in = mm(grad_flat, in_flat, NT)
+    norm1_part = jnp.sum(back_in * normed_all.astype(F32), axis=0) / norm1_gain
+    grad_normed = lax.psum_scatter(
+        back_in.astype(BF16), "mp", scatter_dimension=0, tiled=True
+    ).astype(F32)
+    in_grad = mm(normed_all, grad_flat, TN).astype(BF16)
+    in_grad = in_grad.reshape(seq_count, slice_d, 4 * chans)
+    mix_in_grad = plane_scatter(
+        {a: pick(in_grad, seq_index ^ a, 0) for a in range(seq_count)}
+    ).reshape(slice_d, 4, chans)
+
+    tokens_grad = token_major(
+        grad_hidden + rms_back(grad_normed, own, scale_one, norm1_gain)
+    )
+    small = jnp.stack([group_part, gap_part]).reshape(2, heads, head_size)
+    small = lax.psum_scatter(small, "seq", scatter_dimension=2, tiled=True)
+    norm1_grad = lax.psum_scatter(norm1_part, ("seq", "mp"), scatter_dimension=0, tiled=True)
+    norm2_grad = lax.psum_scatter(norm2_part, ("seq", "mp"), scatter_dimension=0, tiled=True)
+    return (
+        layer_out,
+        tokens_grad,
+        norm1_grad,
+        mix_in_grad,
+        small[1],
+        small[0],
+        mix_out_grad,
+        norm2_grad,
+        gate_up_grad,
+        down_grad,
+    )
+
+
 def solution(mesh):
+    body = plane_device if dict(mesh.shape) == {"seq": 8, "mp": 4} else generic_device
     placed = (
         P(("seq", "mp"), None, None),
         P(),
@@ -365,7 +975,7 @@
         P("seq", None, None),
     )
     return jax.shard_map(
-        on_device,
+        body,
         mesh=mesh,
         in_specs=placed,
         out_specs=(

time: 2180 us -> 1440 us (0.66)
  waiting for transfers between devices: 1190 us -> 503 us
  matrix products: 395 us -> 300 us
  other arithmetic: 188 us -> 94.2 us
  blocking collectives: 116 us -> 199 us
  Pallas kernels: 0 us -> 80.4 us
  local copies, waits for them, and re-layouts: 262 us -> 186 us
  starting transfers between devices: 5.42 us -> 47 us
    reduce_scatter x5 -> x4, waiting for transfers between devices: 705 us -> 109 us  [the longest x1 109 us: plane_device(): lax.psum_scatter(back_in.astype(BF16), 'mp', scatter_dimension=0, tiled=T...]
    ppermute x0 -> x68, waiting for transfers between devices: none -> 288 us  [swap(): lax.ppermute(value, 'seq', [(i, i ^ across) for i in range(lax.axis_size(...]
    unnamed x15 -> x11, waiting for transfers between devices: 194 us -> 1.34 us
    all_gather x4 -> x5, waiting for transfers between devices: 251 us -> 105 us  [the longest x2 51 us: collect(): pairs = lax.all_gather(part, 'mp', axis=0).reshape((2, 2) + part.shape)]
    dot_general x26 -> x24, matrix products: 395 us -> 300 us  [mm(): return lax.dot_general(a, b, (dims, ((), ())), preferred_element_type=F32)]
    all_to_all x1 -> x2, blocking collectives: 53 us -> 135 us  [the longest x1 86 us: plane_device(): lax.all_to_all(heads_out.reshape(mp_count, rows, chans), 'mp', split_axis...]
    pallas_call x0 -> x4, Pallas kernels: none -> 80.4 us  [recur_call(): pl.pallas_call(kernel, grid=(steps,), in_specs=in_specs, out_specs=out_sp...]
    reshape x13 -> x7, local copies, waits for them, and re-layouts: 89.2 us -> 35.2 us  [the longest x1 13.6 us: plane_device(): gu_grad = gu_grad.reshape(chips, 2, slice_d, 2, 2, share)]
  transfers between devices with their start and end apart: 13 -> 78, of which waited for: 9 -> 34; matrix products, arithmetic and copies ran while one was open for 21% -> 32% of each run, Pallas kernels for 0% -> 4%
where the time goes in v1:
time: 1440 us; the launch traced here: 1430 us
  waiting for transfers between devices  503 us (35%)
  matrix products  300 us (21%)
  blocking collectives  199 us (14%)
  local copies, waits for them, and re-layouts  186 us (13%)
  other arithmetic  94.2 us (7%)
  Pallas kernels  80.4 us (6%)
  starting transfers between devices  47 us (3%)
  between operations  15.5 us (1%)
    dot_general x24, matrix products, mm(): return lax.dot_general(a, b, (dims, ((), ())), preferred_element_type=F32)  300 us
    ppermute x68, waiting for transfers between devices, swap(): lax.ppermute(value, 'seq', [(i, i ^ across) for i in range(lax.axis_size(...  288 us
    reduce_scatter x1, waiting for transfers between devices, plane_device(): lax.psum_scatter(back_in.astype(BF16), 'mp', scatter_dimension=0, tiled=T...  109 us
    all_to_all x1, blocking collectives, plane_device(): lax.all_to_all(heads_out.reshape(mp_count, rows, chans), 'mp', split_axis...  86 us
    pallas_call x4, Pallas kernels, recur_call(): pl.pallas_call(kernel, grid=(steps,), in_specs=in_specs, out_specs=out_sp...  80.4 us
    unnamed x167, local copies, waits for them, and re-layouts  67.4 us
    unnamed x1, blocking collectives  55.5 us
    all_gather x2, waiting for transfers between devices, collect(): pairs = lax.all_gather(part, 'mp', axis=0).reshape((2, 2) + part.shape)  51 us
  transfers between devices with their start and end apart: 78, of which 34 were waited for; matrix products, arithmetic and copies ran while one was open for 32% of the time, Pallas kernels for 4%

profile of v1, /device:TPU:0, one launch (start us, length us, event | category | flops | bytes accessed | tf_op | source)
XLA Modules:
  0.0 1425.3 jit_solution(4413659306646455060)
XLA Ops:
  33.6 44.4 %collective-permute-done.3 = bf16[512,2048]{1,0:T(8,128)(2,1)} collective-permute-done((bf16[512,2048]{1,0:T(8,128)(2,1)}, bf16[512,2048]{1,0:T(8,128)(2,1)}, u32[]{:S(2)}, u32[]{:S(2)}) %collective-permute-start.3) | collective-permute-done | bytes 2097184 | tf_op jit(solution)/shard_map/ppermute | solution.py:654
  84.5 19.3 %collective-permute-done.5 = bf16[256,2048]{1,0:T(8,128)(2,1)} collective-permute-done((bf16[256,2048]{1,0:T(8,128)(2,1)S(1)}, bf16[256,2048]{1,0:T(8,128)(2,1)}, u32[]{:S(2)}, u32[]{:S(2)}) %collective-permute-start.5) | collective-permute-done | bytes 1048608 | tf_op jit(solution)/shard_map/ppermute | solution.py:654
  134.7 37.7 %all-gather.11.cloned.1.call-done = bf16[2048,2048]{1,0:T(8,128)(2,1)} async-done(((bf16[512,2048]{1,0:T(8,128)(2,1)}), bf16[2048,2048]{1,0:T(8,128)(2,1)}) %all-gather.11.cloned.1.call-update) | async-done | bytes 8388624 | tf_op jit(solution)/shard_map/all_gather | solution.py:732
  172.3 24.4 %fusion.40 = f32[2048,2048]{1,0:T(8,128)} fusion(bf16[2048,2048]{1,0:T(8,128)(2,1)} %all-gather.11.cloned.1.call-done, bf16[2048,2048]{1,0:T(8,128)(2,1)} %bitcast.271), kind=kOutput, calls=%fused_computation.204 | convolution fusion | flops 17179869184 | bytes 33554432 | tf_op jit(solution)/shard_map/dot_general | solution.py:364
  218.1 15.9 %all-gather.13.cloned.1.call-done = bf16[16,4,128,128]{3,2,1,0:T(8,128)(2,1)} async-done(((bf16[2,4,128,128]{3,2,1,0:T(8,128)(2,1)}), bf16[16,4,128,128]{3,2,1,0:T(8,128)(2,1)}) %all-gather.13.cloned.1.call-update) | async-done | bytes 2097168 | tf_op jit(solution)/shard_map/all_gather | solution.py:782
  235.5 20.0 %mix_forward.1 = (bf16[4,2,256,512]{3,2,1,0:T(8,128)(2,1)S(1)}, f32[4,2,256,512]{3,2,1,0:T(8,128)}, f32[8,2,4,128,128]{4,3,2,1,0:T(8,128)}) custom-call(s32[2,4]{1,0:T(2,128)S(1)} %copy-done.3, s32[2]{0:T(128)S(1)} %pad_add_fusion.start, f32[1,512]{1,0:T(1,128)S(1)} %bitcast.243, f32[1,512]{1,0:T(1,128)S(1)} %bitcast.246, f32[4,2,256,2048]{3,2,1,0:T(8,128)} %bitcast.252, ...), custom_call_target="tpu_custom_call" | custom-call | flops 1610612736 | bytes 18911272 | tf_op jit(solution)/shard_map/mix_forward/pallas_call | solution.py:638
  257.9 86.0 %all_to_all.10 = bf16[4,512,512]{1,2,0:T(8,128)(2,1)S(1)} all-to-all(bf16[4,512,512]{1,2,0:T(8,128)(2,1)} %copy.120), channel_id=1, replica_groups=mesh['seq'=8,'mp'=4] {'mp'}, dimensions={0} | all-to-all | bytes 4194304 | tf_op jit(solution)/shard_map/all_to_all | solution.py:806
  378.6 24.3 %collective-permute-done.13 = bf16[512,2048]{1,0:T(8,128)(2,1)} collective-permute-done((bf16[512,2048]{1,0:T(8,128)(2,1)}, bf16[512,2048]{1,0:T(8,128)(2,1)}, u32[]{:S(2)}, u32[]{:S(2)}) %collective-permute-start.13) | collective-permute-done | bytes 2097184 | tf_op jit(solution)/shard_map/ppermute | solution.py:654
  402.8 51.0 %all-gather.17.cloned.1.call-done = bf16[8192,384]{1,0:T(8,128)(2,1)} async-done(((bf16[2048,384]{1,0:T(8,128)(2,1)}), bf16[8192,384]{1,0:T(8,128)(2,1)}) %all-gather.17.cloned.1.call-update) | async-done | bytes 6291472 | tf_op jit(solution)/shard_map/all_gather | solution.py:748
  466.8 18.6 %collective-permute-done.20 = bf16[256,2048]{1,0:T(8,128)(2,1)S(1)} collective-permute-done((bf16[256,2048]{1,0:T(8,128)(2,1)S(1)}, bf16[256,2048]{1,0:T(8,128)(2,1)S(1)}, u32[]{:S(2)}, u32[]{:S(2)}) %collective-permute-start.20) | collective-permute-done | bytes 1048608 | tf_op jit(solution)/shard_map/ppermute | solution.py:654
  501.2 21.2 %fusion.30 = f32[2048,1536]{0,1:T(8,128)} fusion(bf16[2048,2048]{1,0:T(8,128)(2,1)} %copy-done.43, bf16[2048,384]{1,0:T(8,128)(2,1)} %get-tuple-element.178, bf16[2048,384]{1,0:T(8,128)(2,1)} %get-tuple-element.177, bf16[2048,384]{1,0:T(8,128)(2,1)} %get-tuple-element.219, bf16[2048,384]{1,0:T(8,128)(2,1)} %get-tuple-element.220), kind=kOutput, calls=%fused_computation.194 | convolution fusion | flops 12910067712 | bytes 27262976 | tf_op jit(solution)/shard_map/dot_general | solution.py:364
  522.4 15.7 %multiply_convert_fusion.2 = (bf16[2048,768]{0,1:T(8,128)(2,1)}, bf16[2048,768]{0,1:T(8,128)(2,1)}, bf16[2048,768]{0,1:T(8,128)(2,1)S(1)}) fusion(f32[2048,1536]{0,1:T(8,128)} %fusion.30, bf16[2048,2048]{1,0:T(8,128)(2,1)} %get-tuple-element.218, bf16[768,2048]{1,0:T(8,128)(2,1)S(1)} %bitcast.283), kind=kOutput, calls=%fused_computation.12 | convolution fusion | flops 6466043904 | bytes 33554432 | tf_op jit(solution)/shard_map/dot_general | solution.py:364
  558.4 11.4 fusion.29
  584.7 17.5 %fusion.7 = f32[2048,1536]{1,0:T(8,128)} fusion(bf16[2048,2048]{1,0:T(8,128)(2,1)} %copy-done.43, bf16[2048,768]{0,1:T(8,128)(2,1)S(1)} %copy-done.62, bf16[2048,768]{0,1:T(8,128)(2,1)S(1)} %copy-done.61), kind=kOutput, calls=%fused_computation.47 | convolution fusion | flops 12897484800 | bytes 27262976 | tf_op jit(solution)/shard_map/dot_general | solution.py:364
  607.4 19.6 %convolution_convert_fusion.3 = bf16[2048,2048]{1,0:T(8,128)(2,1)} fusion(bf16[2048,768]{0,1:T(8,128)(2,1)} %get-tuple-element.123, bf16[2048,768]{0,1:T(8,128)(2,1)} %get-tuple-element.122, bf16[2048,384]{1,0:T(8,128)(2,1)} %get-tuple-element.178, bf16[2048,384]{1,0:T(8,128)(2,1)} %get-tuple-element.177, bf16[2048,384]{1,0:T(8,128)(2,1)} %get-tuple-element.219, ...), kind=kOutput, calls=%fused_computation.5 | convolution fusion | flops 12926844928 | bytes 20971520 | tf_op jit(solution)/shard_map/dot_general | solution.py:364
  627.0 12.1 fusion.11
  674.4 13.0 fusion.10
  687.4 16.4 %add_convert_fusion = bf16[2048,1536]{1,0:T(8,128)(2,1)} fusion(f32[2048,1536]{1,0:T(8,128)} %fusion.10, f32[2048,1536]{1,0:T(8,128)} %fusion.7, bf16[1024,2048]{1,0:T(8,128)(2,1)} %copy-done.44, bf16[1024,768]{0,1:T(8,128)(2,1)S(1)} %copy-done.58, bf16[1024,768]{0,1:T(8,128)(2,1)S(1)} %copy-done.57), kind=kOutput, calls=%fused_computation.1 | convolution fusion | flops 6458179584 | bytes 38797312 | tf_op jit(solution)/shard_map/dot_general | solution.py:364
  741.8 13.6 collective-permute-done.28
  761.0 20.2 %collective-permute-done.18 = bf16[256,2048]{1,0:T(8,128)(2,1)S(1)} collective-permute-done((bf16[256,2048]{1,0:T(8,128)(2,1)}, bf16[256,2048]{1,0:T(8,128)(2,1)S(1)}, u32[]{:S(2)}, u32[]{:S(2)}) %collective-permute-start.18) | collective-permute-done | bytes 1048608 | tf_op jit(solution)/shard_map/ppermute | solution.py:654
  781.3 21.1 %collective-permute-done.29 = bf16[256,2048]{1,0:T(8,128)(2,1)S(1)} collective-permute-done((bf16[256,2048]{1,0:T(8,128)(2,1)S(1)}, bf16[256,2048]{1,0:T(8,128)(2,1)S(1)}, u32[]{:S(2)}, u32[]{:S(2)}) %collective-permute-start.29) | collective-permute-done | bytes 1048608 | tf_op jit(solution)/shard_map/ppermute | solution.py:654
  815.7 19.5 %collective-permute-done.38 = bf16[256,2048]{1,0:T(8,128)(2,1)S(1)} collective-permute-done((bf16[256,2048]{1,0:T(8,128)(2,1)S(1)}, bf16[256,2048]{1,0:T(8,128)(2,1)S(1)}, u32[]{:S(2)}, u32[]{:S(2)}) %collective-permute-start.38) | collective-permute-done | bytes 1048608 | tf_op jit(solution)/shard_map/ppermute | solution.py:654
  836.4 24.2 %collective-permute-done.35 = bf16[256,2048]{1,0:T(8,128)(2,1)S(1)} collective-permute-done((bf16[256,2048]{1,0:T(8,128)(2,1)S(1)}, bf16[256,2048]{1,0:T(8,128)(2,1)S(1)}, u32[]{:S(2)}, u32[]{:S(2)}) %collective-permute-start.35) | collective-permute-done | bytes 1048608 | tf_op jit(solution)/shard_map/ppermute | solution.py:654
  864.2 18.0 %collective-permute-done.39 = bf16[256,2048]{1,0:T(8,128)(2,1)S(1)} collective-permute-done((bf16[256,2048]{1,0:T(8,128)(2,1)S(1)}, bf16[256,2048]{1,0:T(8,128)(2,1)S(1)}, u32[]{:S(2)}, u32[]{:S(2)}) %collective-permute-start.39) | collective-permute-done | bytes 1048608 | tf_op jit(solution)/shard_map/ppermute | solution.py:654
  896.2 48.7 %all_to_all.11 = bf16[4,512,512]{2,1,0:T(8,128)(2,1)S(1)} all-to-all(bf16[4,512,512]{2,1,0:T(8,128)(2,1)S(1)} %bitcast.275), channel_id=1, replica_groups=mesh['seq'=8,'mp'=4] {'mp'}, dimensions={0} | all-to-all | bytes 4194304 | tf_op jit(solution)/shard_map/all_to_all | solution.py:852
  944.9 15.2 %gate_back.1 = (f32[4,2,256,512]{3,2,1,0:T(8,128)}, bf16[4,2,256,512]{3,2,1,0:T(8,128)(2,1)S(1)}, f32[1,512]{1,0:T(1,128)S(1)}, f32[2,4,128,128]{3,2,1,0:T(8,128)S(1)}) custom-call(s32[2,4]{1,0:T(2,128)S(1)} %copy-done.3, s32[2]{0:T(128)S(1)} %pad_add_fusion.start, f32[1,512]{1,0:T(1,128)S(1)} %bitcast.244, f32[1,512]{1,0:T(1,128)S(1)} %bitcast.247, ...), custom_call_target="tpu_custom_call" | custom-call | flops 805306368 | bytes 23072808 | tf_op jit(solution)/shard_map/gate_back/pallas_call | solution.py:638
  1012.8 13.6 reshape.213
  1074.7 35.0 %mix_backward.1 = (bf16[4,2,256,2048]{3,2,1,0:T(8,128)(2,1)}, f32[1,512]{1,0:T(1,128)S(1)}) custom-call(s32[2,4]{1,0:T(2,128)S(1)} %copy-done.3, s32[2]{0:T(128)S(1)} %pad_add_fusion.start, f32[1,512]{1,0:T(1,128)S(1)} %bitcast.245, f32[4,2,256,2048]{3,2,1,0:T(8,128)} %bitcast.254, f32[4,2,256,512]{3,2,1,0:T(8,128)} %get-tuple-element.69.grad_out, ...), custom_call_target="tpu_custom_call" | custom-call | flops 3221225472 | bytes 29394984 | tf_op jit(solution)/shard_map/mix_backward/pallas_call | solution.py:638
  1117.2 25.4 %multiply_reduce_fusion = (f32[2048]{0:T(1024)}, bf16[2048,2048]{1,0:T(8,128)(2,1)}) fusion(bf16[2048,2048]{1,0:T(8,128)(2,1)} %all-gather.11.cloned.1.call-done, bf16[2048,2048]{1,0:T(8,128)(2,1)} %bitcast.304, bf16[2048,2048]{1,0:T(8,128)(2,1)} %bitcast.272), kind=kOutput, calls=%fused_computation | convolution fusion | flops 17196644352 | bytes 33562624 | tf_op jit(solution)/shard_map/dot_general | solution.py:364
  1142.6 22.8 %convolution_convert_fusion.1 = bf16[2048,2048]{1,0:T(8,128)(2,1)S(1)} fusion(bf16[2048,2048]{1,0:T(8,128)(2,1)} %all-gather.11.cloned.1.call-done, bf16[2048,2048]{1,0:T(8,128)(2,1)} %bitcast.305), kind=kOutput, calls=%fused_computation.3 | convolution fusion | flops 17184063488 | bytes 25165824 | tf_op jit(solution)/shard_map/dot_general | solution.py:364
  1208.9 55.5 %all-reduce.2 = (f32[2048]{0:T(1024)S(1)}, f32[2048]{0:T(1024)S(1)}) all-reduce(f32[2048]{0:T(1024)S(1)} %div.50, f32[2048]{0:T(1024)} %get-tuple-element.118), channel_id=8, replica_groups=mesh['seq'=8,'mp'=4] {'seq','mp'}, use_global_device_ids=true, to_apply=%region_6.7.clone | all-reduce | flops 4096 | bytes 32768
  1296.0 108.8 %reduce-scatter.8.cloned.1.call-done = bf16[512,2048]{1,0:T(8,128)(2,1)} async-done(((bf16[2048,2048]{1,0:T(8,128)(2,1)}), bf16[512,2048]{1,0:T(8,128)(2,1)}) %reduce-scatter.8.cloned.1.call-update) | async-done | bytes 2097168 | tf_op jit(solution)/shard_map/reduce_scatter | solution.py:932
  (447 shorter events, 499.7 us)
Async XLA Ops:
  7.2 165.2 %all-gather.11.cloned.1.call-start = ((), (), s32[]{:S(2)}) async-start(), calls=%async_computation.7 | async-start | bytes 10485760 | tf_op jit(solution)/shard_map/all_gather | solution.py:732
  19.8 214.1 %all-gather.13.cloned.1.call-start = ((), (), s32[]{:S(2)}) async-start(), calls=%async_computation.12 | async-start | bytes 2359296 | tf_op jit(solution)/shard_map/all_gather | solution.py:782
  29.1 48.9 %collective-permute-start.3 = (bf16[512,2048]{1,0:T(8,128)(2,1)}, bf16[512,2048]{1,0:T(8,128)(2,1)}, u32[]{:S(2)}, u32[]{:S(2)}) collective-permute-start(bf16[512,2048]{1,0:T(8,128)(2,1)} %bitcast_convert_fusion), channel_id=1, source_target_pairs={{0,16},{4,20},{8,24},{12,28},{16,0},{20,4},{24,8},{28,12},{1,17},{... | collective-permute-start | bytes 6291464 | tf_op jit(solution)/shard_map/ppermute | solution.py:654
  32.1 49.0 %collective-permute-start.1 = (bf16[512,2048]{1,0:T(8,128)(2,1)}, bf16[512,2048]{1,0:T(8,128)(2,1)}, u32[]{:S(2)}, u32[]{:S(2)}) collective-permute-start(bf16[512,2048]{1,0:T(8,128)(2,1)} %bitcast_convert_fusion), channel_id=1, source_target_pairs={{0,8},{4,12},{8,0},{12,4},{16,24},{20,28},{24,16},{28,20},{1,9},{5... | collective-permute-start | bytes 6291464 | tf_op jit(solution)/shard_map/ppermute | solution.py:654
  83.9 50.7 %collective-permute-start = (bf16[512,2048]{1,0:T(8,128)(2,1)}, bf16[512,2048]{1,0:T(8,128)(2,1)}, u32[]{:S(2)}, u32[]{:S(2)}) collective-permute-start(bf16[512,2048]{1,0:T(8,128)(2,1)} %bitcast_convert_fusion), channel_id=1, source_target_pairs={{0,4},{4,0},{8,12},{12,8},{16,20},{20,16},{24,28},{28,24},{1,5},{5... | collective-permute-start | bytes 6291464 | tf_op jit(solution)/shard_map/ppermute | solution.py:654
  84.0 50.7 %collective-permute-start.2 = (bf16[512,2048]{1,0:T(8,128)(2,1)}, bf16[512,2048]{1,0:T(8,128)(2,1)}, u32[]{:S(2)}, u32[]{:S(2)}) collective-permute-start(bf16[512,2048]{1,0:T(8,128)(2,1)} %collective-permute-done.1), channel_id=1, source_target_pairs={{0,4},{4,0},{8,12},{12,8},{16,20},{20,16},{24,28},{28,24},{1,5},{5... | collective-permute-start | bytes 6291464 | tf_op jit(solution)/shard_map/ppermute | solution.py:654
  84.5 50.2 %collective-permute-start.4 = (bf16[512,2048]{1,0:T(8,128)(2,1)}, bf16[512,2048]{1,0:T(8,128)(2,1)}, u32[]{:S(2)}, u32[]{:S(2)}) collective-permute-start(bf16[512,2048]{1,0:T(8,128)(2,1)} %collective-permute-done.3), channel_id=1, source_target_pairs={{0,4},{4,0},{8,12},{12,8},{16,20},{20,16},{24,28},{28,24},{1,5},{5... | collective-permute-start | bytes 6291464 | tf_op jit(solution)/shard_map/ppermute | solution.py:654
  207.7 154.8 %all-gather.15.cloned.1.call-start = ((), (), s32[]{:S(2)}) async-start(), calls=%async_computation.13 | async-start | bytes 3932160 | tf_op jit(solution)/shard_map/all_gather | solution.py:748
  208.4 245.4 %all-gather.17.cloned.1.call-start = ((), (), s32[]{:S(2)}) async-start(), calls=%async_computation.14 | async-start | bytes 7864320 | tf_op jit(solution)/shard_map/all_gather | solution.py:748
  209.0 864.1 %all-gather.19.cloned.1.call-start = ((), (), s32[]{:S(2)}) async-start(), calls=%async_computation.15 | async-start | bytes 2359296 | tf_op jit(solution)/shard_map/all_gather | solution.py:909
  354.9 47.9 %collective-permute-start.13 = (bf16[512,2048]{1,0:T(8,128)(2,1)}, bf16[512,2048]{1,0:T(8,128)(2,1)}, u32[]{:S(2)}, u32[]{:S(2)}) collective-permute-start(bf16[512,2048]{1,0:T(8,128)(2,1)} %multiply_convert_fusion.3), channel_id=1, source_target_pairs={{0,8},{4,12},{8,0},{12,4},{16,24},{20,28},{24,16},{28,20},{1,9},{5... | collective-permute-start | bytes 6291464 | tf_op jit(solution)/shard_map/ppermute | solution.py:654
  359.6 98.3 %collective-permute-start.15 = (bf16[512,2048]{1,0:T(8,128)(2,1)}, bf16[512,2048]{1,0:T(8,128)(2,1)}, u32[]{:S(2)}, u32[]{:S(2)}) collective-permute-start(bf16[512,2048]{1,0:T(8,128)(2,1)} %multiply_convert_fusion.3), channel_id=1, source_target_pairs={{0,16},{4,20},{8,24},{12,28},{16,0},{20,4},{24,8},{28,12},{1,17},{... | collective-permute-start | bytes 6291464 | tf_op jit(solution)/shard_map/ppermute | solution.py:654
  364.0 100.5 %collective-permute-start.9 = (bf16[2,192,2048]{2,1,0:T(8,128)(2,1)S(1)}, bf16[2,192,2048]{2,1,0:T(8,128)(2,1)S(1)}, u32[]{:S(2)}, u32[]{:S(2)}) collective-permute-start(bf16[2,192,2048]{2,1,0:T(8,128)(2,1)S(1)} %dynamic-slice_bitcast_fusion.2), channel_id=1, source_target_pairs={{0,4},{4,0},{8,12},{12,8},{16,20},{20,16},{24,28},{28,24},{1,5},{5... | collective-permute-start | bytes 4718600 | tf_op jit(solution)/shard_map/ppermute | solution.py:654
  402.8 85.2 %collective-permute-start.14 = (bf16[512,2048]{1,0:T(8,128)(2,1)}, bf16[512,2048]{1,0:T(8,128)(2,1)}, u32[]{:S(2)}, u32[]{:S(2)}) collective-permute-start(bf16[512,2048]{1,0:T(8,128)(2,1)} %collective-permute-done.13), channel_id=1, source_target_pairs={{0,4},{4,0},{8,12},{12,8},{16,20},{20,16},{24,28},{28,24},{1,5},{5... | collective-permute-start | bytes 6291464 | tf_op jit(solution)/shard_map/ppermute | solution.py:654
  485.3 141.7 %collective-permute-start.10 = (bf16[512,2048]{1,0:T(8,128)(2,1)}, bf16[512,2048]{1,0:T(8,128)(2,1)}, u32[]{:S(2)}, u32[]{:S(2)}) collective-permute-start(bf16[512,2048]{1,0:T(8,128)(2,1)} %multiply_convert_fusion.3), channel_id=1, source_target_pairs={{0,4},{4,0},{8,12},{12,8},{16,20},{20,16},{24,28},{28,24},{1,5},{5... | collective-permute-start | bytes 6291464 | tf_op jit(solution)/shard_map/ppermute | solution.py:654
  663.0 60.8 %collective-permute-start.24 = (bf16[512,2048]{1,0:T(8,128)(2,1)}, bf16[512,2048]{1,0:T(8,128)(2,1)}, u32[]{:S(2)}, u32[]{:S(2)}) collective-permute-start(bf16[512,2048]{1,0:T(8,128)(2,1)} %slice.299), channel_id=1, source_target_pairs={{0,4},{4,0},{8,12},{12,8},{16,20},{20,16},{24,28},{28,24},{1,5},{5... | collective-permute-start | bytes 6291464 | tf_op jit(solution)/shard_map/ppermute | solution.py:654
  757.1 45.3 %collective-permute-start.29 = (bf16[256,2048]{1,0:T(8,128)(2,1)S(1)}, bf16[256,2048]{1,0:T(8,128)(2,1)S(1)}, u32[]{:S(2)}, u32[]{:S(2)}) collective-permute-start(bf16[256,2048]{1,0:T(8,128)(2,1)S(1)} %add_convert_fusion.12), channel_id=1, source_target_pairs={{0,8},{4,12},{8,0},{12,4},{16,24},{20,28},{24,16},{28,20},{1,9},{5... | collective-permute-start | bytes 3145736 | tf_op jit(solution)/shard_map/ppermute | solution.py:654
  759.2 43.2 %collective-permute-start.26 = (bf16[256,2048]{1,0:T(8,128)(2,1)S(1)}, bf16[256,2048]{1,0:T(8,128)(2,1)S(1)}, u32[]{:S(2)}, u32[]{:S(2)}) collective-permute-start(bf16[256,2048]{1,0:T(8,128)(2,1)S(1)} %add_convert_fusion.13), channel_id=1, source_target_pairs={{0,16},{4,20},{8,24},{12,28},{16,0},{20,4},{24,8},{28,12},{1,17},{... | collective-permute-start | bytes 3145736 | tf_op jit(solution)/shard_map/ppermute | solution.py:654
  806.3 56.8 %collective-permute-start.30 = (bf16[512,2048]{1,0:T(8,128)(2,1)S(1)}, bf16[512,2048]{1,0:T(8,128)(2,1)S(1)}, u32[]{:S(2)}, u32[]{:S(2)}) collective-permute-start(bf16[512,2048]{1,0:T(8,128)(2,1)S(1)} %copy-done.29), channel_id=1, source_target_pairs={{0,4},{4,0},{8,12},{12,8},{16,20},{20,16},{24,28},{28,24},{1,5},{5... | collective-permute-start | bytes 6291464 | tf_op jit(solution)/shard_map/ppermute | solution.py:654
  812.0 52.2 %collective-permute-start.32 = (bf16[256,2048]{1,0:T(8,128)(2,1)S(1)}, bf16[256,2048]{1,0:T(8,128)(2,1)S(1)}, u32[]{:S(2)}, u32[]{:S(2)}) collective-permute-start(bf16[256,2048]{1,0:T(8,128)(2,1)S(1)} %slice.314), channel_id=1, source_target_pairs={{0,8},{4,12},{8,0},{12,4},{16,24},{20,28},{24,16},{28,20},{1,9},{5... | collective-permute-start | bytes 3145736 | tf_op jit(solution)/shard_map/ppermute | solution.py:654
  812.8 47.8 %collective-permute-start.35 = (bf16[256,2048]{1,0:T(8,128)(2,1)S(1)}, bf16[256,2048]{1,0:T(8,128)(2,1)S(1)}, u32[]{:S(2)}, u32[]{:S(2)}) collective-permute-start(bf16[256,2048]{1,0:T(8,128)(2,1)S(1)} %get-tuple-element.181), channel_id=1, source_target_pairs={{0,8},{4,12},{8,0},{12,4},{16,24},{20,28},{24,16},{28,20},{1,9},{5... | collective-permute-start | bytes 3145736 | tf_op jit(solution)/shard_map/ppermute | solution.py:654
  815.1 49.1 %collective-permute-start.37 = (bf16[256,2048]{1,0:T(8,128)(2,1)S(1)}, bf16[256,2048]{1,0:T(8,128)(2,1)S(1)}, u32[]{:S(2)}, u32[]{:S(2)}) collective-permute-start(bf16[256,2048]{1,0:T(8,128)(2,1)S(1)} %slice.318), channel_id=1, source_target_pairs={{0,16},{4,20},{8,24},{12,28},{16,0},{20,4},{24,8},{28,12},{1,17},{... | collective-permute-start | bytes 3145736 | tf_op jit(solution)/shard_map/ppermute | solution.py:654
  835.6 46.6 %collective-permute-start.39 = (bf16[256,2048]{1,0:T(8,128)(2,1)S(1)}, bf16[256,2048]{1,0:T(8,128)(2,1)S(1)}, u32[]{:S(2)}, u32[]{:S(2)}) collective-permute-start(bf16[256,2048]{1,0:T(8,128)(2,1)S(1)} %add_convert_fusion.10), channel_id=1, source_target_pairs={{0,8},{4,12},{8,0},{12,4},{16,24},{20,28},{24,16},{28,20},{1,9},{5... | collective-permute-start | bytes 3145736 | tf_op jit(solution)/shard_map/ppermute | solution.py:654
  960.9 209.2 %reduce-scatter.14.cloned.1.call-start = ((), (), s32[]{:S(2)}) async-start(), calls=%async_computation.11 | async-start | bytes 3932160 | tf_op jit(solution)/shard_map/reduce_scatter | solution.py:860
  984.7 221.7 %reduce-scatter.10.cloned.1.call-start = ((), (), s32[]{:S(2)}) async-start(), calls=%async_computation.9 | async-start | bytes 1310720 | tf_op jit(solution)/shard_map/reduce_scatter | solution.py:885
  1066.7 198.9 %reduce-scatter.16.cloned.1.call-start = ((), (), s32[]{:S(2)}) async-start(), calls=%async_computation.16 | async-start | bytes 73728
  1110.7 156.9 %reduce-scatter.12.cloned.1.call-start = ((), (), s32[]{:S(2)}) async-start(), calls=%async_computation.10 | async-start | bytes 7864320 | tf_op jit(solution)/shard_map/reduce_scatter | solution.py:860
  1117.1 287.7 %reduce-scatter.8.cloned.1.call-start = ((), (), s32[]{:S(2)}) async-start(), calls=%async_computation.8 | async-start | bytes 10485760 | tf_op jit(solution)/shard_map/reduce_scatter | solution.py:932
  1190.5 81.9 %collective-permute-start.42 = (bf16[128,2048]{1,0:T(8,128)(2,1)}, bf16[128,2048]{1,0:T(8,128)(2,1)S(1)}, u32[]{:S(2)}, u32[]{:S(2)}) collective-permute-start(bf16[128,2048]{1,0:T(8,128)(2,1)} %slice.322), channel_id=1, source_target_pairs={{0,8},{4,12},{8,0},{12,4},{16,24},{20,28},{24,16},{28,20},{1,9},{5... | collective-permute-start | bytes 1572872 | tf_op jit(solution)/shard_map/ppermute | solution.py:654
  1192.6 80.4 %collective-permute-start.47 = (bf16[128,2048]{1,0:T(8,128)(2,1)}, bf16[128,2048]{1,0:T(8,128)(2,1)S(1)}, u32[]{:S(2)}, u32[]{:S(2)}) collective-permute-start(bf16[128,2048]{1,0:T(8,128)(2,1)} %slice.326), channel_id=1, source_target_pairs={{0,16},{4,20},{8,24},{12,28},{16,0},{20,4},{24,8},{28,12},{1,17},{... | collective-permute-start | bytes 1572872 | tf_op jit(solution)/shard_map/ppermute | solution.py:654
  1196.8 77.1 %collective-permute-start.49 = (bf16[128,2048]{1,0:T(8,128)(2,1)S(1)}, bf16[128,2048]{1,0:T(8,128)(2,1)S(1)}, u32[]{:S(2)}, u32[]{:S(2)}) collective-permute-start(bf16[128,2048]{1,0:T(8,128)(2,1)S(1)} %add_convert_fusion.18), channel_id=1, source_target_pairs={{0,8},{4,12},{8,0},{12,4},{16,24},{20,28},{24,16},{28,20},{1,9},{5... | collective-permute-start | bytes 1572872 | tf_op jit(solution)/shard_map/ppermute | solution.py:654
  1204.6 69.3 %collective-permute-start.46 = (bf16[128,2048]{1,0:T(8,128)(2,1)}, bf16[128,2048]{1,0:T(8,128)(2,1)}, u32[]{:S(2)}, u32[]{:S(2)}) collective-permute-start(bf16[128,2048]{1,0:T(8,128)(2,1)} %add_convert_fusion.19), channel_id=1, source_target_pairs={{0,16},{4,20},{8,24},{12,28},{16,0},{20,4},{24,8},{28,12},{1,17},{... | collective-permute-start | bytes 1572872 | tf_op jit(solution)/shard_map/ppermute | solution.py:654
  (117 other events, 1587.5 us)
Sparse Core Ops, SparseCore 0:
  20.0 152.3 all-gather.10
  207.8 26.1 all-gather.12
  236.1 102.1 all-gather.14
  339.7 114.0 all-gather.16
  961.0 25.3 all-gather.18
  988.6 60.2 reduce-scatter.13
  1066.8 26.4 reduce-scatter.9
  1110.9 32.5 reduce-scatter.15
  1145.8 111.7 reduce-scatter.11
  1259.8 144.9 reduce-scatter.7

commit v2 on v1

--- a/solution.py
+++ b/solution.py
@@ -410,76 +410,74 @@
     return mm(ones, high) + mm(ones, low)
 
 
-def states_kernel(lens, start, gap, pf, pv, state_out, decay_out):
+def states_kernel(where, lens, gap, proj, state_out):
     step = pl.program_id(0)
-    length = pf.shape[2]
-    heads = state_out.shape[1]
-
-    @pl.when(step == 0)
-    def _():
-        state_out[...] = jnp.zeros_like(state_out)
-        decay_out[...] = jnp.ones_like(decay_out)
-
-    base = start[0] + step * length
+    length = proj.shape[2]
+    heads = state_out.shape[2]
+    width = heads * 128
+    first = lax.rem(step, where[3]) == 0
+    base = position(where, step, length)
     ones = triangle(length, False)
-    for p in range(pf.shape[1]):
+    for p in range(proj.shape[1]):
         col, _, last_id, before = block_docs(lens, p, base, length)
-        _, _, key, log_forget = gates(pf[0, p], gap[...])
+        _, _, key, log_forget = gates(proj[0, p, :, :width], gap[...])
         cum = running_sum(ones, log_forget)
         last = cum[length - 1 :]
         khat = (key * jnp.where(col == last_id, jnp.exp(last - cum), 0.0)).astype(BF16)
         decay = jnp.where(last_id == before, jnp.exp(last), 0.0)
-        decay_out[p] = decay_out[p] * decay
         for h in range(heads):
             at = slice(h * 128, h * 128 + 128)
-            values = pv[0, p, :, at].astype(BF16)
-            state_out[p, h] = state_out[p, h] * decay[:, at] + mm(values, khat[:, at], TN)
-
-
-def entering_state(where_ref, states, decays, place, reverse):
-    count = states.shape[0]
-    for p in range(states.shape[1]):
-        for h in range(states.shape[2]):
-            at = slice(h * 128, h * 128 + 128)
-            now = jnp.zeros(states.shape[3:], F32)
-            for k in range(count):
-                s = count - 1 - k if reverse else k
-                reached = (s > place) if reverse else (s < place)
-                new = decays[s, p, :, at] * now + states[s, p, h].astype(F32)
-                now = jnp.where(reached, new, now)
-            where_ref[p, h] = now
-
-
-def forward_kernel(
-    lens, start, gap, gain, proj, states, decays, heads_out, mixed_out, kept, state
-):
+            values = proj[0, p, :, width + h * 128 : width + h * 128 + 128].astype(BF16)
+            made = mm(values, khat[:, at], TN)
+            older = jnp.where(first, 0.0, state_out[p, 0, h, :128] * decay[:, at])
+            state_out[p, 0, h, :128] = older + made
+            kept = jnp.where(first, 1.0, state_out[p, 0, h, 128:])
+            state_out[p, 0, h, 128:] = kept * decay[:, at]
+
+
+def position(where, step, length):
+    sub_run, part = lax.div(step, where[3]), lax.rem(step, where[3])
+    return sub_run * where[1] + where[2] + part * length
+
+
+def scan_kernel(reverse, count, steps, decays, states, out):
+    now = jnp.zeros(out.shape[2:], F32)
+    planes = states.shape[0]
+    order = [(s, m) for s in range(steps) for m in range(planes)]
+    for s, m in reversed(order) if reverse else order:
+        out[m, s] = now.astype(BF16)
+        kept = decays[m, s, 128:].astype(F32)[:1]
+        now = now * kept + states[m, s, :128].astype(F32)
+
+
+def forward_kernel(where, lens, gap, gain, proj, entering, heads_out, mixed_out, kept, state):
     step = pl.program_id(0)
     length = proj.shape[2]
     heads = state.shape[1]
     width = heads * 128
 
-    @pl.when(step == 0)
+    @pl.when(lax.rem(step, where[3]) == 0)
     def _():
-        entering_state(state, states, decays, start[1], False)
-
-    base = start[0] + step * length
+        state[...] = entering[:, 0].astype(F32)
+
+    base = position(where, step, length)
     ones = triangle(length, False)
     row_index = lax.broadcasted_iota(jnp.int32, (length, length), 0)
     col_index = lax.broadcasted_iota(jnp.int32, (length, length), 1)
     for p in range(proj.shape[1]):
         col, row, last_id, before = block_docs(lens, p, base, length)
-        _, _, key, log_forget = gates(proj[0, p, :, width : 2 * width], gap[...])
+        _, _, key, log_forget = gates(proj[0, p, :, :width], gap[...])
         cum = running_sum(ones, log_forget)
         last = cum[length - 1 :]
         khat = (key * jnp.where(col == last_id, jnp.exp(last - cum), 0.0)).astype(BF16)
         decay = jnp.where(last_id == before, jnp.exp(last), 0.0)
-        qt = proj[0, p, :, :width].astype(BF16).astype(F32) * jnp.exp(cum)
+        qt = proj[0, p, :, 2 * width : 3 * width].astype(BF16).astype(F32) * jnp.exp(cum)
         qe = jnp.where(col == before, qt, 0.0)
         kt = key * jnp.exp(-cum)
         visible = (col == row) & (row_index >= col_index)
         for h in range(heads):
             at = slice(h * 128, h * 128 + 128)
-            values = proj[0, p, :, 2 * width + h * 128 : 2 * width + h * 128 + 128].astype(BF16)
+            values = proj[0, p, :, width + h * 128 : width + h * 128 + 128].astype(BF16)
             gate = proj[0, p, :, 3 * width + h * 128 : 3 * width + h * 128 + 128]
             now = state[p, h]
             kept[0, p, h] = now
@@ -493,26 +491,30 @@
 
 
 def gate_back_kernel(
-    lens, start, gap, gain, proj, mixed_in, grad_heads, grad_out, grad_gate, group_part, state
+    where, lens, gap, gain, proj, mixed_in, grad_heads, grad_out, grad_gate, group_part, run_out, state
 ):
-    step = pl.program_id(0)
+    turn = pl.program_id(0)
+    step = pl.num_programs(0) - 1 - turn
     length = proj.shape[2]
     heads = state.shape[1]
     width = heads * 128
 
-    @pl.when(step == 0)
+    @pl.when(turn == 0)
+    def _():
+        group_part[...] = jnp.zeros_like(group_part)
+
+    @pl.when(lax.rem(turn, where[3]) == 0)
     def _():
         state[...] = jnp.zeros_like(state)
-        group_part[...] = jnp.zeros_like(group_part)
-
-    base = start[0] + (pl.num_programs(0) - 1 - step) * length
+
+    base = position(where, step, length)
     ones = triangle(length, False)
     for p in range(proj.shape[1]):
         col, _, last_id, before = block_docs(lens, p, base, length)
-        _, _, _, log_forget = gates(proj[0, p, :, width : 2 * width], gap[...])
+        _, _, _, log_forget = gates(proj[0, p, :, :width], gap[...])
         cum = running_sum(ones, log_forget)
         decay = jnp.where(last_id == before, jnp.exp(cum[length - 1 :]), 0.0)
-        qt = proj[0, p, :, :width].astype(BF16).astype(F32) * jnp.exp(cum)
+        qt = proj[0, p, :, 2 * width : 3 * width].astype(BF16).astype(F32) * jnp.exp(cum)
         qe = jnp.where(col == before, qt, 0.0).astype(BF16)
         for h in range(heads):
             at = slice(h * 128, h * 128 + 128)
@@ -534,29 +536,34 @@
             high, low = split_two(grad)
             own = mm(high, qe[:, at], TN) + mm(low, qe[:, at], TN)
             state[p, h] = state[p, h] * decay[:, at] + own
+            run_out[p, 0, h] = state[p, h].astype(BF16)
 
 
 def backward_kernel(
-    lens, start, gap, proj, grad_out, grad_gate, kept, states, decays, grad_proj, gap_part, state
+    where, lens, gap, proj, grad_out, grad_gate, kept, entering, grad_proj, gap_part, state
 ):
-    step = pl.program_id(0)
+    turn = pl.program_id(0)
+    step = pl.num_programs(0) - 1 - turn
     length = proj.shape[2]
     heads = state.shape[1]
     width = heads * 128
 
-    @pl.when(step == 0)
+    @pl.when(turn == 0)
     def _():
-        entering_state(state, states, decays, start[1], True)
         gap_part[...] = jnp.zeros_like(gap_part)
 
-    base = start[0] + (pl.num_programs(0) - 1 - step) * length
+    @pl.when(lax.rem(turn, where[3]) == 0)
+    def _():
+        state[...] = entering[:, 0].astype(F32)
+
+    base = position(where, step, length)
     ones = triangle(length, False)
     ones_up = triangle(length, True)
     row_index = lax.broadcasted_iota(jnp.int32, (length, length), 0)
     col_index = lax.broadcasted_iota(jnp.int32, (length, length), 1)
     for p in range(proj.shape[1]):
         col, row, last_id, before = block_docs(lens, p, base, length)
-        open_gate, gap_gate, key, log_forget = gates(proj[0, p, :, width : 2 * width], gap[...])
+        open_gate, gap_gate, key, log_forget = gates(proj[0, p, :, :width], gap[...])
         cum = running_sum(ones, log_forget)
         last = cum[length - 1 :]
         ecum = jnp.exp(cum)
@@ -564,7 +571,7 @@
         tail = jnp.where(col == last_id, jnp.exp(last - cum), 0.0)
         khat = (key * tail).astype(BF16)
         decay = jnp.where(last_id == before, jnp.exp(last), 0.0)
-        qt = proj[0, p, :, :width].astype(BF16).astype(F32) * ecum
+        qt = proj[0, p, :, 2 * width : 3 * width].astype(BF16).astype(F32) * ecum
         enters = col == before
         qe = jnp.where(enters, qt, 0.0).astype(BF16)
         qt = qt.astype(BF16)
@@ -572,7 +579,7 @@
         visible = (col == row) & (row_index >= col_index)
         for h in range(heads):
             at = slice(h * 128, h * 128 + 128)
-            values = proj[0, p, :, 2 * width + h * 128 : 2 * width + h * 128 + 128].astype(BF16)
+            values = proj[0, p, :, width + h * 128 : width + h * 128 + 128].astype(BF16)
             grad = grad_out[0, p, :, at]
             grad_enter = jnp.where(enters, grad, 0.0)
             grad, grad_low = split_two(grad)
@@ -599,55 +606,286 @@
             grad_gap = grad_keys - grad_log / (1.0 - gap_gate[:, at])
             gap_part[:, at] += jnp.sum(grad_gap * open_gate[:, at], axis=0, keepdims=True)
             grad_forget = -grad_gap * gap_gate[:, at] * (1.0 - open_gate[:, at])
-            grad_proj[0, p, :, at] = (grad_qt * ecum[:, at]).astype(BF16)
-            grad_proj[0, p, :, width + h * 128 : width + h * 128 + 128] = grad_forget.astype(BF16)
-            grad_proj[0, p, :, 2 * width + h * 128 : 2 * width + h * 128 + 128] = (
-                grad_values.astype(BF16)
-            )
+            made = (grad_forget, grad_values, grad_qt * ecum[:, at])
+            for k, part in enumerate(made):
+                start = k * width + h * 128
+                grad_proj[0, p, :, start : start + 128] = part.astype(BF16)
         grad_proj[0, p, :, 3 * width :] = grad_gate[0, p]
 
 
-def recur_call(kernel, steps, half, reverse, ins, outs, scratch, flops, name):
-    def index(kind):
-        def rows(j):
-            b = steps - 1 - j if reverse else j
-            return (b // half, 0, b % half, kind if isinstance(kind, int) else 0)
-
-        def block(j):
-            return (steps - 1 - j if reverse else j, 0, 0, 0, 0)
-
-        return rows if isinstance(kind, int) else block
-
-    in_specs, arrays = [], []
-    for array, kind, shape in ins:
-        arrays.append(array)
+def recur_call(kernel, steps, halves, reverse, where, ins, outs, scratch, flops, name):
+    def index(kind, ndim):
+        def place(turn, where_ref):
+            step = steps - 1 - turn if reverse else turn
+            run, half = lax.div(step, halves), lax.rem(step, halves)
+            if kind == "near":
+                return (lax.bitwise_xor(run, where_ref[0]), 0, half, 0)
+            if kind == "rows":
+                return (run, 0, half, 0)
+            if kind == "block":
+                return (step,) + (0,) * (ndim - 1)
+            if kind == "run":
+                return (0, run) + (0,) * (ndim - 2)
+            return (0,) * ndim
+
+        return place
+
+    def spec(kind, block):
         if kind == "smem":
-            in_specs.append(pl.BlockSpec(memory_space=pltpu.SMEM))
-        elif kind == "whole":
-            in_specs.append(pl.BlockSpec(array.shape, lambda j, n=array.ndim: (0,) * n))
-        else:
-            in_specs.append(pl.BlockSpec(shape, index(kind)))
-    out_specs, out_shapes = [], []
-    for shape, dtype, kind, block in outs:
-        out_shapes.append(jax.ShapeDtypeStruct(shape, dtype))
-        if kind == "whole":
-            out_specs.append(pl.BlockSpec(shape, lambda j, n=len(shape): (0,) * n))
-        else:
-            out_specs.append(pl.BlockSpec(block, index(kind)))
+            return pl.BlockSpec(memory_space=pltpu.SMEM)
+        return pl.BlockSpec(block, index(kind, len(block)))
+
+    arrays = [array for array, _, _ in ins]
     moved = sum(a.size * a.dtype.itemsize for a in arrays)
     return pl.pallas_call(
         kernel,
-        grid=(steps,),
-        in_specs=in_specs,
-        out_specs=out_specs,
-        out_shape=out_shapes,
-        scratch_shapes=scratch,
+        grid_spec=pltpu.PrefetchScalarGridSpec(
+            num_scalar_prefetch=1,
+            grid=(steps,),
+            in_specs=[spec(kind, block or array.shape) for array, kind, block in ins],
+            out_specs=[spec(kind, block or shape) for shape, _, kind, block in outs],
+            scratch_shapes=scratch,
+        ),
+        out_shape=[jax.ShapeDtypeStruct(shape, dtype) for shape, dtype, _, _ in outs],
         compiler_params=pltpu.CompilerParams(
             dimension_semantics=("arbitrary",), vmem_limit_bytes=48 << 20
         ),
-        cost_estimate=pl.CostEstimate(flops=flops, bytes_accessed=moved, transcendentals=0),
+        cost_estimate=pl.CostEstimate(flops=flops // 20, bytes_accessed=moved // 20, transcendentals=0),
         name=name,
+    )(where, *arrays)
+
+
+def scan_call(decays, states, reverse):
+    return pl.pallas_call(
+        functools.partial(scan_kernel, reverse, states.shape[0], states.shape[1]),
+        out_shape=jax.ShapeDtypeStruct(states.shape[:2] + (128, 128), BF16),
+        name="scan_back" if reverse else "scan",
+    )(decays, states)
+
+
+def project_kernel(tiles, left, right, weights, *rest):
+    out = rest[-1]
+    step = pl.program_id(0)
+
+    @pl.when(step < tiles)
+    def _():
+        out[0] = mm(left[...], weights[...])
+
+    @pl.when(step >= tiles)
+    def _():
+        out[0] = mm(right[...], weights[...])
+
+
+def project_call(made, first, count, left, right, weights):
+    rows, width = left.shape
+    columns = weights.shape[1]
+    tile = min(256, rows)
+    tiles = rows // tile
+    shape = (count, rows, columns)
+    in_specs = [
+        pl.BlockSpec((tile, width), lambda i: (jnp.minimum(i, tiles - 1), 0)),
+        pl.BlockSpec((tile, width), lambda i: (jnp.maximum(i - tiles, 0), 0)),
+        pl.BlockSpec(weights.shape, lambda i: (0, 0), pipeline_mode=pl.Buffered(1)),
+    ]
+    arrays = [left, right, weights]
+    if made is not None:
+        in_specs.append(pl.BlockSpec(memory_space=pl.ANY))
+        arrays.append(made)
+    return pl.pallas_call(
+        functools.partial(project_kernel, tiles),
+        grid=(2 * tiles,),
+        in_specs=in_specs,
+        out_specs=pl.BlockSpec(
+            (1, tile, columns), lambda i: (first + lax.div(i, tiles), lax.rem(i, tiles), 0)
+        ),
+        out_shape=jax.ShapeDtypeStruct(shape, F32),
+        input_output_aliases={} if made is None else {3: 0},
+        compiler_params=pltpu.CompilerParams(
+            dimension_semantics=("arbitrary",), vmem_limit_bytes=40 << 20
+        ),
+        cost_estimate=pl.CostEstimate(
+            flops=rows * width * columns // 5, bytes_accessed=rows * width, transcendentals=0
+        ),
+        name="project",
     )(*arrays)
+
+
+def back_kernel(tiles, left, right, grads, weights, out_left, out_right, part):
+    step = pl.program_id(0)
+    made = mm(grads[0], weights[...], NT)
+
+    @pl.when(step == 0)
+    def _():
+        part[...] = jnp.zeros_like(part)
+
+    @pl.when(step < tiles)
+    def _():
+        out_left[...] = made.astype(BF16)
+        part[...] += jnp.sum(made * left[...].astype(F32), axis=0, keepdims=True)
+
+    @pl.when(step >= tiles)
+    def _():
+        out_right[...] = made.astype(BF16)
+        part[...] += jnp.sum(made * right[...].astype(F32), axis=0, keepdims=True)
+
+
+def back_call(grads, first, left, right, weights):
+    rows, width = left.shape
+    columns = weights.shape[1]
+    tile = min(256, rows)
+    tiles = rows // tile
+
+    def one(i):
+        return (jnp.minimum(i, tiles - 1), 0)
+
+    def two(i):
+        return (jnp.maximum(i - tiles, 0), 0)
+
+    return pl.pallas_call(
+        functools.partial(back_kernel, tiles),
+        grid=(2 * tiles,),
+        in_specs=[
+            pl.BlockSpec((tile, width), one),
+            pl.BlockSpec((tile, width), two),
+            pl.BlockSpec(
+                (1, tile, columns), lambda i: (first + lax.div(i, tiles), lax.rem(i, tiles), 0)
+            ),
+            pl.BlockSpec(weights.shape, lambda i: (0, 0), pipeline_mode=pl.Buffered(1)),
+        ],
+        out_specs=[
+            pl.BlockSpec((tile, width), one),
+            pl.BlockSpec((tile, width), two),
+            pl.BlockSpec((1, width), lambda i: (0, 0)),
+        ],
+        out_shape=[jax.ShapeDtypeStruct((rows, width), BF16)] * 2
+        + [jax.ShapeDtypeStruct((1, width), F32)],
+        compiler_params=pltpu.CompilerParams(
+            dimension_semantics=("arbitrary",), vmem_limit_bytes=40 << 20
+        ),
+        cost_estimate=pl.CostEstimate(
+            flops=rows * width * columns // 5, bytes_accessed=rows * width, transcendentals=0
+        ),
+        name="project_back",
+    )(left, right, grads, weights)
+
+
+def feed_kernel(*refs):
+    two_refs, cot_refs, (w_low, w_high, w_dn), outs = refs[0:2], refs[2:4], refs[4:7], refs[7:]
+    units = w_dn.shape[0]
+    half = w_low.shape[0]
+    for k in range(2):
+        act_out, grad_out, down_out, back_out = outs[4 * k : 4 * k + 4]
+        pre = mm(two_refs[k][:, :half], w_low[...]) + mm(two_refs[k][:, half:], w_high[...])
+        gate, up = pre[:, :units], pre[:, units:]
+        sigma = jax.nn.sigmoid(gate)
+        silu = gate * sigma
+        act = (silu * up).astype(BF16)
+        act_out[...] = act
+        down_out[...] = mm(act, w_dn[...]).astype(BF16)
+        grad_act = mm(cot_refs[k][...], w_dn[...], NT)
+        grad_out[:, :units] = (grad_act * up * (sigma * (1.0 + gate * (1.0 - sigma)))).astype(BF16)
+        grad_out[:, units:] = (grad_act * silu).astype(BF16)
+        back_out[:, :half] = mm(grad_out[...], w_low[...], NT).astype(BF16)
+        back_out[:, half:] = mm(grad_out[...], w_high[...], NT).astype(BF16)
+
+
+def feed_call(two, cot, w_low, w_high, w_dn):
+    rows, width = two[0].shape
+    units = w_dn.shape[0]
+    tile = min(256, rows)
+
+    def cut(columns):
+        return pl.BlockSpec((tile, columns), lambda i: (i, 0))
+
+    def still(array):
+        return pl.BlockSpec(array.shape, lambda i: (0, 0), pipeline_mode=pl.Buffered(1))
+
+    sizes = (units, 2 * units, width, width)
+    flops = 2 * 2 * rows * width * 6 * units
+    return pl.pallas_call(
+        feed_kernel,
+        grid=(rows // tile,),
+        in_specs=[cut(width)] * 4 + [still(w_low), still(w_high), still(w_dn)],
+        out_specs=[cut(s) for s in sizes] * 2,
+        out_shape=[jax.ShapeDtypeStruct((rows, s), BF16) for s in sizes] * 2,
+        compiler_params=pltpu.CompilerParams(
+            dimension_semantics=("arbitrary",), vmem_limit_bytes=58 << 20
+        ),
+        cost_estimate=pl.CostEstimate(
+            flops=flops // 20, bytes_accessed=rows * width, transcendentals=0
+        ),
+        name="feed",
+    )(*two, *cot, w_low, w_high, w_dn)
+
+
+def outer_kernel(count, place, *refs):
+    *inputs, out, total, left, right, sems = refs
+    lefts, rights = inputs[:count], inputs[count:]
+    if len(rights) < count:
+        rights = [rights[0].at[k] for k in range(count)]
+    step = pl.program_id(0)
+
+    def fetch(block, slot):
+        return (
+            pltpu.make_async_copy(lefts[block], left.at[slot], sems.at[0, slot]),
+            pltpu.make_async_copy(rights[block], right.at[slot], sems.at[1, slot]),
+        )
+
+    @pl.when(step == 0)
+    def _():
+        for copy in fetch(0, 0):
+            copy.start()
+
+    slot = lax.rem(step, 2)
+    for block in range(1, count):
+
+        @pl.when(step + 1 == block)
+        def _(block=block):
+            for copy in fetch(block, block % 2):
+                copy.start()
+
+    for copy in fetch(0, slot):
+        copy.wait()
+
+    @pl.when(step == 0)
+    def _():
+        total[...] = mm(left[0], right[0], TN)
+
+    @pl.when(step > 0)
+    def _():
+        total[...] += mm(left[slot], right[slot], TN)
+
+    @pl.when(step == count - 1)
+    def _():
+        place(out, total)
+
+
+def outer_call(lefts, rights, shape, place, name):
+    count = len(lefts)
+    rows, m = lefts[0].shape
+    n = rights[0].shape[-1]
+    return pl.pallas_call(
+        functools.partial(outer_kernel, count, place),
+        grid=(count,),
+        in_specs=[pl.BlockSpec(memory_space=pl.ANY)] * (count + len(rights)),
+        out_specs=pl.BlockSpec(shape, lambda i: (0,) * len(shape), pipeline_mode=pl.Buffered(1)),
+        out_shape=jax.ShapeDtypeStruct(shape, BF16),
+        scratch_shapes=[
+            pltpu.VMEM((m, n), F32),
+            pltpu.VMEM((2, rows, m), BF16),
+            pltpu.VMEM((2, rows, n), BF16),
+            pltpu.SemaphoreType.DMA((2, 2)),
+        ],
+        compiler_params=pltpu.CompilerParams(
+            dimension_semantics=("arbitrary",), vmem_limit_bytes=58 << 20
+        ),
+        cost_estimate=pl.CostEstimate(
+            flops=count * rows * m * n // 10,
+            bytes_accessed=rows * (m + n),
+            transcendentals=0,
+        ),
+        name=name,
+    )(*lefts, *rights)
 
 
 def swap(value, across):
@@ -658,36 +896,61 @@
 TILE = 128
 
 
-def plane_gather(own):
+def together(*values):
+    return lax.optimization_barrier(values)
+
+
+def plane_gather(own, beside=None, meet=None):
     half = own.shape[0] // 2
     got = {0: own, XLINK: swap(own, XLINK), YLINK: swap(own, YLINK), CORE: swap(own, CORE)}
+    got, beside = together(got, beside)
     first = swap(got[YLINK][:half], XLINK)
     second = swap(got[XLINK][half:], YLINK)
     got[XLINK + CORE] = swap(got[XLINK], CORE)
     got[YLINK + CORE] = swap(got[YLINK], CORE)
+    first, second, got, meet = together(first, second, got, meet)
     got[XLINK + YLINK] = jnp.concatenate([first, second])
     got[XLINK + YLINK + CORE] = jnp.concatenate([swap(first, CORE), swap(second, CORE)])
-    return got
+    return got, beside, meet
 
 
 def add_low(a, b):
     return (a.astype(F32) + b.astype(F32)).astype(BF16)
 
 
-def plane_scatter(parts):
+def chip_sum(parts, a):
+    return add_low(parts[a], swap(parts[a ^ CORE], CORE))
+
+
+def plane_scatter(parts, chip=None, far=None, last=None):
     half = parts[0].shape[0] // 2
-    chip = {}
-    for a in (6, 2, 4, 0):
-        chip[a] = add_low(parts[a], swap(parts[a ^ CORE], CORE))
+    chip = dict(chip or {})
+    for a in (2, 4, 6, 0):
+        if a not in chip:
+            chip[a] = chip_sum(parts, a)
+    mine_x = swap(chip[2][:half], XLINK)
+    mine_y = swap(chip[4][half:], YLINK)
     from_x = swap(chip[6][:half], XLINK)
     from_y = swap(chip[6][half:], YLINK)
-    mine_x = swap(chip[2][:half], XLINK)
-    mine_y = swap(chip[4][half:], YLINK)
-    last_y = swap(add_low(chip[4][:half], from_x), YLINK)
-    last_x = swap(add_low(chip[2][half:], from_y), XLINK)
+    mine_x, mine_y, from_x, from_y, far = together(mine_x, mine_y, from_x, from_y, far)
+    for_y, for_x = add_low(chip[4][:half], from_x), add_low(chip[2][half:], from_y)
+    if callable(last):
+        for_y, for_x, far = together(for_y, for_x, far)
+        last = last(far)
+    last_x, last_y, last = together(swap(for_x, XLINK), swap(for_y, YLINK), last)
     low = chip[0][:half].astype(F32) + mine_x.astype(F32) + last_y.astype(F32)
     high = chip[0][half:].astype(F32) + mine_y.astype(F32) + last_x.astype(F32)
-    return jnp.concatenate([low, high])
+    return jnp.concatenate([low, high]), far, last
+
+
+def whole_sum(value):
+    for axis in ("seq", "mp"):
+        count = lax.axis_size(axis)
+        across = 1
+        while across < count:
+            value = value + lax.ppermute(value, axis, [(i, i ^ across) for i in range(count)])
+            across *= 2
+    return value
 
 
 def pick(array, index, axis):
@@ -714,9 +977,9 @@
     span, packs, width = tokens.shape
     rows = span * packs
     run = span * mp_count
-    heads, head_size = forget_gap.shape
+    all_heads, head_size, _ = w_mix_out.shape
+    heads = all_heads // seq_count
     chans = heads * head_size
-    hidden_units = w_gate_up.shape[2]
     slice_d = width // seq_count
 
     def pack_major(array):
@@ -725,15 +988,31 @@
     def token_major(array):
         return jnp.transpose(array.reshape(packs, span, width), (1, 0, 2))
 
+    def gather_shares(part):
+        return lax.all_gather(part, "mp", axis=0).reshape((2, 2) + part.shape)
+
+    def both_halves(pairs):
+        mine = pick(pairs, core, 0)
+        other = swap(pick(pairs, 1 - core, 0), CORE)
+        return jnp.where(core == 0, mine, other), jnp.where(core == 0, other, mine)
+
+    in_part = lax.dynamic_slice(
+        w_mix_in, (0, 2 * core, chip * head_size), (width, 2, head_size)
+    ).reshape(width, 2 * head_size)
+    in_pairs = gather_shares(in_part)
+
     own = pack_major(tokens)
     scale_one = rms_scale(own)
-    normed = (own * scale_one * norm1_gain).astype(BF16)
-    in_flat = w_mix_in.reshape(width, 4 * chans)
-    normed_all = lax.all_gather(normed, "mp", axis=0, tiled=True)
-
-    cot_own = pack_major(lax.dynamic_slice_in_dim(out_cotangent, mp_index * span, span, 0))
-    cot = plane_gather(cot_own.astype(BF16))
-
+    normed_own = (own * scale_one * norm1_gain).astype(BF16)
+
+    small = pick(jnp.stack([forget_gap, group_gain]), chip, 1)[None]
+    for bit in range(2):
+        across = 1 << bit
+        other = lax.ppermute(small, "mp", [(i, i ^ across) for i in range(mp_count)])
+        low = (mp_index >> bit) % 2 == 0
+        small = jnp.concatenate([jnp.where(low, small, other), jnp.where(low, other, small)])
+
+    hidden_units = w_gate_up.shape[2]
     share = -(-hidden_units // (chips * TILE)) * TILE
     local_ff = 2 * share
     spare = share * chips - hidden_units
@@ -743,123 +1022,117 @@
     fresh = lax.broadcasted_iota(jnp.int32, (share, 1), 0) >= chip * share - begin
     dn_part = jnp.where(fresh, dn_part, jnp.zeros_like(dn_part))
     dn_part = lax.dynamic_slice_in_dim(dn_part, core * (share // 2), share // 2, 0)
-
-    def collect(part):
-        pairs = lax.all_gather(part, "mp", axis=0).reshape((2, 2) + part.shape)
-        mine = pick(pairs, core, 0)
-        other = swap(pick(pairs, 1 - core, 0), CORE)
-        return jnp.where(core == 0, mine, other), jnp.where(core == 0, other, mine)
-
-    normed_all, in_flat, gu_part, dn_part, cot = lax.optimization_barrier(
-        (normed_all, in_flat, gu_part, dn_part, cot)
-    )
-    w_gate, w_up = collect(gu_part)
-    w_gu = jnp.concatenate([w_gate[0], w_gate[1], w_up[0], w_up[1]], axis=1)
-    w_dn = jnp.concatenate(collect(dn_part), axis=1).reshape(local_ff, width)
-
-    projected = mm(normed_all, in_flat).reshape(mp_count, packs, span, 4 * chans)
-
-    start = jnp.stack([seq_index * run, seq_index]).astype(jnp.int32)
-    gap_row = forget_gap.reshape(1, chans)
-    gain_row = group_gain.reshape(1, chans)
-    steps, half = run // BLOCK, span // BLOCK
+    out_flat = w_mix_out.reshape(-1, width)
+    normed, (gu_part, dn_part, small), in_pairs = plane_gather(
+        normed_own, (gu_part, dn_part, small), in_pairs
+    )
+    gu_first, gu_second = gu_part[: width // 2], gu_part[width // 2 :]
+    query_forget, value_gate = both_halves(in_pairs)
+    w_in = jnp.concatenate(
+        [
+            part[j, :, k * head_size : (k + 1) * head_size]
+            for part, k in ((query_forget, 1), (value_gate, 0), (query_forget, 0), (value_gate, 1))
+            for j in range(2)
+        ],
+        axis=1,
+    )
+
+    cot_own = pack_major(lax.dynamic_slice_in_dim(out_cotangent, mp_index * span, span, 0))
+    cot_low, gu_first, dn_part, _ = together(cot_own.astype(BF16), gu_first, dn_part, in_pairs)
+    dn_pairs = gather_shares(dn_part)
+    first_pairs = gather_shares(gu_first)
+
+    small = pick(small.reshape(2, 2, 2, head_size), core, 0)
+    gap_row, gain_row = small[:, 0].reshape(1, chans), small[:, 1].reshape(1, chans)
+
+    projected = None
+    for a in range(0, seq_count, 2):
+        projected = project_call(projected, a, seq_count, normed[a], normed[a + 1], w_in)
+    cot, projected, _ = plane_gather(cot_low, projected)
+    projected = projected.reshape(seq_count, packs, span, 4 * chans)
+
+    halves = span // BLOCK
+    steps = seq_count * halves
+    where = jnp.stack([seq_index, run, mp_index * span, halves]).astype(jnp.int32)
     block = (1, packs, BLOCK, chans)
+    fv_block = (1, packs, BLOCK, 2 * chans)
     wide = (1, packs, BLOCK, 4 * chans)
+    pairs = packs * heads
+    runs_shape = (packs, seq_count, heads, head_size, head_size)
+    run_block = (packs, 1, heads, head_size, head_size)
+    tall_shape = (packs, seq_count, heads, head_size + 8, head_size)
+    tall_block = (packs, 1, heads, head_size + 8, head_size)
+    unit = 2 * BLOCK * head_size * head_size * pairs * steps
+    common = [(doc_lengths, "smem", None), (gap_row, "whole", None)]
+    call = functools.partial(recur_call, steps=steps, halves=halves, where=where)
+
+    def to_scan(array):
+        array = jnp.transpose(array, (0, 2, 1, 3, 4)).astype(BF16)
+        array = array.reshape((pairs,) + array.shape[2:])
+        return lax.all_to_all(array, "mp", split_axis=0, concat_axis=0, tiled=True)
+
+    def from_scan(array):
+        array = lax.all_to_all(array, "mp", split_axis=0, concat_axis=0, tiled=True)
+        array = array.reshape((packs, heads) + array.shape[1:])
+        return jnp.transpose(array, (0, 2, 1, 3, 4))
+
+    [run_state] = call(
+        states_kernel,
+        reverse=False,
+        ins=common + [(projected, "near", fv_block)],
+        outs=[(tall_shape, F32, "run", tall_block)],
+        scratch=[],
+        flops=3 * unit,
+        name="run_states",
+    )
+    decays = to_scan(run_state)
+    entering = from_scan(scan_call(decays, decays, False))
+    row_shape = (seq_count, packs, span, chans)
     state_shape = (packs, heads, head_size, head_size)
-    unit = 2 * BLOCK * head_size * head_size * packs * heads * steps
-    common = [(doc_lengths, "smem", None), (start, "smem", None), (gap_row, "whole", None)]
-    run_state, run_decay = recur_call(
-        states_kernel,
-        steps,
-        half,
-        False,
-        common + [(projected, 1, block), (projected, 2, block)],
-        [(state_shape, F32, "whole", None), ((packs, 1, chans), F32, "whole", None)],
-        [],
-        3 * unit,
-        "run_states",
-    )
-    all_states = lax.all_gather(run_state.astype(BF16), "seq")
-    all_decays = lax.all_gather(run_decay, "seq")
-    row_shape = (mp_count, packs, span, chans)
-    heads_out, mixed, kept = recur_call(
+    heads_out, mixed, kept = call(
         forward_kernel,
-        steps,
-        half,
-        False,
-        common
-        + [
-            (gain_row, "whole", None),
-            (projected, 0, wide),
-            (all_states, "whole", None),
-            (all_decays, "whole", None),
-        ],
-        [
-            (row_shape, BF16, 0, block),
-            (row_shape, F32, 0, block),
+        reverse=False,
+        ins=common
+        + [(gain_row, "whole", None), (projected, "near", wide), (entering, "run", run_block)],
+        outs=[
+            (row_shape, BF16, "rows", block),
+            (row_shape, F32, "rows", block),
             ((steps,) + state_shape, F32, "block", (1,) + state_shape),
         ],
-        [pltpu.VMEM(state_shape, F32)],
-        6 * unit,
-        "mix_forward",
-    )
+        scratch=[pltpu.VMEM(state_shape, F32)],
+        flops=6 * unit,
+        name="mix_forward",
+    )
+    gu_second, dn_pairs, first_pairs, cot, _ = together(
+        gu_second, dn_pairs, first_pairs, cot, entering
+    )
+    second_pairs = gather_shares(gu_second)
+
+    def side_by_side(pairs):
+        gate, up = both_halves(pairs)
+        return jnp.concatenate([gate[0], gate[1], up[0], up[1]], axis=1)
+
+    w_dn = jnp.concatenate(both_halves(dn_pairs), axis=1).reshape(local_ff, width)
+    w_low, w_high = side_by_side(first_pairs), side_by_side(second_pairs)
+
+    split = (chips, 2, rows, 2, head_size)
     heads_tok = lax.all_to_all(
-        heads_out.reshape(mp_count, rows, chans), "mp", split_axis=0, concat_axis=0, tiled=True
-    )
-    heads_tok = jnp.transpose(heads_tok, (1, 0, 2)).reshape(rows, mp_count * chans)
-    out_flat = w_mix_out.reshape(-1, width)
+        heads_out.reshape(seq_count, rows, chans), "seq", split_axis=0, concat_axis=0, tiled=True
+    )
+    heads_tok = jnp.transpose(heads_tok.reshape(split), (2, 1, 3, 0, 4)).reshape(rows, -1)
     hidden = own + mm(heads_tok, out_flat)
     scale_two = rms_scale(hidden)
     normed_two = (hidden * scale_two * norm2_gain).astype(BF16)
 
-    two = plane_gather(normed_two)
-    groups = ((6, 7), (2, 3, 4, 5), (0, 1))
-    act_of, pre_of, two_of, cot_of = {}, {}, {}, {}
-    down_parts = {}
-    for group in reversed(groups):
-        two_of[group] = jnp.concatenate([two[a] for a in group])
-        cot_of[group] = jnp.concatenate([cot[a] for a in group])
-        pre = mm(two_of[group], w_gu)
-        pre_of[group] = pre
-        act_of[group] = (jax.nn.silu(pre[:, :local_ff]) * pre[:, local_ff:]).astype(BF16)
-    for group in groups:
-        made = mm(act_of[group], w_dn).astype(BF16)
-        for k, a in enumerate(group):
-            down_parts[a] = made[k * rows : k * rows + rows]
-    back_parts, grad_of = {}, {}
-    for group in groups:
-        pre_gate, pre_up = pre_of[group][:, :local_ff], pre_of[group][:, local_ff:]
-        grad_act = mm(cot_of[group], w_dn, NT)
-        grad_of[group] = jnp.concatenate(
-            [grad_act * pre_up * silu_slope(pre_gate), grad_act * jax.nn.silu(pre_gate)], axis=1
-        ).astype(BF16)
-        made = mm(grad_of[group], w_gu, NT).astype(BF16)
-        for k, a in enumerate(group):
-            back_parts[a] = made[k * rows : k * rows + rows]
-    grad_normed_two = plane_scatter(back_parts)
-    gu_grad = sum(mm(two_of[g], grad_of[g], TN) for g in groups).astype(BF16)
-    dn_grad = sum(mm(act_of[g], cot_of[g], TN) for g in groups).astype(BF16)
-    grad_normed_two, gu_grad, dn_grad, down_parts = lax.optimization_barrier(
-        (grad_normed_two, gu_grad, dn_grad, down_parts)
-    )
-    layer_out = token_major(hidden + plane_scatter(down_parts))
-
-    norm2_part = jnp.sum(grad_normed_two * hidden * scale_two, axis=0)
-    grad_hidden = cot_own + rms_back(grad_normed_two, hidden, scale_two, norm2_gain)
-    grad_mix = grad_hidden.astype(BF16)
-    grad_tok = mm(grad_mix, out_flat, NT).astype(BF16)
-    grad_tok = jnp.transpose(grad_tok.reshape(rows, mp_count, chans), (1, 0, 2))
-    grad_heads = lax.all_to_all(grad_tok, "mp", split_axis=0, concat_axis=0, tiled=True)
-    grad_heads = grad_heads.reshape(row_shape)
-
-    def deliver(parts):
+    def ready(parts):
         mine = pick(parts, core, 0)
         other = swap(pick(parts, 1 - core, 0), CORE)
         low = jnp.where(core == 0, mine, other)
         high = jnp.where(core == 0, other, mine)
-        return lax.psum_scatter(
-            jnp.concatenate([low, high]), "mp", scatter_dimension=0, tiled=True
-        )[0]
+        return jnp.concatenate([low, high])
+
+    def deliver(terms):
+        return lax.psum_scatter(terms, "mp", scatter_dimension=0, tiled=True)[0]
 
     def hand_round(piece):
         got = [pick(piece, chip, 0)]
@@ -867,93 +1140,216 @@
         got = jnp.stack(got)
         return [pick(got, chip ^ c, 0) for c in range(chips)]
 
-    gu_grad = gu_grad.reshape(chips, 2, slice_d, 2, 2, share)
-    gu_grad = jnp.transpose(gu_grad, (1, 4, 3, 0, 2, 5))
-    got = [q.astype(F32) for q in hand_round(jnp.transpose(deliver(gu_grad), (1, 0, 2, 3)))]
+    act, grad_gu, down_parts, back_parts = {}, {}, {}, {}
+    order = range(seq_count)
+
+    def feed(a):
+        made = feed_call((two[a], two[a + 1]), (cot[a], cot[a + 1]), w_low, w_high, w_dn)
+        for k, at in enumerate((a, a + 1)):
+            act[at], grad_gu[at], down_parts[at], back_parts[at] = made[4 * k : 4 * k + 4]
+
+    two = {0: normed_two}
+    for across in (CORE, XLINK, YLINK):
+        two[across] = swap(normed_two, across)
+    feed(0)
+    two[XLINK], two[YLINK], down_parts[0] = together(two[XLINK], two[YLINK], down_parts[0])
+    middle = rows // 2
+    far_first = swap(two[YLINK][:middle], XLINK)
+    far_second = swap(two[XLINK][middle:], YLINK)
+    two[3], two[5] = swap(two[XLINK], CORE), swap(two[YLINK], CORE)
+    feed(2)
+    two[YLINK], down_parts[2] = together(two[YLINK], down_parts[2])
+    feed(4)
+    chip_back = {2: chip_sum(back_parts, 2)}
+    far_first, far_second, chip_back, down_parts[4] = together(
+        far_first, far_second, chip_back, down_parts[4]
+    )
+    two[6] = jnp.concatenate([far_first, far_second])
+    two[7] = jnp.concatenate([swap(far_first, CORE), swap(far_second, CORE)])
+    feed(6)
+    for a in (4, 6, 0):
+        chip_back[a] = chip_sum(back_parts, a)
+
+    def place_gu(out, total):
+        for d in range(seq_count):
+            for j in range(2):
+                for g in range(2):
+                    at = (2 * g + j) * share
+                    out[d % 2, j, d // 2, g] = total[
+                        d * slice_d : (d + 1) * slice_d, at : at + share
+                    ].astype(BF16)
+
+    def place_dn(out, total):
+        for d in range(seq_count):
+            for j in range(2):
+                out[d % 2, j, d // 2] = total[
+                    j * share : (j + 1) * share, d * slice_d : (d + 1) * slice_d
+                ].astype(BF16)
+
+    chip_back, grad_gu = together(chip_back, grad_gu)
+    gu_grad = outer_call(
+        [two[a] for a in order],
+        [grad_gu[a] for a in order],
+        (2, 2, chips, 2, slice_d, share),
+        place_gu,
+        "gate_up_grad",
+    )
+
+    def during_last(gu_grad):
+        held, first_act = together(gu_grad, act[0])
+        dn_grad = outer_call(
+            [first_act] + [act[a] for a in order[1:]],
+            [cot[a] for a in order],
+            (2, 2, chips, share, slice_d),
+            place_dn,
+            "down_grad",
+        )
+        return ready(held), dn_grad
+
+    grad_normed_two, _, (gu_grad, dn_grad) = plane_scatter(
+        back_parts, chip_back, gu_grad, during_last
+    )
+    grad_normed_two, down_parts = together(grad_normed_two, down_parts)
+    gu_grad = deliver(gu_grad)
+
+    norm2_part = jnp.sum(grad_normed_two * hidden * scale_two, axis=0)
+    grad_hidden = cot_own + rms_back(grad_normed_two, hidden, scale_two, norm2_gain)
+    grad_mix = grad_hidden.astype(BF16)
+    grad_tok = mm(grad_mix, out_flat, NT).astype(BF16)
+    grad_tok = jnp.transpose(
+        grad_tok.reshape(rows, 2, 2, chips, head_size), (3, 1, 0, 2, 4)
+    ).reshape(seq_count, rows, chans)
+    grad_tok, dn_grad = together(grad_tok, ready(dn_grad))
+    dn_grad = deliver(dn_grad)
+    grad_heads = lax.all_to_all(grad_tok, "seq", split_axis=0, concat_axis=0, tiled=True)
+    grad_heads = grad_heads.reshape(row_shape)
+
+    out_grad = mm(heads_tok, grad_mix, TN).astype(BF16)
+    out_grad = out_grad.reshape(all_heads, seq_count, head_size // seq_count, width)
+
+    grad_out, grad_gate, group_part, run_grad = call(
+        gate_back_kernel,
+        reverse=True,
+        ins=common
+        + [
+            (gain_row, "whole", None),
+            (projected, "near", wide),
+            (mixed, "rows", block),
+            (grad_heads, "rows", block),
+        ],
+        outs=[
+            (row_shape, F32, "rows", block),
+            (row_shape, BF16, "rows", block),
+            ((1, chans), F32, "whole", None),
+            (runs_shape, BF16, "run", run_block),
+        ],
+        scratch=[pltpu.VMEM(state_shape, F32)],
+        flops=3 * unit,
+        name="gate_back",
+    )
+    entering_back = from_scan(scan_call(decays, to_scan(run_grad), True))
+    out_grad = plane_scatter(
+        {a: pick(out_grad, seq_index ^ a, 1) for a in range(seq_count)}, None, entering_back
+    )[0].astype(BF16)
+    mix_out_grad = lax.psum_scatter(out_grad, "mp", scatter_dimension=0, tiled=True).astype(F32)
+    grad_projected, gap_part = call(
+        backward_kernel,
+        reverse=True,
+        ins=common
+        + [
+            (projected, "near", wide),
+            (grad_out, "rows", block),
+            (grad_gate, "rows", block),
+            (kept, "block", (1,) + state_shape),
+            (entering_back, "run", run_block),
+        ],
+        outs=[
+            ((seq_count, packs, span, 4 * chans), BF16, "near", wide),
+            ((1, chans), F32, "whole", None),
+        ],
+        scratch=[pltpu.VMEM(state_shape, F32)],
+        flops=12 * unit,
+        name="mix_backward",
+    )
+    grad_projected = grad_projected.reshape(seq_count, rows, 4 * chans)
+    def place_in(out, total):
+        for d in range(seq_count):
+            for j in range(2):
+                for k, of in enumerate((2, 0, 1, 3)):
+                    at = of * chans + j * head_size
+                    out[d % 2, j, d // 2, :, k * head_size : (k + 1) * head_size] = total[
+                        d * slice_d : (d + 1) * slice_d, at : at + head_size
+                    ].astype(BF16)
+
+    in_grad = outer_call(
+        [normed[a] for a in order],
+        [grad_projected],
+        (2, 2, chips, slice_d, 4 * head_size),
+        place_in,
+        "mix_in_grad",
+    )
+    grad_projected, in_grad = together(grad_projected, in_grad)
+    in_parts, norm1_part, chip_in = {}, 0.0, {}
+    in_grad = ready(in_grad)
+    for a in (2, 4, 0, 6):
+        in_parts[a], in_parts[a + 1], part = back_call(
+            grad_projected, a, normed[a], normed[a + 1], w_in
+        )
+        norm1_part = norm1_part + part
+        if a == 2:
+            grad_projected, in_grad, part = together(grad_projected, in_grad, part)
+            in_grad = deliver(in_grad)
+        elif a != 6:
+            chip_in[2 if a == 4 else 4] = chip_sum(in_parts, 2 if a == 4 else 4)
+            grad_projected, chip_in, part = together(grad_projected, chip_in, part)
+    norm1_part = norm1_part[0] / norm1_gain
+    layer_out = token_major(
+        hidden + plane_scatter(down_parts, None, entering_back, grad_projected)[0]
+    )
+    got = [q.astype(F32) for q in hand_round(gu_grad)]
     got[-1] = got[-1][:, :, spare:]
     gate_up_grad = jnp.transpose(jnp.concatenate(got, axis=-1), (1, 0, 2))
-    dn_grad = dn_grad.reshape(2, share, chips, 2, slice_d)
-    got = hand_round(deliver(jnp.transpose(dn_grad, (3, 0, 2, 1, 4))))
+    got = hand_round(dn_grad)
     got[-1] = got[-1][spare:]
     down_grad = jnp.concatenate(got, axis=0).astype(F32)
 
-    out_grad = mm(heads_tok, grad_mix, TN).astype(BF16)
-    out_grad = out_grad.reshape(mp_count * heads, seq_count, head_size // seq_count, width)
-    out_grad = plane_scatter(
-        {a: pick(out_grad, seq_index ^ a, 1) for a in range(seq_count)}
-    ).astype(BF16)
-    mix_out_grad = lax.psum_scatter(out_grad, "mp", scatter_dimension=0, tiled=True).astype(F32)
-
-    grad_out, grad_gate, group_part, run_grad = recur_call(
-        gate_back_kernel,
-        steps,
-        half,
-        True,
-        common
-        + [
-            (gain_row, "whole", None),
-            (projected, 0, wide),
-            (mixed, 0, block),
-            (grad_heads, 0, block),
-        ],
-        [
-            (row_shape, F32, 0, block),
-            (row_shape, BF16, 0, block),
-            ((1, chans), F32, "whole", None),
-            (state_shape, F32, "whole", None),
-        ],
-        [],
-        3 * unit,
-        "gate_back",
-    )
-    all_grads = lax.all_gather(run_grad.astype(BF16), "seq")
-    grad_projected, gap_part = recur_call(
-        backward_kernel,
-        steps,
-        half,
-        True,
-        common
-        + [
-            (projected, 0, wide),
-            (grad_out, 0, block),
-            (grad_gate, 0, block),
-            (kept, "block", (1,) + state_shape),
-            (all_grads, "whole", None),
-            (all_decays, "whole", None),
-        ],
-        [((mp_count, packs, span, 4 * chans), BF16, 0, wide), ((1, chans), F32, "whole", None)],
-        [pltpu.VMEM(state_shape, F32)],
-        12 * unit,
-        "mix_backward",
-    )
-    grad_flat = grad_projected.reshape(mp_count * rows, 4 * chans)
-    back_in = mm(grad_flat, in_flat, NT)
-    norm1_part = jnp.sum(back_in * normed_all.astype(F32), axis=0) / norm1_gain
-    grad_normed = lax.psum_scatter(
-        back_in.astype(BF16), "mp", scatter_dimension=0, tiled=True
-    ).astype(F32)
-    in_grad = mm(normed_all, grad_flat, TN).astype(BF16)
-    in_grad = in_grad.reshape(seq_count, slice_d, 4 * chans)
-    mix_in_grad = plane_scatter(
-        {a: pick(in_grad, seq_index ^ a, 0) for a in range(seq_count)}
-    ).reshape(slice_d, 4, chans)
+    grad_normed, _, (gate_up_grad, down_grad, layer_out) = plane_scatter(
+        in_parts, chip_in, None, (gate_up_grad, down_grad, layer_out)
+    )
+    got = [q.astype(F32).reshape(slice_d, 4, head_size) for q in hand_round(in_grad)]
+    mix_in_grad = jnp.concatenate(got, axis=-1)
 
     tokens_grad = token_major(
         grad_hidden + rms_back(grad_normed, own, scale_one, norm1_gain)
     )
-    small = jnp.stack([group_part, gap_part]).reshape(2, heads, head_size)
-    small = lax.psum_scatter(small, "seq", scatter_dimension=2, tiled=True)
-    norm1_grad = lax.psum_scatter(norm1_part, ("seq", "mp"), scatter_dimension=0, tiled=True)
-    norm2_grad = lax.psum_scatter(norm2_part, ("seq", "mp"), scatter_dimension=0, tiled=True)
+
+    def set_heads(part):
+        row = jnp.zeros((2, 2, chips, head_size), F32)
+        mine = part.reshape(1, 2, 1, head_size)
+        return lax.dynamic_update_slice(row, mine, (core, 0, chip, 0)).reshape(-1)
+
+    gains = whole_sum(
+        jnp.stack([norm1_part, norm2_part, set_heads(gap_part), set_heads(group_part)])
+    )
+    own_slice = width // (seq_count * mp_count)
+    norms = lax.dynamic_slice_in_dim(
+        gains[:2], (seq_index * mp_count + mp_index) * own_slice, own_slice, 1
+    )
+    tall, narrow = all_heads // mp_count, head_size // seq_count
+    small = lax.dynamic_slice(
+        gains[2:].reshape(2, all_heads, head_size),
+        (0, mp_index * tall, seq_index * narrow),
+        (2, tall, narrow),
+    )
     return (
         layer_out,
         tokens_grad,
-        norm1_grad,
+        norms[0],
         mix_in_grad,
+        small[0],
         small[1],
-        small[0],
         mix_out_grad,
-        norm2_grad,
+        norms[1],
         gate_up_grad,
         down_grad,
     )

time: 1440 us -> 1120 us (0.78)
  Pallas kernels: 80.4 us -> 369 us
  matrix products: 300 us -> 24.7 us
  blocking collectives: 199 us -> 0 us
  waiting for transfers between devices: 503 us -> 325 us
  starting transfers between devices: 47 us -> 99.2 us
  local copies, waits for them, and re-layouts: 186 us -> 141 us
  other arithmetic: 94.2 us -> 132 us
    pallas_call x4 -> x21, Pallas kernels: 80.4 us -> 369 us  [the longest x4 115 us: feed_call(): pl.pallas_call(feed_kernel, grid=(rows // tile,), in_specs=[cut(width)] *...]
    dot_general x24 -> x3, matrix products: 300 us -> 24.7 us  [mm(): return lax.dot_general(a, b, (dims, ((), ())), preferred_element_type=F32)]
    all_to_all x0 -> x6, waiting for transfers between devices: none -> 149 us  [the longest x2 69 us: to_scan(): return lax.all_to_all(array, 'mp', split_axis=0, concat_axis=0, tiled=True)]
    ppermute x68 -> x83, waiting for transfers between devices: 288 us -> 151 us  [swap(): lax.ppermute(value, 'seq', [(i, i ^ across) for i in range(lax.axis_size(...]
    all_to_all x2 -> x0, blocking collectives: 135 us -> none  [the longest x1 86 us: plane_device(): lax.all_to_all(heads_out.reshape(mp_count, rows, chans), 'mp', split_axis...]
    reduce_scatter x3, waiting for transfers between devices: 109 us -> 0.04 us  [deliver(): return lax.psum_scatter(terms, 'mp', scatter_dimension=0, tiled=True)[0]]
    all_gather x5 -> x4, waiting for transfers between devices: 105 us -> 0.08 us  [gather_shares(): return lax.all_gather(part, 'mp', axis=0).reshape((2, 2) + part.shape)]
    unnamed x1 -> x0, blocking collectives: 55.5 us -> none
  transfers between devices with their start and end apart: 78 -> 104, of which waited for: 34 -> 36; matrix products, arithmetic and copies ran while one was open for 32% -> 22% of each run, Pallas kernels for 4% -> 33%
where the time goes in v2:
time: 1120 us; the launch traced here: 1110 us
  Pallas kernels  369 us (33%)
  waiting for transfers between devices  325 us (29%)
  local copies, waits for them, and re-layouts  141 us (13%)
  other arithmetic  132 us (12%)
  starting transfers between devices  99.2 us (9%)
  matrix products  24.7 us (2%)
  between operations  16.3 us (1%)
    ppermute x83, waiting for transfers between devices, swap(): lax.ppermute(value, 'seq', [(i, i ^ across) for i in range(lax.axis_size(...  151 us
    pallas_call x4, Pallas kernels, feed_call(): pl.pallas_call(feed_kernel, grid=(rows // tile,), in_specs=[cut(width)] *...  115 us
    pallas_call x4, Pallas kernels, recur_call(): pl.pallas_call(kernel, grid_spec=pltpu.PrefetchScalarGridSpec(num_scalar_...  103 us
    pallas_call x3, Pallas kernels, outer_call(): pl.pallas_call(functools.partial(outer_kernel, count, place), grid=(count...  76.9 us
    all_to_all x2, waiting for transfers between devices, to_scan(): return lax.all_to_all(array, 'mp', split_axis=0, concat_axis=0, tiled=True)  69 us
    ppermute x83, starting transfers between devices, swap(): lax.ppermute(value, 'seq', [(i, i ^ across) for i in range(lax.axis_size(...  62.1 us
    convert_element_type x21, other arithmetic, add_low(): return (a.astype(F32) + b.astype(F32)).astype(BF16)  57.3 us
    unnamed x193, local copies, waits for them, and re-layouts  42.4 us
  transfers between devices with their start and end apart: 104, of which 36 were waited for; matrix products, arithmetic and copies ran while one was open for 22% of the time, Pallas kernels for 33%

profile of v2, /device:TPU:0, one launch (start us, length us, event | category | flops | bytes accessed | tf_op | source)
XLA Modules:
  0.0 1108.2 jit_solution(11673580747778713472)
XLA Ops:
  31.3 9.2 constant_dynamic-slice_fusion.10
  43.9 25.5 %collective-permute-done.1.left.refs_2_ = bf16[512,2048]{1,0:T(8,128)(2,1)} collective-permute-done((bf16[512,2048]{1,0:T(8,128)(2,1)S(1)}, bf16[512,2048]{1,0:T(8,128)(2,1)}, u32[]{:S(2)}, u32[]{:S(2)}) %collective-permute-start.1) | collective-permute-done | bytes 2097184 | tf_op jit(solution)/shard_map/ppermute | solution.py:892
  86.6 12.6 %collective-permute-done.5 = bf16[256,2048]{1,0:T(8,128)(2,1)} collective-permute-done((bf16[256,2048]{1,0:T(8,128)(2,1)S(1)}, bf16[256,2048]{1,0:T(8,128)(2,1)}, u32[]{:S(2)}, u32[]{:S(2)}) %collective-permute-start.5) | collective-permute-done | bytes 1048608 | tf_op jit(solution)/shard_map/ppermute | solution.py:892
  118.4 8.7 project.4.rest_0_
  158.2 16.2 %run_states.1 = f32[2,8,2,136,128]{4,3,2,1,0:T(8,128)S(1)} custom-call(s32[4]{0:T(128)S(1)} %pad_add_fusion.where, s32[2,4]{1,0:T(2,128)S(1)} %copy-done.16, f32[1,256]{1,0:T(1,128)S(1)} %get-tuple-element.476.gap, f32[8,2,256,1024]{3,2,1,0:T(8,128)} %bitcast.284), custom_call_target="tpu_custom_call" | custom-call | flops 40265320 | bytes 838913 | tf_op jit(solution)/shard_map/run_states/pallas_call | solution.py:640
  187.4 50.2 %all-to-all-done.decays.states = bf16[4,8,136,128]{3,2,1,0:T(8,128)(2,1)S(1)} async-done(((bf16[4,8,136,128]{3,2,1,0:T(8,128)(2,1)}), bf16[4,8,136,128]{3,2,1,0:T(8,128)(2,1)S(1)}, u32[]{:S(2)}, u32[]{:S(2)}) %all-to-all-start) | async-done | bytes 1114144 | tf_op jit(solution)/shard_map/all_to_all | solution.py:1072
  252.4 21.8 %all-to-all-done.1 = bf16[4,8,128,128]{3,2,1,0:T(8,128)(2,1)S(1)} async-done(((bf16[4,8,128,128]{3,2,1,0:T(8,128)(2,1)}), bf16[4,8,128,128]{3,2,1,0:T(8,128)(2,1)S(1)}, u32[]{:S(2)}, u32[]{:S(2)}) %all-to-all-start.1) | async-done | bytes 1048608 | tf_op jit(solution)/shard_map/all_to_all | solution.py:1075
  277.2 26.2 %mix_forward.1 = (bf16[8,2,256,256]{3,2,1,0:T(8,128)(2,1)S(1)}, f32[8,2,256,256]{3,2,1,0:T(8,128)}, f32[16,2,2,128,128]{4,3,2,1,0:T(8,128)}) custom-call(s32[4]{0:T(128)S(1)} %pad_add_fusion.where, s32[2,4]{1,0:T(2,128)S(1)} %copy-done.16, f32[1,256]{1,0:T(1,128)S(1)} %get-tuple-element.476.gap, f32[1,256]{1,0:T(1,128)S(1)} %get-tuple-element.475.gain, ...), custom_call_target="tpu_custom_call" | custom-call | flops 80530640 | bytes 891393 | tf_op jit(solution)/shard_map/mix_forward/pallas_call | solution.py:640
  316.4 19.9 %all-to-all-done.2 = bf16[8,512,256]{1,2,0:T(8,128)(2,1)S(1)} async-done(((bf16[8,512,256]{1,2,0:T(8,128)(2,1)}), bf16[8,512,256]{1,2,0:T(8,128)(2,1)S(1)}, u32[]{:S(2)}, u32[]{:S(2)}) %all-to-all-start.2) | async-done | bytes 2097184 | tf_op jit(solution)/shard_map/all_to_all | solution.py:1119
  339.3 9.7 multiply_reduce_fusion.2
  367.2 28.6 %feed.4 = (bf16[512,768]{1,0:T(8,128)(2,1)}, bf16[512,1536]{1,0:T(8,128)(2,1)}, bf16[512,2048]{1,0:T(8,128)(2,1)}, bf16[512,2048]{1,0:T(8,128)(2,1)}, bf16[512,7...) custom-call(bf16[512,2048]{1,0:T(8,128)(2,1)} %copy-done.27, ...), custom_call_target="tpu_custom_call" | custom-call | flops 966367616 | bytes 1048576 | tf_op jit(solution)/shard_map/feed/pallas_call | solution.py:805
  395.8 8.8 collective-permute-done.26.refs_0_.refs_2_
  413.4 29.0 %feed.5 = (bf16[512,768]{1,0:T(8,128)(2,1)}, bf16[512,1536]{1,0:T(8,128)(2,1)}, bf16[512,2048]{1,0:T(8,128)(2,1)}, bf16[512,2048]{1,0:T(8,128)(2,1)}, bf16[512,7...) custom-call(bf16[512,2048]{1,0:T(8,128)(2,1)} %copy-done.32, ...), custom_call_target="tpu_custom_call" | custom-call | flops 966367616 | bytes 1048576 | tf_op jit(solution)/shard_map/feed/pallas_call | solution.py:805
  448.2 28.8 %feed.6 = (bf16[512,768]{1,0:T(8,128)(2,1)}, bf16[512,1536]{1,0:T(8,128)(2,1)}, bf16[512,2048]{1,0:T(8,128)(2,1)}, bf16[512,2048]{1,0:T(8,128)(2,1)}, bf16[512,7...) custom-call(bf16[512,2048]{1,0:T(8,128)(2,1)} %collective-permute-done.27.ref, ...), custom_call_target="tpu_custom_call" | custom-call | flops 966367616 | bytes 1048576 | tf_op jit(solution)/shard_map/feed/pallas_call | solution.py:805
  486.1 28.8 %feed.7 = (bf16[512,768]{1,0:T(8,128)(2,1)}, bf16[512,1536]{1,0:T(8,128)(2,1)}, bf16[512,2048]{1,0:T(8,128)(2,1)}, bf16[512,2048]{1,0:T(8,128)(2,1)}, bf16[512,7...) custom-call(bf16[512,2048]{1,0:T(8,128)(2,1)} %copy-done.35, ...), custom_call_target="tpu_custom_call" | custom-call | flops 966367616 | bytes 1048576 | tf_op jit(solution)/shard_map/feed/pallas_call | solution.py:805
  531.2 33.8 %gate_up_grad.1 = bf16[2,2,4,2,256,384]{5,4,3,2,1,0:T(8,128)(2,1)} custom-call(bf16[512,2048]{1,0:T(8,128)(2,1)} %copy-done.27, bf16[512,2048]{1,0:T(8,128)(2,1)} %copy-done.41, bf16[512,2048]{1,0:T(8,128)(2,1)} %copy-done.32, bf16[512,2048]{1,0:T(8,128)(2,1)} %copy-done.46, bf16[512,2048]{1,0:T(8,128)(2,1)} %collective-permute-done.27.refs_0_.refs_4_, ...), custom_call_target="tpu_custom_call" | custom-call | flops 1288490240 | bytes 1835008 | tf_op jit(solution)/shard_map/gate_up_grad/pallas_call | solution.py:867
  584.6 19.1 %down_grad.1 = bf16[2,2,4,384,256]{4,3,2,1,0:T(8,128)(2,1)} custom-call(bf16[512,768]{1,0:T(8,128)(2,1)} %get-tuple-element.273.refs_0_, bf16[512,768]{1,0:T(8,128)(2,1)} %get-tuple-element.274.refs_1_, bf16[512,768]{1,0:T(8,128)(2,1)} %get-tuple-element.275.refs_2_, bf16[512,768]{1,0:T(8,128)(2,1)} %get-tuple-element.276.refs_3_, ...), custom_call_target="tpu_custom_call" | custom-call | flops 644245120 | bytes 1441792 | tf_op jit(solution)/shard_map/down_grad/pallas_call | solution.py:867
  621.5 8.0 convolution_convert_fusion.1
  648.0 26.0 %all-to-all-done.3 = bf16[8,512,256]{2,1,0:T(8,128)(2,1)S(1)} async-done(((bf16[8,512,256]{2,1,0:T(8,128)(2,1)}), bf16[8,512,256]{2,1,0:T(8,128)(2,1)S(1)}, u32[]{:S(2)}, u32[]{:S(2)}) %all-to-all-start.3) | async-done | bytes 2097184 | tf_op jit(solution)/shard_map/all_to_all | solution.py:1224
  674.0 20.0 %gate_back.1 = (f32[8,2,256,256]{3,2,1,0:T(8,128)}, bf16[8,2,256,256]{3,2,1,0:T(8,128)(2,1)S(1)}, f32[1,256]{1,0:T(1,128)S(1)}, bf16[2,8,2,128,128]{4,3,2,1,0:T(8,128)(2,1)S(1)}) custom-call(s32[4]{0:T(128)S(1)} %pad_add_fusion.where, s32[2,4]{1,0:T(2,128)S(1)} %copy-done.16, f32[1,256]{1,0:T(1,128)S(1)} %get-tuple-element.476.gap, ...), custom_call_target="tpu_custom_call" | custom-call | flops 40265320 | bytes 1153537 | tf_op jit(solution)/shard_map/gate_back/pallas_call | solution.py:640
  712.6 18.8 %all-to-all-done.4.states = bf16[4,8,128,128]{3,2,1,0:T(8,128)(2,1)S(1)} async-done(((bf16[4,8,128,128]{3,2,1,0:T(8,128)(2,1)}), bf16[4,8,128,128]{3,2,1,0:T(8,128)(2,1)S(1)}, u32[]{:S(2)}, u32[]{:S(2)}) %all-to-all-start.4) | async-done | bytes 1048608 | tf_op jit(solution)/shard_map/all_to_all | solution.py:1072
  751.9 12.7 %all-to-all-done.5 = bf16[4,8,128,128]{3,2,1,0:T(8,128)(2,1)S(1)} async-done(((bf16[4,8,128,128]{3,2,1,0:T(8,128)(2,1)}), bf16[4,8,128,128]{3,2,1,0:T(8,128)(2,1)S(1)}, u32[]{:S(2)}, u32[]{:S(2)}) %all-to-all-start.5) | async-done | bytes 1048608 | tf_op jit(solution)/shard_map/all_to_all | solution.py:1075
  777.7 9.8 collective-permute-done.88
  794.1 40.1 %mix_backward.1 = (bf16[8,2,256,1024]{3,2,1,0:T(8,128)(2,1)}, f32[1,256]{1,0:T(1,128)S(1)}) custom-call(s32[4]{0:T(128)S(1)} %pad_add_fusion.where, s32[2,4]{1,0:T(2,128)S(1)} %copy-done.16, f32[1,256]{1,0:T(1,128)S(1)} %get-tuple-element.476.gap, f32[8,2,256,1024]{3,2,1,0:T(8,128)} %bitcast.287, f32[8,2,256,256]{3,2,1,0:T(8,128)} %get-tuple-element.295.grad_out, ...), custom_call_target="tpu_custom_call" | custom-call | flops 161061280 | bytes 1415630 | tf_op jit(solution)/shard_map/mix_backward/pallas_call | solution.py:640
  834.2 24.0 %mix_in_grad.1 = bf16[2,2,4,256,512]{4,3,2,1,0:T(8,128)(2,1)} custom-call(bf16[512,2048]{1,0:T(8,128)(2,1)} %copy-done.4, bf16[512,2048]{1,0:T(8,128)(2,1)} %collective-permute-done.right.refs_1_, bf16[512,2048]{1,0:T(8,128)(2,1)} %collective-permute-done.1.left.refs_2_, bf16[512,2048]{1,0:T(8,128)(2,1)} %collective-permute-done.7.right.refs_3_, ...), custom_call_target="tpu_custom_call" | custom-call | flops 858993472 | bytes 1572864 | tf_op jit(solution)/shard_map/mix_in_grad/pallas_call | solution.py:867
  876.4 9.9 project_back.4
  892.8 9.9 project_back.5
  938.5 9.5 project_back.6
  952.1 9.3 project_back.7
  981.1 20.6 %collective-permute-done.74 = f32[4,2048]{1,0:T(4,128)S(1)} collective-permute-done((f32[4,2048]{1,0:T(4,128)S(1)}, f32[4,2048]{1,0:T(4,128)S(1)}, u32[]{:S(2)}, u32[]{:S(2)}) %collective-permute-start.74) | collective-permute-done | bytes 32800 | tf_op jit(solution)/shard_map/ppermute | solution.py:951
  1033.4 10.1 collective-permute-done.52
  1054.1 16.7 %collective-permute-done.53 = bf16[256,2048]{1,0:T(8,128)(2,1)S(1)} collective-permute-done((bf16[256,2048]{1,0:T(8,128)(2,1)S(1)}, bf16[256,2048]{1,0:T(8,128)(2,1)S(1)}, u32[]{:S(2)}, u32[]{:S(2)}) %collective-permute-start.53) | collective-permute-done | bytes 1048608 | tf_op jit(solution)/shard_map/ppermute | solution.py:892
  (555 shorter events, 469.5 us)
Async XLA Ops:
  7.2 92.1 %all-gather.8.cloned.1.call-start = ((), (), s32[]{:S(2)}) async-start(), calls=%async_computation.10 | async-start | bytes 5242880 | tf_op jit(solution)/shard_map/all_gather | solution.py:992
  12.4 262.0 %all-gather.10.cloned.1.call-start = ((), (), s32[]{:S(2)}) async-start(), calls=%async_computation.15 | async-start | bytes 3932160 | tf_op jit(solution)/shard_map/all_gather | solution.py:992
  20.6 48.9 %collective-permute-start.1 = (bf16[512,2048]{1,0:T(8,128)(2,1)S(1)}, bf16[512,2048]{1,0:T(8,128)(2,1)}, u32[]{:S(2)}, u32[]{:S(2)}) collective-permute-start(bf16[512,2048]{1,0:T(8,128)(2,1)S(1)} %fusion.1.left.refs_0_), channel_id=1, source_target_pairs={{0,8},{4,12},{8,0},{12,4},{16,24},{20,28},{24,16},{28,20},{1,9},{5... | collective-permute-start | bytes 6291464 | tf_op jit(solution)/shard_map/ppermute | solution.py:892
  23.1 47.8 %collective-permute-start.2 = (bf16[512,2048]{1,0:T(8,128)(2,1)S(1)}, bf16[512,2048]{1,0:T(8,128)(2,1)}, u32[]{:S(2)}, u32[]{:S(2)}) collective-permute-start(bf16[512,2048]{1,0:T(8,128)(2,1)S(1)} %fusion.1.left.refs_0_), channel_id=1, source_target_pairs={{0,16},{4,20},{8,24},{12,28},{16,0},{20,4},{24,8},{28,12},{1,17},{... | collective-permute-start | bytes 6291464 | tf_op jit(solution)/shard_map/ppermute | solution.py:892
  99.3 175.1 %all-gather.12.cloned.1.call-start = ((), (), s32[]{:S(2)}) async-start(), calls=%async_computation.16 | async-start | bytes 3932160 | tf_op jit(solution)/shard_map/all_gather | solution.py:992
  103.1 46.0 %collective-permute-start.9 = (bf16[512,2048]{1,0:T(8,128)(2,1)}, bf16[512,2048]{1,0:T(8,128)(2,1)}, u32[]{:S(2)}, u32[]{:S(2)}) collective-permute-start(bf16[512,2048]{1,0:T(8,128)(2,1)} %bitcast_convert_fusion.refs_2_.refs_8_), channel_id=1, source_target_pairs={{0,4},{4,0},{8,12},{12,8},{16,20},{20,16},{24,28},{28,24},{1,5},{5... | collective-permute-start | bytes 6291464 | tf_op jit(solution)/shard_map/ppermute | solution.py:892
  103.5 48.0 %collective-permute-start.10 = (bf16[512,2048]{1,0:T(8,128)(2,1)}, bf16[512,2048]{1,0:T(8,128)(2,1)}, u32[]{:S(2)}, u32[]{:S(2)}) collective-permute-start(bf16[512,2048]{1,0:T(8,128)(2,1)} %bitcast_convert_fusion.refs_2_.refs_8_), channel_id=1, source_target_pairs={{0,8},{4,12},{8,0},{12,4},{16,24},{20,28},{24,16},{28,20},{1,9},{5... | collective-permute-start | bytes 6291464 | tf_op jit(solution)/shard_map/ppermute | solution.py:892
  109.9 47.8 %collective-permute-start.11 = (bf16[512,2048]{1,0:T(8,128)(2,1)S(1)}, bf16[512,2048]{1,0:T(8,128)(2,1)}, u32[]{:S(2)}, u32[]{:S(2)}) collective-permute-start(bf16[512,2048]{1,0:T(8,128)(2,1)S(1)} %copy-done.26), channel_id=1, source_target_pairs={{0,16},{4,20},{8,24},{12,28},{16,0},{20,4},{24,8},{28,12},{1,17},{... | collective-permute-start | bytes 6291464 | tf_op jit(solution)/shard_map/ppermute | solution.py:892
  157.7 88.7 %collective-permute-start.18 = (bf16[512,2048]{1,0:T(8,128)(2,1)}, bf16[512,2048]{1,0:T(8,128)(2,1)}, u32[]{:S(2)}, u32[]{:S(2)}) collective-permute-start(bf16[512,2048]{1,0:T(8,128)(2,1)} %collective-permute-done.10.refs_2_.refs_10_), channel_id=1, source_target_pairs={{0,4},{4,0},{8,12},{12,8},{16,20},{20,16},{24,28},{28,24},{1,5},{5... | collective-permute-start | bytes 6291464 | tf_op jit(solution)/shard_map/ppermute | solution.py:892
  157.7 88.7 %collective-permute-start.19 = (bf16[512,2048]{1,0:T(8,128)(2,1)}, bf16[512,2048]{1,0:T(8,128)(2,1)}, u32[]{:S(2)}, u32[]{:S(2)}) collective-permute-start(bf16[512,2048]{1,0:T(8,128)(2,1)} %collective-permute-done.11.refs_2_.refs_12_), channel_id=1, source_target_pairs={{0,4},{4,0},{8,12},{12,8},{16,20},{20,16},{24,28},{28,24},{1,5},{5... | collective-permute-start | bytes 6291464 | tf_op jit(solution)/shard_map/ppermute | solution.py:892
  175.7 61.9 %all-to-all-start = ((bf16[4,8,136,128]{3,2,1,0:T(8,128)(2,1)}), bf16[4,8,136,128]{3,2,1,0:T(8,128)(2,1)S(1)}, u32[]{:S(2)}, u32[]{:S(2)}) async-start(bf16[4,8,136,128]{3,2,1,0:T(8,128)(2,1)} %bitcast.28), calls=%async_computation | async-start | bytes 2228224 | tf_op jit(solution)/shard_map/all_to_all | solution.py:1072
  184.3 62.1 %collective-permute-start.16 = (bf16[256,2048]{1,0:T(8,128)(2,1)}, bf16[256,2048]{1,0:T(8,128)(2,1)}, u32[]{:S(2)}, u32[]{:S(2)}) collective-permute-start(bf16[256,2048]{1,0:T(8,128)(2,1)} %slice.216), channel_id=1, source_target_pairs={{0,8},{4,12},{8,0},{12,4},{16,24},{20,28},{24,16},{28,20},{1,9},{5... | collective-permute-start | bytes 3145736 | tf_op jit(solution)/shard_map/ppermute | solution.py:892
  185.9 60.5 %collective-permute-start.17 = (bf16[256,2048]{1,0:T(8,128)(2,1)S(1)}, bf16[256,2048]{1,0:T(8,128)(2,1)}, u32[]{:S(2)}, u32[]{:S(2)}) collective-permute-start(bf16[256,2048]{1,0:T(8,128)(2,1)S(1)} %slice.217), channel_id=1, source_target_pairs={{0,16},{4,20},{8,24},{12,28},{16,0},{20,4},{24,8},{28,12},{1,17},{... | collective-permute-start | bytes 3145736 | tf_op jit(solution)/shard_map/ppermute | solution.py:892
  246.4 102.6 %all-gather.14.cloned.1.call-start = ((), (), s32[]{:S(2)}) async-start(), calls=%async_computation.17 | async-start | bytes 3932160 | tf_op jit(solution)/shard_map/all_gather | solution.py:992
  356.8 47.8 %collective-permute-start.26 = (bf16[512,2048]{1,0:T(8,128)(2,1)S(1)}, bf16[512,2048]{1,0:T(8,128)(2,1)S(1)}, u32[]{:S(2)}, u32[]{:S(2)}) collective-permute-start(bf16[512,2048]{1,0:T(8,128)(2,1)S(1)} %multiply_convert_fusion.refs_0_), channel_id=1, source_target_pairs={{0,8},{4,12},{8,0},{12,4},{16,24},{20,28},{24,16},{28,20},{1,9},{5... | collective-permute-start | bytes 6291464 | tf_op jit(solution)/shard_map/ppermute | solution.py:892
  357.3 47.6 %collective-permute-start.27 = (bf16[512,2048]{1,0:T(8,128)(2,1)S(1)}, bf16[512,2048]{1,0:T(8,128)(2,1)}, u32[]{:S(2)}, u32[]{:S(2)}) collective-permute-start(bf16[512,2048]{1,0:T(8,128)(2,1)S(1)} %multiply_convert_fusion.refs_0_), channel_id=1, source_target_pairs={{0,16},{4,20},{8,24},{12,28},{16,0},{20,4},{24,8},{28,12},{1,17},{... | collective-permute-start | bytes 6291464 | tf_op jit(solution)/shard_map/ppermute | solution.py:892
  404.9 43.3 %collective-permute-start.32 = (bf16[512,2048]{1,0:T(8,128)(2,1)}, bf16[512,2048]{1,0:T(8,128)(2,1)}, u32[]{:S(2)}, u32[]{:S(2)}) collective-permute-start(bf16[512,2048]{1,0:T(8,128)(2,1)} %collective-permute-done.27.refs_0_.refs_4_), channel_id=1, source_target_pairs={{0,4},{4,0},{8,12},{12,8},{16,20},{20,16},{24,28},{28,24},{1,5},{5... | collective-permute-start | bytes 6291464 | tf_op jit(solution)/shard_map/ppermute | solution.py:892
  529.1 43.5 %collective-permute-start.39 = (bf16[256,2048]{1,0:T(8,128)(2,1)}, bf16[256,2048]{1,0:T(8,128)(2,1)}, u32[]{:S(2)}, u32[]{:S(2)}) collective-permute-start(bf16[256,2048]{1,0:T(8,128)(2,1)} %get-tuple-element.429), channel_id=1, source_target_pairs={{0,8},{4,12},{8,0},{12,4},{16,24},{20,28},{24,16},{28,20},{1,9},{5... | collective-permute-start | bytes 3145736 | tf_op jit(solution)/shard_map/ppermute | solution.py:892
  530.6 43.3 %collective-permute-start.40 = (bf16[256,2048]{1,0:T(8,128)(2,1)}, bf16[256,2048]{1,0:T(8,128)(2,1)}, u32[]{:S(2)}, u32[]{:S(2)}) collective-permute-start(bf16[256,2048]{1,0:T(8,128)(2,1)} %get-tuple-element.428), channel_id=1, source_target_pairs={{0,16},{4,20},{8,24},{12,28},{16,0},{20,4},{24,8},{28,12},{1,17},{... | collective-permute-start | bytes 3145736 | tf_op jit(solution)/shard_map/ppermute | solution.py:892
  647.4 272.7 %reduce-scatter.7.cloned.1.call-start = ((), (), s32[]{:S(2)}) async-start(), calls=%async_computation.12 | async-start | bytes 3932160 | tf_op jit(solution)/shard_map/reduce_scatter | solution.py:1135
  738.6 231.0 %reduce-scatter.11.cloned.1.call-start = ((), (), s32[]{:S(2)}) async-start(), calls=%async_computation.14 | async-start | bytes 1310720 | tf_op jit(solution)/shard_map/reduce_scatter | solution.py:1254
  791.6 229.8 %reduce-scatter.5.cloned.1.call-start = ((), (), s32[]{:S(2)}) async-start(), calls=%async_computation.11 | async-start | bytes 7864320 | tf_op jit(solution)/shard_map/reduce_scatter | solution.py:1135
  792.4 287.6 %reduce-scatter.9.cloned.1.call-start = ((), (), s32[]{:S(2)}) async-start(), calls=%async_computation.13 | async-start | bytes 5242880 | tf_op jit(solution)/shard_map/reduce_scatter | solution.py:1135
  792.4 67.9 %collective-permute-start.62 = (bf16[512,2048]{1,0:T(8,128)(2,1)}, bf16[512,2048]{1,0:T(8,128)(2,1)}, u32[]{:S(2)}, u32[]{:S(2)}) collective-permute-start(bf16[512,2048]{1,0:T(8,128)(2,1)} %get-tuple-element.324), channel_id=1, source_target_pairs={{0,4},{4,0},{8,12},{12,8},{16,20},{20,16},{24,28},{28,24},{1,5},{5... | collective-permute-start | bytes 6291464 | tf_op jit(solution)/shard_map/ppermute | solution.py:892
  792.5 73.2 %collective-permute-start.64 = (bf16[512,2048]{1,0:T(8,128)(2,1)}, bf16[512,2048]{1,0:T(8,128)(2,1)}, u32[]{:S(2)}, u32[]{:S(2)}) collective-permute-start(bf16[512,2048]{1,0:T(8,128)(2,1)} %get-tuple-element.326), channel_id=1, source_target_pairs={{0,4},{4,0},{8,12},{12,8},{16,20},{20,16},{24,28},{28,24},{1,5},{5... | collective-permute-start | bytes 6291464 | tf_op jit(solution)/shard_map/ppermute | solution.py:892
  793.0 77.6 %collective-permute-start.66 = (bf16[512,2048]{1,0:T(8,128)(2,1)}, bf16[512,2048]{1,0:T(8,128)(2,1)}, u32[]{:S(2)}, u32[]{:S(2)}) collective-permute-start(bf16[512,2048]{1,0:T(8,128)(2,1)} %get-tuple-element.328), channel_id=1, source_target_pairs={{0,4},{4,0},{8,12},{12,8},{16,20},{20,16},{24,28},{28,24},{1,5},{5... | collective-permute-start | bytes 6291464 | tf_op jit(solution)/shard_map/ppermute | solution.py:892
  793.7 94.5 %collective-permute-start.61 = (bf16[512,2048]{1,0:T(8,128)(2,1)}, bf16[512,2048]{1,0:T(8,128)(2,1)}, u32[]{:S(2)}, u32[]{:S(2)}) collective-permute-start(bf16[512,2048]{1,0:T(8,128)(2,1)} %get-tuple-element.322), channel_id=1, source_target_pairs={{0,4},{4,0},{8,12},{12,8},{16,20},{20,16},{24,28},{28,24},{1,5},{5... | collective-permute-start | bytes 6291464 | tf_op jit(solution)/shard_map/ppermute | solution.py:892
  888.1 46.4 %collective-permute-start.46 = (bf16[512,2048]{1,0:T(8,128)(2,1)}, bf16[512,2048]{1,0:T(8,128)(2,1)}, u32[]{:S(2)}, u32[]{:S(2)}) collective-permute-start(bf16[512,2048]{1,0:T(8,128)(2,1)} %get-tuple-element.305), channel_id=1, source_target_pairs={{0,4},{4,0},{8,12},{12,8},{16,20},{20,16},{24,28},{28,24},{1,5},{5... | collective-permute-start | bytes 6291464 | tf_op jit(solution)/shard_map/ppermute | solution.py:892
  902.7 45.3 %collective-permute-start.47 = (bf16[512,2048]{1,0:T(8,128)(2,1)}, bf16[512,2048]{1,0:T(8,128)(2,1)}, u32[]{:S(2)}, u32[]{:S(2)}) collective-permute-start(bf16[512,2048]{1,0:T(8,128)(2,1)} %get-tuple-element.310), channel_id=1, source_target_pairs={{0,4},{4,0},{8,12},{12,8},{16,20},{20,16},{24,28},{28,24},{1,5},{5... | collective-permute-start | bytes 6291464 | tf_op jit(solution)/shard_map/ppermute | solution.py:892
  930.1 45.1 %collective-permute-start.69 = (bf16[256,2048]{1,0:T(8,128)(2,1)}, bf16[256,2048]{1,0:T(8,128)(2,1)}, u32[]{:S(2)}, u32[]{:S(2)}) collective-permute-start(bf16[256,2048]{1,0:T(8,128)(2,1)} %add_convert_fusion.13), channel_id=1, source_target_pairs={{0,8},{4,12},{8,0},{12,4},{16,24},{20,28},{24,16},{28,20},{1,9},{5... | collective-permute-start | bytes 3145736 | tf_op jit(solution)/shard_map/ppermute | solution.py:892
  975.2 49.3 %collective-permute-start.48 = (bf16[256,2048]{1,0:T(8,128)(2,1)}, bf16[256,2048]{1,0:T(8,128)(2,1)S(1)}, u32[]{:S(2)}, u32[]{:S(2)}) collective-permute-start(bf16[256,2048]{1,0:T(8,128)(2,1)} %slice.237), channel_id=1, source_target_pairs={{0,8},{4,12},{8,0},{12,4},{16,24},{20,28},{24,16},{28,20},{1,9},{5... | collective-permute-start | bytes 3145736 | tf_op jit(solution)/shard_map/ppermute | solution.py:892
  975.5 50.2 %collective-permute-start.49 = (bf16[256,2048]{1,0:T(8,128)(2,1)}, bf16[256,2048]{1,0:T(8,128)(2,1)}, u32[]{:S(2)}, u32[]{:S(2)}) collective-permute-start(bf16[256,2048]{1,0:T(8,128)(2,1)} %slice.238), channel_id=1, source_target_pairs={{0,16},{4,20},{8,24},{12,28},{16,0},{20,4},{24,8},{28,12},{1,17},{... | collective-permute-start | bytes 3145736 | tf_op jit(solution)/shard_map/ppermute | solution.py:892
  (159 other events, 2405.9 us)
Sparse Core Ops, SparseCore 0:
  12.5 83.5 all-gather.7
  99.4 64.8 all-gather.9
  166.5 100.6 all-gather.11
  274.5 62.1 all-gather.13
  650.2 67.5 reduce-scatter.6
  791.7 28.1 reduce-scatter.10
  822.3 109.4 reduce-scatter.4
  963.5 78.2 reduce-scatter.8

commit v3 on v2

--- a/solution.py
+++ b/solution.py
@@ -650,7 +650,7 @@
         compiler_params=pltpu.CompilerParams(
             dimension_semantics=("arbitrary",), vmem_limit_bytes=48 << 20
         ),
-        cost_estimate=pl.CostEstimate(flops=flops // 20, bytes_accessed=moved // 20, transcendentals=0),
+        cost_estimate=pl.CostEstimate(flops=flops, bytes_accessed=moved // 20, transcendentals=0),
         name=name,
     )(where, *arrays)
 
@@ -704,7 +704,7 @@
             dimension_semantics=("arbitrary",), vmem_limit_bytes=40 << 20
         ),
         cost_estimate=pl.CostEstimate(
-            flops=rows * width * columns // 5, bytes_accessed=rows * width, transcendentals=0
+            flops=rows * width * columns * 240 // 100, bytes_accessed=rows * width, transcendentals=0
         ),
         name="project",
     )(*arrays)
@@ -763,7 +763,7 @@
             dimension_semantics=("arbitrary",), vmem_limit_bytes=40 << 20
         ),
         cost_estimate=pl.CostEstimate(
-            flops=rows * width * columns // 5, bytes_accessed=rows * width, transcendentals=0
+            flops=rows * width * columns * 240 // 100, bytes_accessed=rows * width, transcendentals=0
         ),
         name="project_back",
     )(left, right, grads, weights)
@@ -812,10 +812,77 @@
             dimension_semantics=("arbitrary",), vmem_limit_bytes=58 << 20
         ),
         cost_estimate=pl.CostEstimate(
-            flops=flops // 20, bytes_accessed=rows * width, transcendentals=0
+            flops=flops * 60 // 100, bytes_accessed=rows * width, transcendentals=0
         ),
         name="feed",
     )(*two, *cot, w_low, w_high, w_dn)
+
+
+def spread_kernel(grads, weights, out):
+    units = weights[0, :, 0].reshape(-1, weights.shape[-1])
+    out[0] = mm(grads[...], units, NT).astype(BF16)
+
+
+def spread_call(grads, weights):
+    cores, shards, chips, size, width = weights.shape
+    rows = grads.shape[0]
+    return pl.pallas_call(
+        spread_kernel,
+        grid=(cores * chips,),
+        in_specs=[
+            pl.BlockSpec(grads.shape, lambda s: (0, 0)),
+            pl.BlockSpec(
+                (1, shards, 1, size, width),
+                lambda s: (lax.rem(s, cores), 0, lax.div(s, cores), 0, 0),
+            ),
+        ],
+        out_specs=pl.BlockSpec((1, rows, shards * size), lambda s: (s, 0, 0)),
+        out_shape=jax.ShapeDtypeStruct((cores * chips, rows, shards * size), BF16),
+        compiler_params=pltpu.CompilerParams(
+            dimension_semantics=("arbitrary",), vmem_limit_bytes=32 << 20
+        ),
+        cost_estimate=pl.CostEstimate(
+            flops=rows * width * size * 1920 // 100, bytes_accessed=rows * width, transcendentals=0
+        ),
+        name="spread",
+    )(grads, weights)
+
+
+def heads_grad_kernel(pieces, heads, grads, out):
+    made = mm(heads[0], grads[...], TN).astype(BF16)
+    tall = made.shape[0] // out.shape[2]
+    low = tall // pieces
+    for j in range(out.shape[2]):
+        for s in range(pieces):
+            out[s, 0, j, 0] = made[j * tall + s * low : j * tall + (s + 1) * low]
+
+
+def heads_grad_call(heads, grads, cores, shards):
+    count, rows, chans = heads.shape
+    width = grads.shape[1]
+    size = chans // shards
+    chips = count // cores
+    shape = (count, cores, shards, chips, size // count, width)
+    return pl.pallas_call(
+        functools.partial(heads_grad_kernel, count),
+        grid=(count,),
+        in_specs=[
+            pl.BlockSpec((1, rows, chans), lambda s: (s, 0, 0)),
+            pl.BlockSpec(grads.shape, lambda s: (0, 0)),
+        ],
+        out_specs=pl.BlockSpec(
+            (count, 1, shards, 1, size // count, width),
+            lambda s: (0, lax.rem(s, cores), 0, lax.div(s, cores), 0, 0),
+        ),
+        out_shape=jax.ShapeDtypeStruct(shape, BF16),
+        compiler_params=pltpu.CompilerParams(
+            dimension_semantics=("arbitrary",), vmem_limit_bytes=32 << 20
+        ),
+        cost_estimate=pl.CostEstimate(
+            flops=rows * width * size * 1920 // 100, bytes_accessed=rows * width, transcendentals=0
+        ),
+        name="mix_out_grad",
+    )(heads, grads)
 
 
 def outer_kernel(count, place, *refs):
@@ -880,7 +947,7 @@
             dimension_semantics=("arbitrary",), vmem_limit_bytes=58 << 20
         ),
         cost_estimate=pl.CostEstimate(
-            flops=count * rows * m * n // 10,
+            flops=count * rows * m * n * 120 // 100,
             bytes_accessed=rows * (m + n),
             transcendentals=0,
         ),
@@ -922,35 +989,30 @@
     return add_low(parts[a], swap(parts[a ^ CORE], CORE))
 
 
-def plane_scatter(parts, chip=None, far=None, last=None):
-    half = parts[0].shape[0] // 2
-    chip = dict(chip or {})
-    for a in (2, 4, 6, 0):
-        if a not in chip:
-            chip[a] = chip_sum(parts, a)
-    mine_x = swap(chip[2][:half], XLINK)
-    mine_y = swap(chip[4][half:], YLINK)
-    from_x = swap(chip[6][:half], XLINK)
-    from_y = swap(chip[6][half:], YLINK)
-    mine_x, mine_y, from_x, from_y, far = together(mine_x, mine_y, from_x, from_y, far)
-    for_y, for_x = add_low(chip[4][:half], from_x), add_low(chip[2][half:], from_y)
-    if callable(last):
-        for_y, for_x, far = together(for_y, for_x, far)
-        last = last(far)
-    last_x, last_y, last = together(swap(for_x, XLINK), swap(for_y, YLINK), last)
-    low = chip[0][:half].astype(F32) + mine_x.astype(F32) + last_y.astype(F32)
-    high = chip[0][half:].astype(F32) + mine_y.astype(F32) + last_x.astype(F32)
-    return jnp.concatenate([low, high]), far, last
-
-
-def whole_sum(value):
-    for axis in ("seq", "mp"):
-        count = lax.axis_size(axis)
-        across = 1
-        while across < count:
-            value = value + lax.ppermute(value, axis, [(i, i ^ across) for i in range(count)])
-            across *= 2
-    return value
+def first_hops(chip):
+    half = chip[0].shape[0] // 2
+    return (
+        swap(chip[2][:half], XLINK),
+        swap(chip[4][half:], YLINK),
+        swap(chip[6][:half], XLINK),
+        swap(chip[6][half:], YLINK),
+    )
+
+
+def turned(chip, hops):
+    half = chip[4].shape[0] // 2
+    return add_low(chip[4][:half], hops[2]), add_low(chip[2][half:], hops[3])
+
+
+def last_hops(pair):
+    return swap(pair[0], YLINK), swap(pair[1], XLINK)
+
+
+def arrived(chip, hops, lasts):
+    half = chip[0].shape[0] // 2
+    low = chip[0][:half].astype(F32) + hops[0].astype(F32) + lasts[0].astype(F32)
+    high = chip[0][half:].astype(F32) + hops[1].astype(F32) + lasts[1].astype(F32)
+    return jnp.concatenate([low, high])
 
 
 def pick(array, index, axis):
@@ -1039,6 +1101,7 @@
 
     cot_own = pack_major(lax.dynamic_slice_in_dim(out_cotangent, mp_index * span, span, 0))
     cot_low, gu_first, dn_part, _ = together(cot_own.astype(BF16), gu_first, dn_part, in_pairs)
+
     dn_pairs = gather_shares(dn_part)
     first_pairs = gather_shares(gu_first)
 
@@ -1048,7 +1111,6 @@
     projected = None
     for a in range(0, seq_count, 2):
         projected = project_call(projected, a, seq_count, normed[a], normed[a + 1], w_in)
-    cot, projected, _ = plane_gather(cot_low, projected)
     projected = projected.reshape(seq_count, packs, span, 4 * chans)
 
     halves = span // BLOCK
@@ -1082,9 +1144,10 @@
         ins=common + [(projected, "near", fv_block)],
         outs=[(tall_shape, F32, "run", tall_block)],
         scratch=[],
-        flops=3 * unit,
+        flops=27 * unit,
         name="run_states",
     )
+    cot, run_state, _ = plane_gather(cot_low, run_state)
     decays = to_scan(run_state)
     entering = from_scan(scan_call(decays, decays, False))
     row_shape = (seq_count, packs, span, chans)
@@ -1100,7 +1163,7 @@
             ((steps,) + state_shape, F32, "block", (1,) + state_shape),
         ],
         scratch=[pltpu.VMEM(state_shape, F32)],
-        flops=6 * unit,
+        flops=45 * unit,
         name="mix_forward",
     )
     gu_second, dn_pairs, first_pairs, cot, _ = together(
@@ -1116,10 +1179,10 @@
     w_low, w_high = side_by_side(first_pairs), side_by_side(second_pairs)
 
     split = (chips, 2, rows, 2, head_size)
-    heads_tok = lax.all_to_all(
+    heads_by = lax.all_to_all(
         heads_out.reshape(seq_count, rows, chans), "seq", split_axis=0, concat_axis=0, tiled=True
     )
-    heads_tok = jnp.transpose(heads_tok.reshape(split), (2, 1, 3, 0, 4)).reshape(rows, -1)
+    heads_tok = jnp.transpose(heads_by.reshape(split), (2, 1, 3, 0, 4)).reshape(rows, -1)
     hidden = own + mm(heads_tok, out_flat)
     scale_two = rms_scale(hidden)
     normed_two = (hidden * scale_two * norm2_gain).astype(BF16)
@@ -1134,11 +1197,11 @@
     def deliver(terms):
         return lax.psum_scatter(terms, "mp", scatter_dimension=0, tiled=True)[0]
 
-    def hand_round(piece):
-        got = [pick(piece, chip, 0)]
-        got += [swap(pick(piece, chip ^ a, 0), 2 * a) for a in range(1, chips)]
-        got = jnp.stack(got)
-        return [pick(got, chip ^ c, 0) for c in range(chips)]
+    def handed(piece):
+        groups = [list(range(k, seq_count, 2)) for k in range(2)]
+        return lax.all_to_all(
+            piece, "seq", split_axis=0, concat_axis=0, axis_index_groups=groups, tiled=True
+        )
 
     act, grad_gu, down_parts, back_parts = {}, {}, {}, {}
     order = range(seq_count)
@@ -1166,9 +1229,11 @@
     )
     two[6] = jnp.concatenate([far_first, far_second])
     two[7] = jnp.concatenate([swap(far_first, CORE), swap(far_second, CORE)])
+    other = swap(back_parts[5], CORE)
     feed(6)
-    for a in (4, 6, 0):
-        chip_back[a] = chip_sum(back_parts, a)
+    other, back_parts = together(other, back_parts)
+    chip_back[4] = add_low(back_parts[4], other)
+    chip_back[6] = chip_sum(back_parts, 6)
 
     def place_gu(out, total):
         for d in range(seq_count):
@@ -1194,38 +1259,32 @@
         place_gu,
         "gate_up_grad",
     )
-
-    def during_last(gu_grad):
-        held, first_act = together(gu_grad, act[0])
-        dn_grad = outer_call(
-            [first_act] + [act[a] for a in order[1:]],
-            [cot[a] for a in order],
-            (2, 2, chips, share, slice_d),
-            place_dn,
-            "down_grad",
-        )
-        return ready(held), dn_grad
-
-    grad_normed_two, _, (gu_grad, dn_grad) = plane_scatter(
-        back_parts, chip_back, gu_grad, during_last
-    )
+    chip_back[0] = chip_sum(back_parts, 0)
+    hops, chip_back, gu_grad = together(first_hops(chip_back), chip_back, gu_grad)
+    onward, act = together(turned(chip_back, hops), act)
+    dn_grad = outer_call(
+        [act[a] for a in order],
+        [cot[a] for a in order],
+        (2, 2, chips, share, slice_d),
+        place_dn,
+        "down_grad",
+    )
+    lasts, dn_grad = together(last_hops(onward), dn_grad)
+    grad_normed_two = arrived(chip_back, hops, lasts)
     grad_normed_two, down_parts = together(grad_normed_two, down_parts)
-    gu_grad = deliver(gu_grad)
 
     norm2_part = jnp.sum(grad_normed_two * hidden * scale_two, axis=0)
     grad_hidden = cot_own + rms_back(grad_normed_two, hidden, scale_two, norm2_gain)
     grad_mix = grad_hidden.astype(BF16)
-    grad_tok = mm(grad_mix, out_flat, NT).astype(BF16)
-    grad_tok = jnp.transpose(
-        grad_tok.reshape(rows, 2, 2, chips, head_size), (3, 1, 0, 2, 4)
-    ).reshape(seq_count, rows, chans)
+    grad_tok = spread_call(grad_mix, w_mix_out.reshape(2, 2, chips, head_size, width))
     grad_tok, dn_grad = together(grad_tok, ready(dn_grad))
     dn_grad = deliver(dn_grad)
     grad_heads = lax.all_to_all(grad_tok, "seq", split_axis=0, concat_axis=0, tiled=True)
-    grad_heads = grad_heads.reshape(row_shape)
-
-    out_grad = mm(heads_tok, grad_mix, TN).astype(BF16)
-    out_grad = out_grad.reshape(all_heads, seq_count, head_size // seq_count, width)
+    chip_down = {a: chip_sum(down_parts, a) for a in (2, 4, 6, 0)}
+    out_grad = heads_grad_call(heads_by, grad_mix, 2, 2)
+    grad_heads, chip_down, out_grad = together(
+        grad_heads.reshape(row_shape), chip_down, out_grad
+    )
 
     grad_out, grad_gate, group_part, run_grad = call(
         gate_back_kernel,
@@ -1244,14 +1303,17 @@
             (runs_shape, BF16, "run", run_block),
         ],
         scratch=[pltpu.VMEM(state_shape, F32)],
-        flops=3 * unit,
+        flops=35 * unit,
         name="gate_back",
     )
-    entering_back = from_scan(scan_call(decays, to_scan(run_grad), True))
-    out_grad = plane_scatter(
-        {a: pick(out_grad, seq_index ^ a, 1) for a in range(seq_count)}, None, entering_back
-    )[0].astype(BF16)
-    mix_out_grad = lax.psum_scatter(out_grad, "mp", scatter_dimension=0, tiled=True).astype(F32)
+    out_grad = out_grad.reshape(seq_count, all_heads, head_size // seq_count, width)
+    out_parts = {a: pick(out_grad, seq_index ^ a, 0) for a in range(seq_count)}
+    chip_out = {a: chip_sum(out_parts, a) for a in (2, 4, 6, 0)}
+    run_grad, chip_out = together(to_scan(run_grad), chip_out)
+    entering_back = from_scan(scan_call(decays, run_grad, True))
+    hops_down = first_hops(chip_down)
+    entering_back, gu_grad = together(entering_back, ready(gu_grad))
+    gu_grad = deliver(gu_grad)
     grad_projected, gap_part = call(
         backward_kernel,
         reverse=True,
@@ -1268,10 +1330,15 @@
             ((1, chans), F32, "whole", None),
         ],
         scratch=[pltpu.VMEM(state_shape, F32)],
-        flops=12 * unit,
+        flops=69 * unit,
         name="mix_backward",
     )
     grad_projected = grad_projected.reshape(seq_count, rows, 4 * chans)
+    grad_projected, dn_grad, hops_down = together(grad_projected, dn_grad, hops_down)
+    dn_round = handed(dn_grad)
+    lasts_down = last_hops(turned(chip_down, hops_down))
+    chip_out = together(chip_out, grad_projected)[0]
+    hops_out = first_hops(chip_out)
     def place_in(out, total):
         for d in range(seq_count):
             for j in range(2):
@@ -1288,68 +1355,98 @@
         place_in,
         "mix_in_grad",
     )
-    grad_projected, in_grad = together(grad_projected, in_grad)
-    in_parts, norm1_part, chip_in = {}, 0.0, {}
-    in_grad = ready(in_grad)
-    for a in (2, 4, 0, 6):
+    grad_projected, in_grad, lasts_down, dn_round = together(
+        grad_projected, in_grad, lasts_down, dn_round
+    )
+    layer_out = token_major(hidden + arrived(chip_down, hops_down, lasts_down))
+    in_parts, chip_in = {}, {}
+
+    def back(a):
         in_parts[a], in_parts[a + 1], part = back_call(
             grad_projected, a, normed[a], normed[a + 1], w_in
         )
-        norm1_part = norm1_part + part
-        if a == 2:
-            grad_projected, in_grad, part = together(grad_projected, in_grad, part)
-            in_grad = deliver(in_grad)
-        elif a != 6:
-            chip_in[2 if a == 4 else 4] = chip_sum(in_parts, 2 if a == 4 else 4)
-            grad_projected, chip_in, part = together(grad_projected, chip_in, part)
-    norm1_part = norm1_part[0] / norm1_gain
-    layer_out = token_major(
-        hidden + plane_scatter(down_parts, None, entering_back, grad_projected)[0]
-    )
-    got = [q.astype(F32) for q in hand_round(gu_grad)]
-    got[-1] = got[-1][:, :, spare:]
-    gate_up_grad = jnp.transpose(jnp.concatenate(got, axis=-1), (1, 0, 2))
-    got = hand_round(dn_grad)
-    got[-1] = got[-1][spare:]
-    down_grad = jnp.concatenate(got, axis=0).astype(F32)
-
-    grad_normed, _, (gate_up_grad, down_grad, layer_out) = plane_scatter(
-        in_parts, chip_in, None, (gate_up_grad, down_grad, layer_out)
-    )
-    got = [q.astype(F32).reshape(slice_d, 4, head_size) for q in hand_round(in_grad)]
-    mix_in_grad = jnp.concatenate(got, axis=-1)
-
-    tokens_grad = token_major(
-        grad_hidden + rms_back(grad_normed, own, scale_one, norm1_gain)
-    )
-
+        return part
+
+    def from_core(a):
+        return swap(in_parts[a + 1], CORE)
+
+    half = rows // 2
+    in_mine = pick(in_grad, core, 0)
+    in_other = swap(pick(in_grad, 1 - core, 0), CORE)
+    norm1_part = back(6)
+    grad_projected, in_mine, in_other, hops_out, in_parts = together(
+        grad_projected, in_mine, in_other, hops_out, in_parts
+    )
+    lasts_out = last_hops(turned(chip_out, hops_out))
+    in_grad = jnp.concatenate(
+        [jnp.where(core == 0, in_mine, in_other), jnp.where(core == 0, in_other, in_mine)]
+    )
+    other = from_core(6)
+    norm1_part = norm1_part + back(2)
+    grad_projected, lasts_out, other, in_parts, in_grad, gu_grad = together(
+        grad_projected, lasts_out, other, in_parts, in_grad, gu_grad
+    )
+    in_grad = deliver(in_grad)
+    chip_in[6] = add_low(in_parts[6], other)
+    far_hops = swap(chip_in[6][:half], XLINK), swap(chip_in[6][half:], YLINK)
+    out_grad = arrived(chip_out, hops_out, lasts_out).astype(BF16)
+    out_grad = out_grad.reshape((mp_count, all_heads // mp_count) + out_grad.shape[1:])
+    other = from_core(2)
+    norm1_part = norm1_part + back(4)
+    grad_projected, other, in_parts = together(grad_projected, other, in_parts)
+    chip_in[2] = add_low(in_parts[2], other)
+    mine_x = swap(chip_in[2][:half], XLINK)
+    other = from_core(4)
+    norm1_part = norm1_part + back(0)
     def set_heads(part):
         row = jnp.zeros((2, 2, chips, head_size), F32)
         mine = part.reshape(1, 2, 1, head_size)
-        return lax.dynamic_update_slice(row, mine, (core, 0, chip, 0)).reshape(-1)
-
-    gains = whole_sum(
-        jnp.stack([norm1_part, norm2_part, set_heads(gap_part), set_heads(group_part)])
-    )
-    own_slice = width // (seq_count * mp_count)
-    norms = lax.dynamic_slice_in_dim(
-        gains[:2], (seq_index * mp_count + mp_index) * own_slice, own_slice, 1
-    )
-    tall, narrow = all_heads // mp_count, head_size // seq_count
-    small = lax.dynamic_slice(
-        gains[2:].reshape(2, all_heads, head_size),
-        (0, mp_index * tall, seq_index * narrow),
-        (2, tall, narrow),
-    )
+        row = lax.dynamic_update_slice(row, mine, (core, 0, chip, 0))
+        row = row.reshape(mp_count, all_heads // mp_count, seq_count, head_size // seq_count)
+        return jnp.transpose(row, (2, 0, 1, 3)).reshape(-1)
+
+    gains = jnp.stack(
+        [norm1_part[0] / norm1_gain, norm2_part, set_heads(gap_part), set_heads(group_part)]
+    )
+    gains = jnp.transpose(gains.reshape(4, seq_count, width // seq_count), (1, 0, 2))
+    far_hops, other, in_parts, chip_in, gu_round, gains, out_grad = together(
+        far_hops, other, in_parts, chip_in, handed(gu_grad), gains, out_grad
+    )
+    out_grad = lax.psum_scatter(out_grad, "mp", scatter_dimension=0, tiled=True)[0]
+    chip_in[4] = add_low(in_parts[4], other)
+    hops = mine_x, swap(chip_in[4][half:], YLINK)
+    lasts = last_hops(turned(chip_in, (None, None) + far_hops))
+    chip_in[0] = chip_sum(in_parts, 0)
+    gains = jnp.sum(lax.all_to_all(gains, "seq", split_axis=0, concat_axis=0, tiled=True), axis=0)
+    gains = jnp.transpose(gains.reshape(4, mp_count, -1), (1, 0, 2))
+    hops, lasts, chip_in, layer_out, gains = together(hops, lasts, chip_in, layer_out, gains)
+    gains = jnp.sum(lax.all_to_all(gains, "mp", split_axis=0, concat_axis=0, tiled=True), axis=0)
+    grad_normed = arrived(chip_in, hops, lasts)
+    got = [gu_round[c].astype(F32) for c in range(chips)]
+    got[-1] = got[-1][:, :, spare:]
+    gate_up_grad = jnp.transpose(jnp.concatenate(got, axis=-1), (1, 0, 2))
+    got = [dn_round[c] for c in range(chips)]
+    got[-1] = got[-1][spare:]
+    down_grad = jnp.concatenate(got, axis=0).astype(F32)
+    mix_out_grad = out_grad.astype(F32)
+    in_round = handed(in_grad)
+    got = [in_round[c].astype(F32).reshape(slice_d, 4, head_size) for c in range(chips)]
+    mix_in_grad = jnp.concatenate(got, axis=-1)
+
+    tokens_grad = token_major(
+        grad_hidden + rms_back(grad_normed, own, scale_one, norm1_gain)
+    )
+
+    small = gains[2:].reshape(2, all_heads // mp_count, head_size // seq_count)
     return (
         layer_out,
         tokens_grad,
-        norms[0],
+        gains[0],
         mix_in_grad,
         small[0],
         small[1],
         mix_out_grad,
-        norms[1],
+        gains[1],
         gate_up_grad,
         down_grad,
     )

time: 1120 us -> 1080 us (0.964)
  waiting for transfers between devices: 325 us -> 284 us
  Pallas kernels: 369 us -> 382 us
  matrix products: 24.7 us -> 11.8 us
    ppermute x83 -> x74, waiting for transfers between devices: 151 us -> 91.4 us  [swap(): lax.ppermute(value, 'seq', [(i, i ^ across) for i in range(lax.axis_size(...]
    all_to_all x0 -> x5, waiting for transfers between devices: none -> 41.1 us  [the longest x1 36.7 us: plane_device(): lax.all_to_all(gains, 'seq', split_axis=0, concat_axis=0, tiled=True)]
    ppermute x5 -> x0, waiting for transfers between devices: 23.8 us -> none  [whole_sum(): lax.ppermute(value, axis, [(i, i ^ across) for i in range(count)])]
    all_to_all x0 -> x5, starting transfers between devices: none -> 18.3 us  [the longest x3 11.5 us: handed(): lax.all_to_all(piece, 'seq', split_axis=0, concat_axis=0, axis_index_grou...]
    all_to_all x1, waiting for transfers between devices: 26 us -> 9.94 us  [plane_device(): lax.all_to_all(grad_tok, 'seq', split_axis=0, concat_axis=0, tiled=True)]
    all_to_all x2, waiting for transfers between devices: 34.5 us -> 48.5 us  [from_scan(): array = lax.all_to_all(array, 'mp', split_axis=0, concat_axis=0, tiled=True)]
    pallas_call x0 -> x2, Pallas kernels: none -> 14 us  [the longest x1 7.37 us: spread_call(): pl.pallas_call(spread_kernel, grid=(cores * chips,), in_specs=[pl.BlockSp...]
    dot_general x3 -> x1, matrix products: 24.7 us -> 11.8 us  [mm(): return lax.dot_general(a, b, (dims, ((), ())), preferred_element_type=F32)]
  transfers between devices with their start and end apart: 104 -> 95, of which waited for: 36 -> 28; matrix products, arithmetic and copies ran while one was open for 22% -> 23% of each run, Pallas kernels for 33% -> 36%
where the time goes in v3:
time: 1080 us; the launch traced here: 1070 us
  Pallas kernels  382 us (35%)
  waiting for transfers between devices  284 us (26%)
  local copies, waits for them, and re-layouts  143 us (13%)
  other arithmetic  136 us (13%)
  starting transfers between devices  96.8 us (9%)
  between operations  16.1 us (1%)
  matrix products  11.8 us (1%)
    pallas_call x4, Pallas kernels, feed_call(): pl.pallas_call(feed_kernel, grid=(rows // tile,), in_specs=[cut(width)] *...  115 us
    pallas_call x4, Pallas kernels, recur_call(): pl.pallas_call(kernel, grid_spec=pltpu.PrefetchScalarGridSpec(num_scalar_...  102 us
    ppermute x74, waiting for transfers between devices, swap(): lax.ppermute(value, 'seq', [(i, i ^ across) for i in range(lax.axis_size(...  91.4 us
    pallas_call x3, Pallas kernels, outer_call(): pl.pallas_call(functools.partial(outer_kernel, count, place), grid=(count...  77.3 us
    all_to_all x2, waiting for transfers between devices, to_scan(): return lax.all_to_all(array, 'mp', split_axis=0, concat_axis=0, tiled=True)  72 us
    convert_element_type x21, other arithmetic, add_low(): return (a.astype(F32) + b.astype(F32)).astype(BF16)  60.9 us
    unnamed x171, local copies, waits for them, and re-layouts  50.3 us
    ppermute x74, starting transfers between devices, swap(): lax.ppermute(value, 'seq', [(i, i ^ across) for i in range(lax.axis_size(...  49.3 us
  transfers between devices with their start and end apart: 95, of which 28 were waited for; matrix products, arithmetic and copies ran while one was open for 23% of the time, Pallas kernels for 36%

profile of v3, /device:TPU:0, one launch (start us, length us, event | category | flops | bytes accessed | tf_op | source)
XLA Modules:
  0.0 1069.1 jit_solution(7037501401365665847)
XLA Ops:
  31.3 9.0 constant_dynamic-slice_fusion.4
  43.7 25.8 %collective-permute-done.1.left.refs_2_ = bf16[512,2048]{1,0:T(8,128)(2,1)} collective-permute-done((bf16[512,2048]{1,0:T(8,128)(2,1)S(1)}, bf16[512,2048]{1,0:T(8,128)(2,1)}, u32[]{:S(2)}, u32[]{:S(2)}) %collective-permute-start.1) | collective-permute-done | bytes 2097184 | tf_op jit(solution)/shard_map/ppermute | solution.py:959
  86.6 12.6 %collective-permute-done.5 = bf16[256,2048]{1,0:T(8,128)(2,1)} collective-permute-done((bf16[256,2048]{1,0:T(8,128)(2,1)S(1)}, bf16[256,2048]{1,0:T(8,128)(2,1)}, u32[]{:S(2)}, u32[]{:S(2)}) %collective-permute-start.5) | collective-permute-done | bytes 1048608 | tf_op jit(solution)/shard_map/ppermute | solution.py:959
  118.4 8.7 project.4.rest_0_
  127.1 8.0 project.5.rest_0_
  135.1 8.0 project.6.rest_0_
  149.2 16.2 %run_states.1 = f32[2,8,2,136,128]{4,3,2,1,0:T(8,128)S(1)} custom-call(s32[4]{0:T(128)S(1)} %pad_add_fusion.where, s32[2,4]{1,0:T(2,128)S(1)} %copy-done.20, f32[1,256]{1,0:T(1,128)S(1)} %get-tuple-element.578.gap, f32[8,2,256,1024]{3,2,1,0:T(8,128)} %bitcast.245), custom_call_target="tpu_custom_call" | custom-call | flops 7247757312 | bytes 838913 | tf_op jit(solution)/shard_map/run_states/pallas_call | solution.py:640
  177.0 51.3 %all-to-all-done.decays.states = bf16[4,8,136,128]{3,2,1,0:T(8,128)(2,1)S(1)} async-done(((bf16[4,8,136,128]{3,2,1,0:T(8,128)(2,1)}), bf16[4,8,136,128]{3,2,1,0:T(8,128)(2,1)S(1)}, u32[]{:S(2)}, u32[]{:S(2)}) %all-to-all-start) | async-done | bytes 1114144 | tf_op jit(solution)/shard_map/all_to_all | solution.py:1134
  243.1 29.3 %all-to-all-done.1 = bf16[4,8,128,128]{3,2,1,0:T(8,128)(2,1)S(1)} async-done(((bf16[4,8,128,128]{3,2,1,0:T(8,128)(2,1)}), bf16[4,8,128,128]{3,2,1,0:T(8,128)(2,1)S(1)}, u32[]{:S(2)}, u32[]{:S(2)}) %all-to-all-start.1) | async-done | bytes 1048608 | tf_op jit(solution)/shard_map/all_to_all | solution.py:1137
  275.4 26.2 %mix_forward.1 = (bf16[8,2,256,256]{3,2,1,0:T(8,128)(2,1)S(1)}, f32[8,2,256,256]{3,2,1,0:T(8,128)}, f32[16,2,2,128,128]{4,3,2,1,0:T(8,128)}) custom-call(s32[4]{0:T(128)S(1)} %pad_add_fusion.where, s32[2,4]{1,0:T(2,128)S(1)} %copy-done.20, f32[1,256]{1,0:T(1,128)S(1)} %get-tuple-element.578.gap, f32[1,256]{1,0:T(1,128)S(1)} %get-tuple-element.577.gain, ...), custom_call_target="tpu_custom_call" | custom-call | flops 12079595520 | bytes 891393 | tf_op jit(solution)/shard_map/mix_forward/pallas_call | solution.py:640
  313.6 19.9 %all-to-all-done.2.heads = bf16[8,512,256]{2,1,0:T(8,128)(2,1)S(1)} async-done(((bf16[8,512,256]{2,1,0:T(8,128)(2,1)}), bf16[8,512,256]{2,1,0:T(8,128)(2,1)S(1)}, u32[]{:S(2)}, u32[]{:S(2)}) %all-to-all-start.2) | async-done | bytes 2097184 | tf_op jit(solution)/shard_map/all_to_all | solution.py:1182
  341.7 11.8 %multiply_reduce_fusion.2 = (f32[512]{0:T(512)S(1)}, f32[512,2048]{1,0:T(8,128)}) fusion(bf16[512,2048]{0,1:T(8,128)(2,1)} %bitcast.257, bf16[2048,2048]{1,0:T(8,128)(2,1)} %bitcast.232, f32[256,2,2048]{2,0,1:T(8,128)} %copy-done.26), kind=kOutput, calls=%fused_computation.36 | convolution fusion | flops 4298112512 | bytes 18876416 | tf_op jit(solution)/shard_map/dot_general | solution.py:364
  370.6 28.9 %feed.4 = (bf16[512,768]{1,0:T(8,128)(2,1)}, bf16[512,1536]{1,0:T(8,128)(2,1)}, bf16[512,2048]{1,0:T(8,128)(2,1)}, bf16[512,2048]{1,0:T(8,128)(2,1)}, bf16[512,7...) custom-call(bf16[512,2048]{1,0:T(8,128)(2,1)} %copy-done.58, ...), custom_call_target="tpu_custom_call" | custom-call | flops 11596411904 | bytes 1048576 | tf_op jit(solution)/shard_map/feed/pallas_call | solution.py:805
  399.5 14.0 %collective-permute-done.15.refs_0_.refs_2_ = bf16[512,2048]{1,0:T(8,128)(2,1)} collective-permute-done((bf16[512,2048]{1,0:T(8,128)(2,1)S(1)}, bf16[512,2048]{1,0:T(8,128)(2,1)}, u32[]{:S(2)}, u32[]{:S(2)}) %collective-permute-start.15) | collective-permute-done | bytes 2097184 | tf_op jit(solution)/shard_map/ppermute | solution.py:959
  422.1 28.8 %feed.5 = (bf16[512,768]{1,0:T(8,128)(2,1)}, bf16[512,1536]{1,0:T(8,128)(2,1)}, bf16[512,2048]{1,0:T(8,128)(2,1)}, bf16[512,2048]{1,0:T(8,128)(2,1)}, bf16[512,7...) custom-call(bf16[512,2048]{1,0:T(8,128)(2,1)} %collective-permute-done.15.ref, ...), custom_call_target="tpu_custom_call" | custom-call | flops 11596411904 | bytes 1048576 | tf_op jit(solution)/shard_map/feed/pallas_call | solution.py:805
  457.8 29.0 %feed.6 = (bf16[512,768]{1,0:T(8,128)(2,1)}, bf16[512,1536]{1,0:T(8,128)(2,1)}, bf16[512,2048]{1,0:T(8,128)(2,1)}, bf16[512,2048]{1,0:T(8,128)(2,1)}, bf16[512,7...) custom-call(bf16[512,2048]{1,0:T(8,128)(2,1)} %collective-permute-done.16.ref, ...), custom_call_target="tpu_custom_call" | custom-call | flops 11596411904 | bytes 1048576 | tf_op jit(solution)/shard_map/feed/pallas_call | solution.py:805
  497.6 28.8 %feed.7 = (bf16[512,768]{1,0:T(8,128)(2,1)}, bf16[512,1536]{1,0:T(8,128)(2,1)}, bf16[512,2048]{1,0:T(8,128)(2,1)}, bf16[512,2048]{1,0:T(8,128)(2,1)}, bf16[512,7...) custom-call(bf16[512,2048]{1,0:T(8,128)(2,1)} %copy-done.62, ...), custom_call_target="tpu_custom_call" | custom-call | flops 11596411904 | bytes 1048576 | tf_op jit(solution)/shard_map/feed/pallas_call | solution.py:805
  541.7 33.7 %gate_up_grad.1 = bf16[2,2,4,2,256,384]{5,4,3,2,1,0:T(8,128)(2,1)} custom-call(bf16[512,2048]{1,0:T(8,128)(2,1)} %copy-done.58, bf16[512,2048]{1,0:T(8,128)(2,1)} %copy-done.72, bf16[512,2048]{1,0:T(8,128)(2,1)} %collective-permute-done.15.refs_0_.refs_2_, bf16[512,2048]{1,0:T(8,128)(2,1)} %copy-done.73, ...), custom_call_target="tpu_custom_call" | custom-call | flops 15461881856 | bytes 1835008 | tf_op jit(solution)/shard_map/gate_up_grad/pallas_call | solution.py:934
  593.8 19.3 %down_grad.1 = bf16[2,2,4,384,256]{4,3,2,1,0:T(8,128)(2,1)} custom-call(bf16[512,768]{1,0:T(8,128)(2,1)} %get-tuple-element.335.refs_0_, bf16[512,768]{1,0:T(8,128)(2,1)} %get-tuple-element.336.refs_1_, bf16[512,768]{1,0:T(8,128)(2,1)} %get-tuple-element.337.refs_2_, bf16[512,768]{1,0:T(8,128)(2,1)} %get-tuple-element.338.refs_3_, ...), custom_call_target="tpu_custom_call" | custom-call | flops 7730940928 | bytes 1441792 | tf_op jit(solution)/shard_map/down_grad/pallas_call | solution.py:934
  625.8 7.4 spread.1
  665.7 9.9 all-to-all-done.3
  680.7 20.0 %gate_back.1 = (f32[8,2,256,256]{3,2,1,0:T(8,128)}, bf16[8,2,256,256]{3,2,1,0:T(8,128)(2,1)S(1)}, f32[1,256]{1,0:T(1,128)S(1)}, bf16[2,8,2,128,128]{4,3,2,1,0:T(8,128)(2,1)S(1)}) custom-call(s32[4]{0:T(128)S(1)} %pad_add_fusion.where, s32[2,4]{1,0:T(2,128)S(1)} %copy-done.21, f32[1,256]{1,0:T(1,128)S(1)} %get-tuple-element.578.gap, ...), custom_call_target="tpu_custom_call" | custom-call | flops 9395240960 | bytes 1153537 | tf_op jit(solution)/shard_map/gate_back/pallas_call | solution.py:640
  712.8 20.8 %all-to-all-done.4.states = bf16[4,8,128,128]{3,2,1,0:T(8,128)(2,1)S(1)} async-done(((bf16[4,8,128,128]{3,2,1,0:T(8,128)(2,1)}), bf16[4,8,128,128]{3,2,1,0:T(8,128)(2,1)S(1)}, u32[]{:S(2)}, u32[]{:S(2)}) %all-to-all-start.4) | async-done | bytes 1048608 | tf_op jit(solution)/shard_map/all_to_all | solution.py:1134
  747.9 19.2 %all-to-all-done.5 = bf16[4,8,128,128]{3,2,1,0:T(8,128)(2,1)S(1)} async-done(((bf16[4,8,128,128]{3,2,1,0:T(8,128)(2,1)}), bf16[4,8,128,128]{3,2,1,0:T(8,128)(2,1)S(1)}, u32[]{:S(2)}, u32[]{:S(2)}) %all-to-all-start.5) | async-done | bytes 1048608 | tf_op jit(solution)/shard_map/all_to_all | solution.py:1137
  773.6 39.7 %mix_backward.1 = (bf16[8,2,256,1024]{3,2,1,0:T(8,128)(2,1)}, f32[1,256]{1,0:T(1,128)S(1)}) custom-call(s32[4]{0:T(128)S(1)} %pad_add_fusion.where, s32[2,4]{1,0:T(2,128)S(1)} %copy-done.21, f32[1,256]{1,0:T(1,128)S(1)} %get-tuple-element.578.gap, f32[8,2,256,1024]{3,2,1,0:T(8,128)} %bitcast.248, f32[8,2,256,256]{3,2,1,0:T(8,128)} %get-tuple-element.366.grad_out, ...), custom_call_target="tpu_custom_call" | custom-call | flops 18522046464 | bytes 1415630 | tf_op jit(solution)/shard_map/mix_backward/pallas_call | solution.py:640
  828.4 24.2 %mix_in_grad.1 = bf16[2,2,4,256,512]{4,3,2,1,0:T(8,128)(2,1)} custom-call(bf16[512,2048]{1,0:T(8,128)(2,1)} %copy-done.6, bf16[512,2048]{1,0:T(8,128)(2,1)} %collective-permute-done.right.refs_1_, bf16[512,2048]{1,0:T(8,128)(2,1)} %collective-permute-done.1.left.refs_2_, bf16[512,2048]{1,0:T(8,128)(2,1)} %collective-permute-done.7.right.refs_3_, ...), custom_call_target="tpu_custom_call" | custom-call | flops 10307921920 | bytes 1572864 | tf_op jit(solution)/shard_map/mix_in_grad/pallas_call | solution.py:934
  863.2 9.1 project_back.4
  875.1 9.4 collective-permute-done.60
  894.5 9.8 project_back.5
  931.0 9.8 project_back.6
  945.6 8.4 project_back.7
  987.3 36.7 %all-to-all-done.8 = f32[8,4,256]{2,1,0:T(4,128)S(1)} async-done(((f32[8,4,256]{2,1,0:T(4,128)}), f32[8,4,256]{2,1,0:T(4,128)S(1)}, u32[]{:S(2)}, u32[]{:S(2)}) %all-to-all-start.8) | async-done | bytes 32800 | tf_op jit(solution)/shard_map/all_to_all | solution.py:1420
  (516 shorter events, 419.3 us)
Async XLA Ops:
  7.2 92.1 %all-gather.8.cloned.1.call-start = ((), (), s32[]{:S(2)}) async-start(), calls=%async_computation.15 | async-start | bytes 5242880 | tf_op jit(solution)/shard_map/all_gather | solution.py:1054
  12.4 260.2 %all-gather.10.cloned.1.call-start = ((), (), s32[]{:S(2)}) async-start(), calls=%async_computation.20 | async-start | bytes 3932160 | tf_op jit(solution)/shard_map/all_gather | solution.py:1054
  20.6 48.9 %collective-permute-start.1 = (bf16[512,2048]{1,0:T(8,128)(2,1)S(1)}, bf16[512,2048]{1,0:T(8,128)(2,1)}, u32[]{:S(2)}, u32[]{:S(2)}) collective-permute-start(bf16[512,2048]{1,0:T(8,128)(2,1)S(1)} %fusion.1.left.refs_0_), channel_id=1, source_target_pairs={{0,8},{4,12},{8,0},{12,4},{16,24},{20,28},{24,16},{28,20},{1,9},{5... | collective-permute-start | bytes 6291464 | tf_op jit(solution)/shard_map/ppermute | solution.py:959
  23.1 47.8 %collective-permute-start.2 = (bf16[512,2048]{1,0:T(8,128)(2,1)S(1)}, bf16[512,2048]{1,0:T(8,128)(2,1)}, u32[]{:S(2)}, u32[]{:S(2)}) collective-permute-start(bf16[512,2048]{1,0:T(8,128)(2,1)S(1)} %fusion.1.left.refs_0_), channel_id=1, source_target_pairs={{0,16},{4,20},{8,24},{12,28},{16,0},{20,4},{24,8},{28,12},{1,17},{... | collective-permute-start | bytes 6291464 | tf_op jit(solution)/shard_map/ppermute | solution.py:959
  99.3 173.3 %all-gather.12.cloned.1.call-start = ((), (), s32[]{:S(2)}) async-start(), calls=%async_computation.21 | async-start | bytes 3932160 | tf_op jit(solution)/shard_map/all_gather | solution.py:1054
  103.1 62.3 %collective-permute-start.12 = (bf16[512,2048]{1,0:T(8,128)(2,1)}, bf16[512,2048]{1,0:T(8,128)(2,1)}, u32[]{:S(2)}, u32[]{:S(2)}) collective-permute-start(bf16[512,2048]{1,0:T(8,128)(2,1)} %bitcast_convert_fusion.refs_2_.refs_8_), channel_id=1, source_target_pairs={{0,4},{4,0},{8,12},{12,8},{16,20},{20,16},{24,28},{28,24},{1,5},{5... | collective-permute-start | bytes 6291464 | tf_op jit(solution)/shard_map/ppermute | solution.py:959
  103.5 61.8 %collective-permute-start.13 = (bf16[512,2048]{1,0:T(8,128)(2,1)}, bf16[512,2048]{1,0:T(8,128)(2,1)}, u32[]{:S(2)}, u32[]{:S(2)}) collective-permute-start(bf16[512,2048]{1,0:T(8,128)(2,1)} %bitcast_convert_fusion.refs_2_.refs_8_), channel_id=1, source_target_pairs={{0,8},{4,12},{8,0},{12,4},{16,24},{20,28},{24,16},{28,20},{1,9},{5... | collective-permute-start | bytes 6291464 | tf_op jit(solution)/shard_map/ppermute | solution.py:959
  109.9 55.5 %collective-permute-start.14 = (bf16[512,2048]{1,0:T(8,128)(2,1)S(1)}, bf16[512,2048]{1,0:T(8,128)(2,1)}, u32[]{:S(2)}, u32[]{:S(2)}) collective-permute-start(bf16[512,2048]{1,0:T(8,128)(2,1)S(1)} %copy-done.54), channel_id=1, source_target_pairs={{0,16},{4,20},{8,24},{12,28},{16,0},{20,4},{24,8},{28,12},{1,17},{... | collective-permute-start | bytes 6291464 | tf_op jit(solution)/shard_map/ppermute | solution.py:959
  165.4 71.7 %collective-permute-start.20 = (bf16[512,2048]{1,0:T(8,128)(2,1)}, bf16[512,2048]{1,0:T(8,128)(2,1)}, u32[]{:S(2)}, u32[]{:S(2)}) collective-permute-start(bf16[512,2048]{1,0:T(8,128)(2,1)} %collective-permute-done.13.refs_2_.refs_10_), channel_id=1, source_target_pairs={{0,4},{4,0},{8,12},{12,8},{16,20},{20,16},{24,28},{28,24},{1,5},{5... | collective-permute-start | bytes 6291464 | tf_op jit(solution)/shard_map/ppermute | solution.py:959
  165.5 71.7 %collective-permute-start.21 = (bf16[512,2048]{1,0:T(8,128)(2,1)}, bf16[512,2048]{1,0:T(8,128)(2,1)}, u32[]{:S(2)}, u32[]{:S(2)}) collective-permute-start(bf16[512,2048]{1,0:T(8,128)(2,1)} %collective-permute-done.14.refs_2_.refs_12_), channel_id=1, source_target_pairs={{0,4},{4,0},{8,12},{12,8},{16,20},{20,16},{24,28},{28,24},{1,5},{5... | collective-permute-start | bytes 6291464 | tf_op jit(solution)/shard_map/ppermute | solution.py:959
  167.2 61.0 %all-to-all-start = ((bf16[4,8,136,128]{3,2,1,0:T(8,128)(2,1)}), bf16[4,8,136,128]{3,2,1,0:T(8,128)(2,1)S(1)}, u32[]{:S(2)}, u32[]{:S(2)}) async-start(bf16[4,8,136,128]{3,2,1,0:T(8,128)(2,1)} %bitcast.28), calls=%async_computation | async-start | bytes 2228224 | tf_op jit(solution)/shard_map/all_to_all | solution.py:1134
  174.9 62.2 %collective-permute-start.18 = (bf16[256,2048]{1,0:T(8,128)(2,1)S(1)}, bf16[256,2048]{1,0:T(8,128)(2,1)}, u32[]{:S(2)}, u32[]{:S(2)}) collective-permute-start(bf16[256,2048]{1,0:T(8,128)(2,1)S(1)} %slice.250), channel_id=1, source_target_pairs={{0,8},{4,12},{8,0},{12,4},{16,24},{20,28},{24,16},{28,20},{1,9},{5... | collective-permute-start | bytes 3145736 | tf_op jit(solution)/shard_map/ppermute | solution.py:959
  176.4 60.7 %collective-permute-start.19 = (bf16[256,2048]{1,0:T(8,128)(2,1)S(1)}, bf16[256,2048]{1,0:T(8,128)(2,1)}, u32[]{:S(2)}, u32[]{:S(2)}) collective-permute-start(bf16[256,2048]{1,0:T(8,128)(2,1)S(1)} %slice.251), channel_id=1, source_target_pairs={{0,16},{4,20},{8,24},{12,28},{16,0},{20,4},{24,8},{28,12},{1,17},{... | collective-permute-start | bytes 3145736 | tf_op jit(solution)/shard_map/ppermute | solution.py:959
  237.1 116.4 %all-gather.14.cloned.1.call-start = ((), (), s32[]{:S(2)}) async-start(), calls=%async_computation.22 | async-start | bytes 3932160 | tf_op jit(solution)/shard_map/all_gather | solution.py:1054
  309.8 48.8 %collective-permute-start.24 = (bf16[2,1024,384]{2,1,0:T(8,128)(2,1)}, bf16[2,1024,384]{2,1,0:T(8,128)(2,1)}, u32[]{:S(2)}, u32[]{:S(2)}) collective-permute-start(bf16[2,1024,384]{2,1,0:T(8,128)(2,1)} %dynamic-slice_bitcast_fusion.8), channel_id=1, source_target_pairs={{0,4},{4,0},{8,12},{12,8},{16,20},{20,16},{24,28},{28,24},{1,5},{5... | collective-permute-start | bytes 4718600 | tf_op jit(solution)/shard_map/ppermute | solution.py:959
  365.5 48.0 %collective-permute-start.15 = (bf16[512,2048]{1,0:T(8,128)(2,1)S(1)}, bf16[512,2048]{1,0:T(8,128)(2,1)}, u32[]{:S(2)}, u32[]{:S(2)}) collective-permute-start(bf16[512,2048]{1,0:T(8,128)(2,1)S(1)} %multiply_convert_fusion.refs_0_), channel_id=1, source_target_pairs={{0,8},{4,12},{8,0},{12,4},{16,24},{20,28},{24,16},{28,20},{1,9},{5... | collective-permute-start | bytes 6291464 | tf_op jit(solution)/shard_map/ppermute | solution.py:959
  366.1 47.7 %collective-permute-start.16 = (bf16[512,2048]{1,0:T(8,128)(2,1)S(1)}, bf16[512,2048]{1,0:T(8,128)(2,1)}, u32[]{:S(2)}, u32[]{:S(2)}) collective-permute-start(bf16[512,2048]{1,0:T(8,128)(2,1)S(1)} %multiply_convert_fusion.refs_0_), channel_id=1, source_target_pairs={{0,16},{4,20},{8,24},{12,28},{16,0},{20,4},{24,8},{28,12},{1,17},{... | collective-permute-start | bytes 6291464 | tf_op jit(solution)/shard_map/ppermute | solution.py:959
  413.8 44.0 %collective-permute-start.31 = (bf16[512,2048]{1,0:T(8,128)(2,1)}, bf16[512,2048]{1,0:T(8,128)(2,1)}, u32[]{:S(2)}, u32[]{:S(2)}) collective-permute-start(bf16[512,2048]{1,0:T(8,128)(2,1)} %collective-permute-done.16.refs_0_.refs_4_), channel_id=1, source_target_pairs={{0,4},{4,0},{8,12},{12,8},{16,20},{20,16},{24,28},{28,24},{1,5},{5... | collective-permute-start | bytes 6291464 | tf_op jit(solution)/shard_map/ppermute | solution.py:959
  536.4 45.0 %collective-permute-start.36 = (bf16[256,2048]{1,0:T(8,128)(2,1)}, bf16[256,2048]{1,0:T(8,128)(2,1)S(1)}, u32[]{:S(2)}, u32[]{:S(2)}) collective-permute-start(bf16[256,2048]{1,0:T(8,128)(2,1)} %slice.262), channel_id=1, source_target_pairs={{0,8},{4,12},{8,0},{12,4},{16,24},{20,28},{24,16},{28,20},{1,9},{5... | collective-permute-start | bytes 3145736 | tf_op jit(solution)/shard_map/ppermute | solution.py:959
  593.8 147.1 %collective-permute-start.52 = (bf16[2,4,2,256,384]{4,3,2,1,0:T(8,128)(2,1)}, bf16[2,4,2,256,384]{4,3,2,1,0:T(8,128)(2,1)}, u32[]{:S(2)}, u32[]{:S(2)}) collective-permute-start(bf16[2,4,2,256,384]{4,3,2,1,0:T(8,128)(2,1)} %dynamic-slice_bitcast_fusion.1), channel_id=1, source_target_pairs={{0,4},{4,0},{8,12},{12,8},{16,20},{20,16},{24,28},{28,24},{1,5},{5... | collective-permute-start | bytes 9437192 | tf_op jit(solution)/shard_map/ppermute | solution.py:959
  649.0 168.3 %reduce-scatter.5.cloned.1.call-start = ((), (), s32[]{:S(2)}) async-start(), calls=%async_computation.16 | async-start | bytes 3932160 | tf_op jit(solution)/shard_map/reduce_scatter | solution.py:1198
  740.8 163.5 %reduce-scatter.7.cloned.1.call-start = ((), (), s32[]{:S(2)}) async-start(), calls=%async_computation.17 | async-start | bytes 7864320 | tf_op jit(solution)/shard_map/reduce_scatter | solution.py:1198
  769.2 44.2 %collective-permute-start.55 = (bf16[256,2048]{1,0:T(8,128)(2,1)S(1)}, bf16[256,2048]{1,0:T(8,128)(2,1)}, u32[]{:S(2)}, u32[]{:S(2)}) collective-permute-start(bf16[256,2048]{1,0:T(8,128)(2,1)S(1)} %get-tuple-element.541), channel_id=1, source_target_pairs={{0,8},{4,12},{8,0},{12,4},{16,24},{20,28},{24,16},{28,20},{1,9},{5... | collective-permute-start | bytes 3145736 | tf_op jit(solution)/shard_map/ppermute | solution.py:959
  773.0 44.3 %collective-permute-start.54 = (bf16[256,2048]{1,0:T(8,128)(2,1)S(1)}, bf16[256,2048]{1,0:T(8,128)(2,1)}, u32[]{:S(2)}, u32[]{:S(2)}) collective-permute-start(bf16[256,2048]{1,0:T(8,128)(2,1)S(1)} %slice.271), channel_id=1, source_target_pairs={{0,16},{4,20},{8,24},{12,28},{16,0},{20,4},{24,8},{28,12},{1,17},{... | collective-permute-start | bytes 3145736 | tf_op jit(solution)/shard_map/ppermute | solution.py:959
  828.4 212.7 %reduce-scatter.9.cloned.1.call-start = ((), (), s32[]{:S(2)}) async-start(), calls=%async_computation.18 | async-start | bytes 5242880 | tf_op jit(solution)/shard_map/reduce_scatter | solution.py:1198
  961.6 66.2 %collective-permute-start.68 = (bf16[256,2048]{1,0:T(8,128)(2,1)}, bf16[256,2048]{1,0:T(8,128)(2,1)S(1)}, u32[]{:S(2)}, u32[]{:S(2)}) collective-permute-start(bf16[256,2048]{1,0:T(8,128)(2,1)} %slice.330), channel_id=1, source_target_pairs={{0,8},{4,12},{8,0},{12,4},{16,24},{20,28},{24,16},{28,20},{1,9},{5... | collective-permute-start | bytes 3145736 | tf_op jit(solution)/shard_map/ppermute | solution.py:959
  965.7 58.4 %collective-permute-start.75 = (bf16[512,2048]{1,0:T(8,128)(2,1)}, bf16[512,2048]{1,0:T(8,128)(2,1)}, u32[]{:S(2)}, u32[]{:S(2)}) collective-permute-start(bf16[512,2048]{1,0:T(8,128)(2,1)} %copy-done.19), channel_id=1, source_target_pairs={{0,4},{4,0},{8,12},{12,8},{16,20},{20,16},{24,28},{28,24},{1,5},{5... | collective-permute-start | bytes 6291464 | tf_op jit(solution)/shard_map/ppermute | solution.py:959
  968.6 59.2 %collective-permute-start.74 = (bf16[256,2048]{1,0:T(8,128)(2,1)}, bf16[256,2048]{1,0:T(8,128)(2,1)}, u32[]{:S(2)}, u32[]{:S(2)}) collective-permute-start(bf16[256,2048]{1,0:T(8,128)(2,1)} %add_convert_fusion.12), channel_id=1, source_target_pairs={{0,8},{4,12},{8,0},{12,4},{16,24},{20,28},{24,16},{28,20},{1,9},{5... | collective-permute-start | bytes 3145736 | tf_op jit(solution)/shard_map/ppermute | solution.py:959
  975.6 52.2 %collective-permute-start.73 = (bf16[256,2048]{1,0:T(8,128)(2,1)}, bf16[256,2048]{1,0:T(8,128)(2,1)}, u32[]{:S(2)}, u32[]{:S(2)}) collective-permute-start(bf16[256,2048]{1,0:T(8,128)(2,1)} %add_convert_fusion.13), channel_id=1, source_target_pairs={{0,16},{4,20},{8,24},{12,28},{16,0},{20,4},{24,8},{28,12},{1,17},{... | collective-permute-start | bytes 3145736 | tf_op jit(solution)/shard_map/ppermute | solution.py:959
  976.5 51.3 %collective-permute-start.72 = (bf16[256,2048]{1,0:T(8,128)(2,1)}, bf16[256,2048]{1,0:T(8,128)(2,1)}, u32[]{:S(2)}, u32[]{:S(2)}) collective-permute-start(bf16[256,2048]{1,0:T(8,128)(2,1)} %slice.333), channel_id=1, source_target_pairs={{0,16},{4,20},{8,24},{12,28},{16,0},{20,4},{24,8},{28,12},{1,17},{... | collective-permute-start | bytes 3145736 | tf_op jit(solution)/shard_map/ppermute | solution.py:959
  979.8 44.1 %all-to-all-start.8 = ((f32[8,4,256]{2,1,0:T(4,128)}), f32[8,4,256]{2,1,0:T(4,128)S(1)}, u32[]{:S(2)}, u32[]{:S(2)}) async-start(f32[8,4,256]{2,1,0:T(4,128)} %copy.125), calls=%async_computation.10 | async-start | bytes 65536 | tf_op jit(solution)/shard_map/all_to_all | solution.py:1420
  983.2 71.6 %reduce-scatter.11.cloned.1.call-start = ((), (), s32[]{:S(2)}) async-start(), calls=%async_computation.19 | async-start | bytes 1310720 | tf_op jit(solution)/shard_map/reduce_scatter | solution.py:1415
  (139 other events, 2086.6 us)
Sparse Core Ops, SparseCore 0:
  12.5 83.5 all-gather.7
  99.4 64.8 all-gather.9
  166.5 105.2 all-gather.11
  275.5 62.0 all-gather.13
  651.9 59.9 reduce-scatter.4
  767.3 109.6 reduce-scatter.6
  904.5 74.7 reduce-scatter.8
  987.4 25.8 reduce-scatter.10

commit v4 on v3

--- a/solution.py
+++ b/solution.py
@@ -1397,7 +1397,6 @@
     chip_in[2] = add_low(in_parts[2], other)
     mine_x = swap(chip_in[2][:half], XLINK)
     other = from_core(4)
-    norm1_part = norm1_part + back(0)
     def set_heads(part):
         row = jnp.zeros((2, 2, chips, head_size), F32)
         mine = part.reshape(1, 2, 1, head_size)
@@ -1405,21 +1404,24 @@
         row = row.reshape(mp_count, all_heads // mp_count, seq_count, head_size // seq_count)
         return jnp.transpose(row, (2, 0, 1, 3)).reshape(-1)
 
-    gains = jnp.stack(
-        [norm1_part[0] / norm1_gain, norm2_part, set_heads(gap_part), set_heads(group_part)]
-    )
-    gains = jnp.transpose(gains.reshape(4, seq_count, width // seq_count), (1, 0, 2))
-    far_hops, other, in_parts, chip_in, gu_round, gains, out_grad = together(
-        far_hops, other, in_parts, chip_in, handed(gu_grad), gains, out_grad
+    grad_projected, far_hops, other, in_parts, chip_in, gu_round, out_grad = together(
+        grad_projected, far_hops, other, in_parts, chip_in, handed(gu_grad), out_grad
     )
     out_grad = lax.psum_scatter(out_grad, "mp", scatter_dimension=0, tiled=True)[0]
     chip_in[4] = add_low(in_parts[4], other)
     hops = mine_x, swap(chip_in[4][half:], YLINK)
     lasts = last_hops(turned(chip_in, (None, None) + far_hops))
+    norm1_part = norm1_part + back(0)
+    gains = jnp.stack(
+        [norm1_part[0] / norm1_gain, norm2_part, set_heads(gap_part), set_heads(group_part)]
+    )
+    gains = jnp.transpose(gains.reshape(4, seq_count, width // seq_count), (1, 0, 2))
+    hops, lasts, chip_in, in_parts, layer_out, gains = together(
+        hops, lasts, chip_in, in_parts, layer_out, gains
+    )
     chip_in[0] = chip_sum(in_parts, 0)
     gains = jnp.sum(lax.all_to_all(gains, "seq", split_axis=0, concat_axis=0, tiled=True), axis=0)
     gains = jnp.transpose(gains.reshape(4, mp_count, -1), (1, 0, 2))
-    hops, lasts, chip_in, layer_out, gains = together(hops, lasts, chip_in, layer_out, gains)
     gains = jnp.sum(lax.all_to_all(gains, "mp", split_axis=0, concat_axis=0, tiled=True), axis=0)
     grad_normed = arrived(chip_in, hops, lasts)
     got = [gu_round[c].astype(F32) for c in range(chips)]

time: 1080 us -> 1110 us (1.028)
  waiting for transfers between devices: 284 us -> 315 us
    ppermute x74, waiting for transfers between devices: 91.4 us -> 144 us  [swap(): lax.ppermute(value, 'seq', [(i, i ^ across) for i in range(lax.axis_size(...]
    all_to_all x1, waiting for transfers between devices: 36.7 us -> 2.53 us  [plane_device(): lax.all_to_all(gains, 'seq', split_axis=0, concat_axis=0, tiled=True)]
    unnamed x171 -> x173, local copies, waits for them, and re-layouts: 50.3 us -> 48.2 us
  transfers between devices with their start and end apart: 95 -> 95, of which waited for: 28 -> 35; matrix products, arithmetic and copies ran while one was open for 23% -> 22% of each run, Pallas kernels for 36% -> 35%
where the time goes in v4:
time: 1110 us; the launch traced here: 1100 us
  Pallas kernels  381 us (34%)
  waiting for transfers between devices  315 us (28%)
  local copies, waits for them, and re-layouts  141 us (13%)
  other arithmetic  134 us (12%)
  starting transfers between devices  97.4 us (9%)
  between operations  16.3 us (1%)
  matrix products  11.9 us (1%)
    ppermute x74, waiting for transfers between devices, swap(): lax.ppermute(value, 'seq', [(i, i ^ across) for i in range(lax.axis_size(...  144 us
    pallas_call x4, Pallas kernels, feed_call(): pl.pallas_call(feed_kernel, grid=(rows // tile,), in_specs=[cut(width)] *...  115 us
    pallas_call x4, Pallas kernels, recur_call(): pl.pallas_call(kernel, grid_spec=pltpu.PrefetchScalarGridSpec(num_scalar_...  102 us
    pallas_call x3, Pallas kernels, outer_call(): pl.pallas_call(functools.partial(outer_kernel, count, place), grid=(count...  77 us
    all_to_all x2, waiting for transfers between devices, to_scan(): return lax.all_to_all(array, 'mp', split_axis=0, concat_axis=0, tiled=True)  72.1 us
    convert_element_type x21, other arithmetic, add_low(): return (a.astype(F32) + b.astype(F32)).astype(BF16)  59.6 us
    ppermute x74, starting transfers between devices, swap(): lax.ppermute(value, 'seq', [(i, i ^ across) for i in range(lax.axis_size(...  49.5 us
    all_to_all x2, waiting for transfers between devices, from_scan(): array = lax.all_to_all(array, 'mp', split_axis=0, concat_axis=0, tiled=True)  48.5 us
  transfers between devices with their start and end apart: 95, of which 35 were waited for; matrix products, arithmetic and copies ran while one was open for 22% of the time, Pallas kernels for 35%

profile of v4, /device:TPU:0, one launch (start us, length us, event | category | flops | bytes accessed | tf_op | source)
XLA Modules:
  0.0 1097.3 jit_solution(12770255756456520507)
XLA Ops:
  31.3 9.1 constant_dynamic-slice_fusion.4
  43.8 25.7 %collective-permute-done.1.left.refs_2_ = bf16[512,2048]{1,0:T(8,128)(2,1)} collective-permute-done((bf16[512,2048]{1,0:T(8,128)(2,1)S(1)}, bf16[512,2048]{1,0:T(8,128)(2,1)}, u32[]{:S(2)}, u32[]{:S(2)}) %collective-permute-start.1) | collective-permute-done | bytes 2097184 | tf_op jit(solution)/shard_map/ppermute | solution.py:959
  86.6 12.6 %collective-permute-done.5 = bf16[256,2048]{1,0:T(8,128)(2,1)} collective-permute-done((bf16[256,2048]{1,0:T(8,128)(2,1)S(1)}, bf16[256,2048]{1,0:T(8,128)(2,1)}, u32[]{:S(2)}, u32[]{:S(2)}) %collective-permute-start.5) | collective-permute-done | bytes 1048608 | tf_op jit(solution)/shard_map/ppermute | solution.py:959
  118.4 9.0 project.4.rest_0_
  149.5 16.2 %run_states.1 = f32[2,8,2,136,128]{4,3,2,1,0:T(8,128)S(1)} custom-call(s32[4]{0:T(128)S(1)} %pad_add_fusion.where, s32[2,4]{1,0:T(2,128)S(1)} %copy-done.19, f32[1,256]{1,0:T(1,128)S(1)} %get-tuple-element.576.gap, f32[8,2,256,1024]{3,2,1,0:T(8,128)} %bitcast.245), custom_call_target="tpu_custom_call" | custom-call | flops 7247757312 | bytes 838913 | tf_op jit(solution)/shard_map/run_states/pallas_call | solution.py:640
  177.3 51.3 %all-to-all-done.decays.states = bf16[4,8,136,128]{3,2,1,0:T(8,128)(2,1)S(1)} async-done(((bf16[4,8,136,128]{3,2,1,0:T(8,128)(2,1)}), bf16[4,8,136,128]{3,2,1,0:T(8,128)(2,1)S(1)}, u32[]{:S(2)}, u32[]{:S(2)}) %all-to-all-start) | async-done | bytes 1114144 | tf_op jit(solution)/shard_map/all_to_all | solution.py:1134
  243.6 29.2 %all-to-all-done.1 = bf16[4,8,128,128]{3,2,1,0:T(8,128)(2,1)S(1)} async-done(((bf16[4,8,128,128]{3,2,1,0:T(8,128)(2,1)}), bf16[4,8,128,128]{3,2,1,0:T(8,128)(2,1)S(1)}, u32[]{:S(2)}, u32[]{:S(2)}) %all-to-all-start.1) | async-done | bytes 1048608 | tf_op jit(solution)/shard_map/all_to_all | solution.py:1137
  275.7 26.2 %mix_forward.1 = (bf16[8,2,256,256]{3,2,1,0:T(8,128)(2,1)S(1)}, f32[8,2,256,256]{3,2,1,0:T(8,128)}, f32[16,2,2,128,128]{4,3,2,1,0:T(8,128)}) custom-call(s32[4]{0:T(128)S(1)} %pad_add_fusion.where, s32[2,4]{1,0:T(2,128)S(1)} %copy-done.19, f32[1,256]{1,0:T(1,128)S(1)} %get-tuple-element.576.gap, f32[1,256]{1,0:T(1,128)S(1)} %get-tuple-element.575.gain, ...), custom_call_target="tpu_custom_call" | custom-call | flops 12079595520 | bytes 891393 | tf_op jit(solution)/shard_map/mix_forward/pallas_call | solution.py:640
  313.7 19.9 %all-to-all-done.2.heads = bf16[8,512,256]{2,1,0:T(8,128)(2,1)S(1)} async-done(((bf16[8,512,256]{2,1,0:T(8,128)(2,1)}), bf16[8,512,256]{2,1,0:T(8,128)(2,1)S(1)}, u32[]{:S(2)}, u32[]{:S(2)}) %all-to-all-start.2) | async-done | bytes 2097184 | tf_op jit(solution)/shard_map/all_to_all | solution.py:1182
  341.7 11.9 %multiply_reduce_fusion.2 = (f32[512]{0:T(512)S(1)}, f32[512,2048]{1,0:T(8,128)}) fusion(bf16[512,2048]{0,1:T(8,128)(2,1)} %bitcast.257, bf16[2048,2048]{1,0:T(8,128)(2,1)} %bitcast.232, f32[256,2,2048]{2,0,1:T(8,128)} %copy-done.25), kind=kOutput, calls=%fused_computation.36 | convolution fusion | flops 4298112512 | bytes 18876416 | tf_op jit(solution)/shard_map/dot_general | solution.py:364
  370.8 29.0 %feed.4 = (bf16[512,768]{1,0:T(8,128)(2,1)}, bf16[512,1536]{1,0:T(8,128)(2,1)}, bf16[512,2048]{1,0:T(8,128)(2,1)}, bf16[512,2048]{1,0:T(8,128)(2,1)}, bf16[512,7...) custom-call(bf16[512,2048]{1,0:T(8,128)(2,1)} %copy-done.57, ...), custom_call_target="tpu_custom_call" | custom-call | flops 11596411904 | bytes 1048576 | tf_op jit(solution)/shard_map/feed/pallas_call | solution.py:805
  399.7 14.0 %collective-permute-done.15.refs_0_.refs_2_ = bf16[512,2048]{1,0:T(8,128)(2,1)} collective-permute-done((bf16[512,2048]{1,0:T(8,128)(2,1)S(1)}, bf16[512,2048]{1,0:T(8,128)(2,1)}, u32[]{:S(2)}, u32[]{:S(2)}) %collective-permute-start.15) | collective-permute-done | bytes 2097184 | tf_op jit(solution)/shard_map/ppermute | solution.py:959
  422.2 29.0 %feed.5 = (bf16[512,768]{1,0:T(8,128)(2,1)}, bf16[512,1536]{1,0:T(8,128)(2,1)}, bf16[512,2048]{1,0:T(8,128)(2,1)}, bf16[512,2048]{1,0:T(8,128)(2,1)}, bf16[512,7...) custom-call(bf16[512,2048]{1,0:T(8,128)(2,1)} %collective-permute-done.15.ref, ...), custom_call_target="tpu_custom_call" | custom-call | flops 11596411904 | bytes 1048576 | tf_op jit(solution)/shard_map/feed/pallas_call | solution.py:805
  458.1 28.7 %feed.6 = (bf16[512,768]{1,0:T(8,128)(2,1)}, bf16[512,1536]{1,0:T(8,128)(2,1)}, bf16[512,2048]{1,0:T(8,128)(2,1)}, bf16[512,2048]{1,0:T(8,128)(2,1)}, bf16[512,7...) custom-call(bf16[512,2048]{1,0:T(8,128)(2,1)} %collective-permute-done.16.ref, ...), custom_call_target="tpu_custom_call" | custom-call | flops 11596411904 | bytes 1048576 | tf_op jit(solution)/shard_map/feed/pallas_call | solution.py:805
  497.7 28.8 %feed.7 = (bf16[512,768]{1,0:T(8,128)(2,1)}, bf16[512,1536]{1,0:T(8,128)(2,1)}, bf16[512,2048]{1,0:T(8,128)(2,1)}, bf16[512,2048]{1,0:T(8,128)(2,1)}, bf16[512,7...) custom-call(bf16[512,2048]{1,0:T(8,128)(2,1)} %copy-done.63, ...), custom_call_target="tpu_custom_call" | custom-call | flops 11596411904 | bytes 1048576 | tf_op jit(solution)/shard_map/feed/pallas_call | solution.py:805
  541.9 33.9 %gate_up_grad.1 = bf16[2,2,4,2,256,384]{5,4,3,2,1,0:T(8,128)(2,1)} custom-call(bf16[512,2048]{1,0:T(8,128)(2,1)} %copy-done.57, bf16[512,2048]{1,0:T(8,128)(2,1)} %copy-done.73, bf16[512,2048]{1,0:T(8,128)(2,1)} %collective-permute-done.15.refs_0_.refs_2_, bf16[512,2048]{1,0:T(8,128)(2,1)} %copy-done.74, ...), custom_call_target="tpu_custom_call" | custom-call | flops 15461881856 | bytes 1835008 | tf_op jit(solution)/shard_map/gate_up_grad/pallas_call | solution.py:934
  594.0 19.0 %down_grad.1 = bf16[2,2,4,384,256]{4,3,2,1,0:T(8,128)(2,1)} custom-call(bf16[512,768]{1,0:T(8,128)(2,1)} %get-tuple-element.334.refs_0_, bf16[512,768]{1,0:T(8,128)(2,1)} %get-tuple-element.335.refs_1_, bf16[512,768]{1,0:T(8,128)(2,1)} %get-tuple-element.336.refs_2_, bf16[512,768]{1,0:T(8,128)(2,1)} %get-tuple-element.337.refs_3_, ...), custom_call_target="tpu_custom_call" | custom-call | flops 7730940928 | bytes 1441792 | tf_op jit(solution)/shard_map/down_grad/pallas_call | solution.py:934
  665.6 9.9 all-to-all-done.3
  680.5 20.0 %gate_back.1 = (f32[8,2,256,256]{3,2,1,0:T(8,128)}, bf16[8,2,256,256]{3,2,1,0:T(8,128)(2,1)S(1)}, f32[1,256]{1,0:T(1,128)S(1)}, bf16[2,8,2,128,128]{4,3,2,1,0:T(8,128)(2,1)S(1)}) custom-call(s32[4]{0:T(128)S(1)} %pad_add_fusion.where, s32[2,4]{1,0:T(2,128)S(1)} %copy-done.20, f32[1,256]{1,0:T(1,128)S(1)} %get-tuple-element.576.gap, ...), custom_call_target="tpu_custom_call" | custom-call | flops 9395240960 | bytes 1153537 | tf_op jit(solution)/shard_map/gate_back/pallas_call | solution.py:640
  712.7 20.8 %all-to-all-done.4.states = bf16[4,8,128,128]{3,2,1,0:T(8,128)(2,1)S(1)} async-done(((bf16[4,8,128,128]{3,2,1,0:T(8,128)(2,1)}), bf16[4,8,128,128]{3,2,1,0:T(8,128)(2,1)S(1)}, u32[]{:S(2)}, u32[]{:S(2)}) %all-to-all-start.4) | async-done | bytes 1048608 | tf_op jit(solution)/shard_map/all_to_all | solution.py:1134
  747.7 19.3 %all-to-all-done.5 = bf16[4,8,128,128]{3,2,1,0:T(8,128)(2,1)S(1)} async-done(((bf16[4,8,128,128]{3,2,1,0:T(8,128)(2,1)}), bf16[4,8,128,128]{3,2,1,0:T(8,128)(2,1)S(1)}, u32[]{:S(2)}, u32[]{:S(2)}) %all-to-all-start.5) | async-done | bytes 1048608 | tf_op jit(solution)/shard_map/all_to_all | solution.py:1137
  773.6 39.7 %mix_backward.1 = (bf16[8,2,256,1024]{3,2,1,0:T(8,128)(2,1)}, f32[1,256]{1,0:T(1,128)S(1)}) custom-call(s32[4]{0:T(128)S(1)} %pad_add_fusion.where, s32[2,4]{1,0:T(2,128)S(1)} %copy-done.20, f32[1,256]{1,0:T(1,128)S(1)} %get-tuple-element.576.gap, f32[8,2,256,1024]{3,2,1,0:T(8,128)} %bitcast.248, f32[8,2,256,256]{3,2,1,0:T(8,128)} %get-tuple-element.365.grad_out, ...), custom_call_target="tpu_custom_call" | custom-call | flops 18522046464 | bytes 1415630 | tf_op jit(solution)/shard_map/mix_backward/pallas_call | solution.py:640
  828.8 24.0 %mix_in_grad.1 = bf16[2,2,4,256,512]{4,3,2,1,0:T(8,128)(2,1)} custom-call(bf16[512,2048]{1,0:T(8,128)(2,1)} %copy-done.6, bf16[512,2048]{1,0:T(8,128)(2,1)} %collective-permute-done.right.refs_1_, bf16[512,2048]{1,0:T(8,128)(2,1)} %collective-permute-done.1.left.refs_2_, bf16[512,2048]{1,0:T(8,128)(2,1)} %collective-permute-done.7.right.refs_3_, ...), custom_call_target="tpu_custom_call" | custom-call | flops 10307921920 | bytes 1572864 | tf_op jit(solution)/shard_map/mix_in_grad/pallas_call | solution.py:934
  862.5 8.1 project_back.4
  874.4 9.4 collective-permute-done.60
  893.8 8.8 project_back.5
  908.2 10.0 project_back.6
  935.5 13.6 %collective-permute-done.69 = bf16[256,2048]{1,0:T(8,128)(2,1)} collective-permute-done((bf16[256,2048]{1,0:T(8,128)(2,1)}, bf16[256,2048]{1,0:T(8,128)(2,1)}, u32[]{:S(2)}, u32[]{:S(2)}) %collective-permute-start.69) | collective-permute-done | bytes 1048608 | tf_op jit(solution)/shard_map/ppermute | solution.py:959
  949.1 9.6 collective-permute-done.70
  992.6 8.5 project_back.7
  1002.5 17.8 %collective-permute-done.74 = bf16[256,2048]{1,0:T(8,128)(2,1)} collective-permute-done((bf16[256,2048]{1,0:T(8,128)(2,1)}, bf16[256,2048]{1,0:T(8,128)(2,1)}, u32[]{:S(2)}, u32[]{:S(2)}) %collective-permute-start.74) | collective-permute-done | bytes 1048608 | tf_op jit(solution)/shard_map/ppermute | solution.py:959
  1020.4 10.7 collective-permute-done.72
  (518 shorter events, 457.1 us)
Async XLA Ops:
  7.2 92.1 %all-gather.8.cloned.1.call-start = ((), (), s32[]{:S(2)}) async-start(), calls=%async_computation.15 | async-start | bytes 5242880 | tf_op jit(solution)/shard_map/all_gather | solution.py:1054
  12.4 260.5 %all-gather.10.cloned.1.call-start = ((), (), s32[]{:S(2)}) async-start(), calls=%async_computation.20 | async-start | bytes 3932160 | tf_op jit(solution)/shard_map/all_gather | solution.py:1054
  20.6 48.9 %collective-permute-start.1 = (bf16[512,2048]{1,0:T(8,128)(2,1)S(1)}, bf16[512,2048]{1,0:T(8,128)(2,1)}, u32[]{:S(2)}, u32[]{:S(2)}) collective-permute-start(bf16[512,2048]{1,0:T(8,128)(2,1)S(1)} %fusion.1.left.refs_0_), channel_id=1, source_target_pairs={{0,8},{4,12},{8,0},{12,4},{16,24},{20,28},{24,16},{28,20},{1,9},{5... | collective-permute-start | bytes 6291464 | tf_op jit(solution)/shard_map/ppermute | solution.py:959
  23.1 47.8 %collective-permute-start.2 = (bf16[512,2048]{1,0:T(8,128)(2,1)S(1)}, bf16[512,2048]{1,0:T(8,128)(2,1)}, u32[]{:S(2)}, u32[]{:S(2)}) collective-permute-start(bf16[512,2048]{1,0:T(8,128)(2,1)S(1)} %fusion.1.left.refs_0_), channel_id=1, source_target_pairs={{0,16},{4,20},{8,24},{12,28},{16,0},{20,4},{24,8},{28,12},{1,17},{... | collective-permute-start | bytes 6291464 | tf_op jit(solution)/shard_map/ppermute | solution.py:959
  99.3 173.6 %all-gather.12.cloned.1.call-start = ((), (), s32[]{:S(2)}) async-start(), calls=%async_computation.21 | async-start | bytes 3932160 | tf_op jit(solution)/shard_map/all_gather | solution.py:1054
  103.1 62.6 %collective-permute-start.12 = (bf16[512,2048]{1,0:T(8,128)(2,1)}, bf16[512,2048]{1,0:T(8,128)(2,1)}, u32[]{:S(2)}, u32[]{:S(2)}) collective-permute-start(bf16[512,2048]{1,0:T(8,128)(2,1)} %bitcast_convert_fusion.refs_2_.refs_8_), channel_id=1, source_target_pairs={{0,4},{4,0},{8,12},{12,8},{16,20},{20,16},{24,28},{28,24},{1,5},{5... | collective-permute-start | bytes 6291464 | tf_op jit(solution)/shard_map/ppermute | solution.py:959
  103.5 62.2 %collective-permute-start.13 = (bf16[512,2048]{1,0:T(8,128)(2,1)}, bf16[512,2048]{1,0:T(8,128)(2,1)}, u32[]{:S(2)}, u32[]{:S(2)}) collective-permute-start(bf16[512,2048]{1,0:T(8,128)(2,1)} %bitcast_convert_fusion.refs_2_.refs_8_), channel_id=1, source_target_pairs={{0,8},{4,12},{8,0},{12,4},{16,24},{20,28},{24,16},{28,20},{1,9},{5... | collective-permute-start | bytes 6291464 | tf_op jit(solution)/shard_map/ppermute | solution.py:959
  109.9 55.8 %collective-permute-start.14 = (bf16[512,2048]{1,0:T(8,128)(2,1)S(1)}, bf16[512,2048]{1,0:T(8,128)(2,1)}, u32[]{:S(2)}, u32[]{:S(2)}) collective-permute-start(bf16[512,2048]{1,0:T(8,128)(2,1)S(1)} %copy-done.53), channel_id=1, source_target_pairs={{0,16},{4,20},{8,24},{12,28},{16,0},{20,4},{24,8},{28,12},{1,17},{... | collective-permute-start | bytes 6291464 | tf_op jit(solution)/shard_map/ppermute | solution.py:959
  165.7 71.8 %collective-permute-start.20 = (bf16[512,2048]{1,0:T(8,128)(2,1)}, bf16[512,2048]{1,0:T(8,128)(2,1)}, u32[]{:S(2)}, u32[]{:S(2)}) collective-permute-start(bf16[512,2048]{1,0:T(8,128)(2,1)} %collective-permute-done.13.refs_2_.refs_10_), channel_id=1, source_target_pairs={{0,4},{4,0},{8,12},{12,8},{16,20},{20,16},{24,28},{28,24},{1,5},{5... | collective-permute-start | bytes 6291464 | tf_op jit(solution)/shard_map/ppermute | solution.py:959
  165.8 71.8 %collective-permute-start.21 = (bf16[512,2048]{1,0:T(8,128)(2,1)}, bf16[512,2048]{1,0:T(8,128)(2,1)}, u32[]{:S(2)}, u32[]{:S(2)}) collective-permute-start(bf16[512,2048]{1,0:T(8,128)(2,1)} %collective-permute-done.14.refs_2_.refs_12_), channel_id=1, source_target_pairs={{0,4},{4,0},{8,12},{12,8},{16,20},{20,16},{24,28},{28,24},{1,5},{5... | collective-permute-start | bytes 6291464 | tf_op jit(solution)/shard_map/ppermute | solution.py:959
  167.5 61.0 %all-to-all-start = ((bf16[4,8,136,128]{3,2,1,0:T(8,128)(2,1)}), bf16[4,8,136,128]{3,2,1,0:T(8,128)(2,1)S(1)}, u32[]{:S(2)}, u32[]{:S(2)}) async-start(bf16[4,8,136,128]{3,2,1,0:T(8,128)(2,1)} %bitcast.28), calls=%async_computation | async-start | bytes 2228224 | tf_op jit(solution)/shard_map/all_to_all | solution.py:1134
  175.2 62.3 %collective-permute-start.18 = (bf16[256,2048]{1,0:T(8,128)(2,1)S(1)}, bf16[256,2048]{1,0:T(8,128)(2,1)}, u32[]{:S(2)}, u32[]{:S(2)}) collective-permute-start(bf16[256,2048]{1,0:T(8,128)(2,1)S(1)} %slice.250), channel_id=1, source_target_pairs={{0,8},{4,12},{8,0},{12,4},{16,24},{20,28},{24,16},{28,20},{1,9},{5... | collective-permute-start | bytes 3145736 | tf_op jit(solution)/shard_map/ppermute | solution.py:959
  176.8 60.7 %collective-permute-start.19 = (bf16[256,2048]{1,0:T(8,128)(2,1)S(1)}, bf16[256,2048]{1,0:T(8,128)(2,1)}, u32[]{:S(2)}, u32[]{:S(2)}) collective-permute-start(bf16[256,2048]{1,0:T(8,128)(2,1)S(1)} %slice.251), channel_id=1, source_target_pairs={{0,16},{4,20},{8,24},{12,28},{16,0},{20,4},{24,8},{28,12},{1,17},{... | collective-permute-start | bytes 3145736 | tf_op jit(solution)/shard_map/ppermute | solution.py:959
  237.5 116.1 %all-gather.14.cloned.1.call-start = ((), (), s32[]{:S(2)}) async-start(), calls=%async_computation.22 | async-start | bytes 3932160 | tf_op jit(solution)/shard_map/all_gather | solution.py:1054
  309.9 48.8 %collective-permute-start.24 = (bf16[2,1024,384]{2,1,0:T(8,128)(2,1)}, bf16[2,1024,384]{2,1,0:T(8,128)(2,1)}, u32[]{:S(2)}, u32[]{:S(2)}) collective-permute-start(bf16[2,1024,384]{2,1,0:T(8,128)(2,1)} %dynamic-slice_bitcast_fusion.8), channel_id=1, source_target_pairs={{0,4},{4,0},{8,12},{12,8},{16,20},{20,16},{24,28},{28,24},{1,5},{5... | collective-permute-start | bytes 4718600 | tf_op jit(solution)/shard_map/ppermute | solution.py:959
  365.7 48.0 %collective-permute-start.15 = (bf16[512,2048]{1,0:T(8,128)(2,1)S(1)}, bf16[512,2048]{1,0:T(8,128)(2,1)}, u32[]{:S(2)}, u32[]{:S(2)}) collective-permute-start(bf16[512,2048]{1,0:T(8,128)(2,1)S(1)} %multiply_convert_fusion.refs_0_), channel_id=1, source_target_pairs={{0,8},{4,12},{8,0},{12,4},{16,24},{20,28},{24,16},{28,20},{1,9},{5... | collective-permute-start | bytes 6291464 | tf_op jit(solution)/shard_map/ppermute | solution.py:959
  366.2 47.7 %collective-permute-start.16 = (bf16[512,2048]{1,0:T(8,128)(2,1)S(1)}, bf16[512,2048]{1,0:T(8,128)(2,1)}, u32[]{:S(2)}, u32[]{:S(2)}) collective-permute-start(bf16[512,2048]{1,0:T(8,128)(2,1)S(1)} %multiply_convert_fusion.refs_0_), channel_id=1, source_target_pairs={{0,16},{4,20},{8,24},{12,28},{16,0},{20,4},{24,8},{28,12},{1,17},{... | collective-permute-start | bytes 6291464 | tf_op jit(solution)/shard_map/ppermute | solution.py:959
  413.9 44.2 %collective-permute-start.31 = (bf16[512,2048]{1,0:T(8,128)(2,1)}, bf16[512,2048]{1,0:T(8,128)(2,1)}, u32[]{:S(2)}, u32[]{:S(2)}) collective-permute-start(bf16[512,2048]{1,0:T(8,128)(2,1)} %collective-permute-done.16.refs_0_.refs_4_), channel_id=1, source_target_pairs={{0,4},{4,0},{8,12},{12,8},{16,20},{20,16},{24,28},{28,24},{1,5},{5... | collective-permute-start | bytes 6291464 | tf_op jit(solution)/shard_map/ppermute | solution.py:959
  536.6 45.0 %collective-permute-start.36 = (bf16[256,2048]{1,0:T(8,128)(2,1)}, bf16[256,2048]{1,0:T(8,128)(2,1)S(1)}, u32[]{:S(2)}, u32[]{:S(2)}) collective-permute-start(bf16[256,2048]{1,0:T(8,128)(2,1)} %slice.262), channel_id=1, source_target_pairs={{0,8},{4,12},{8,0},{12,4},{16,24},{20,28},{24,16},{28,20},{1,9},{5... | collective-permute-start | bytes 3145736 | tf_op jit(solution)/shard_map/ppermute | solution.py:959
  539.2 42.8 %collective-permute-start.37 = (bf16[256,2048]{1,0:T(8,128)(2,1)}, bf16[256,2048]{1,0:T(8,128)(2,1)}, u32[]{:S(2)}, u32[]{:S(2)}) collective-permute-start(bf16[256,2048]{1,0:T(8,128)(2,1)} %slice.263), channel_id=1, source_target_pairs={{0,16},{4,20},{8,24},{12,28},{16,0},{20,4},{24,8},{28,12},{1,17},{... | collective-permute-start | bytes 3145736 | tf_op jit(solution)/shard_map/ppermute | solution.py:959
  594.0 146.9 %collective-permute-start.52 = (bf16[2,4,2,256,384]{4,3,2,1,0:T(8,128)(2,1)}, bf16[2,4,2,256,384]{4,3,2,1,0:T(8,128)(2,1)}, u32[]{:S(2)}, u32[]{:S(2)}) collective-permute-start(bf16[2,4,2,256,384]{4,3,2,1,0:T(8,128)(2,1)} %dynamic-slice_bitcast_fusion.1), channel_id=1, source_target_pairs={{0,4},{4,0},{8,12},{12,8},{16,20},{20,16},{24,28},{28,24},{1,5},{5... | collective-permute-start | bytes 9437192 | tf_op jit(solution)/shard_map/ppermute | solution.py:959
  648.9 168.4 %reduce-scatter.5.cloned.1.call-start = ((), (), s32[]{:S(2)}) async-start(), calls=%async_computation.16 | async-start | bytes 3932160 | tf_op jit(solution)/shard_map/reduce_scatter | solution.py:1198
  740.8 164.4 %reduce-scatter.7.cloned.1.call-start = ((), (), s32[]{:S(2)}) async-start(), calls=%async_computation.17 | async-start | bytes 7864320 | tf_op jit(solution)/shard_map/reduce_scatter | solution.py:1198
  769.1 44.2 %collective-permute-start.55 = (bf16[256,2048]{1,0:T(8,128)(2,1)S(1)}, bf16[256,2048]{1,0:T(8,128)(2,1)}, u32[]{:S(2)}, u32[]{:S(2)}) collective-permute-start(bf16[256,2048]{1,0:T(8,128)(2,1)S(1)} %get-tuple-element.539), channel_id=1, source_target_pairs={{0,8},{4,12},{8,0},{12,4},{16,24},{20,28},{24,16},{28,20},{1,9},{5... | collective-permute-start | bytes 3145736 | tf_op jit(solution)/shard_map/ppermute | solution.py:959
  770.7 42.7 %collective-permute-start.56 = (bf16[256,2048]{1,0:T(8,128)(2,1)S(1)}, bf16[256,2048]{1,0:T(8,128)(2,1)}, u32[]{:S(2)}, u32[]{:S(2)}) collective-permute-start(bf16[256,2048]{1,0:T(8,128)(2,1)S(1)} %get-tuple-element.538), channel_id=1, source_target_pairs={{0,16},{4,20},{8,24},{12,28},{16,0},{20,4},{24,8},{28,12},{1,17},{... | collective-permute-start | bytes 3145736 | tf_op jit(solution)/shard_map/ppermute | solution.py:959
  772.2 43.9 %collective-permute-start.53 = (bf16[256,2048]{1,0:T(8,128)(2,1)S(1)}, bf16[256,2048]{1,0:T(8,128)(2,1)}, u32[]{:S(2)}, u32[]{:S(2)}) collective-permute-start(bf16[256,2048]{1,0:T(8,128)(2,1)S(1)} %slice.270), channel_id=1, source_target_pairs={{0,8},{4,12},{8,0},{12,4},{16,24},{20,28},{24,16},{28,20},{1,9},{5... | collective-permute-start | bytes 3145736 | tf_op jit(solution)/shard_map/ppermute | solution.py:959
  773.0 44.3 %collective-permute-start.54 = (bf16[256,2048]{1,0:T(8,128)(2,1)S(1)}, bf16[256,2048]{1,0:T(8,128)(2,1)}, u32[]{:S(2)}, u32[]{:S(2)}) collective-permute-start(bf16[256,2048]{1,0:T(8,128)(2,1)S(1)} %slice.271), channel_id=1, source_target_pairs={{0,16},{4,20},{8,24},{12,28},{16,0},{20,4},{24,8},{28,12},{1,17},{... | collective-permute-start | bytes 3145736 | tf_op jit(solution)/shard_map/ppermute | solution.py:959
  918.2 48.3 %collective-permute-start.71 = (bf16[512,2048]{1,0:T(8,128)(2,1)}, bf16[512,2048]{1,0:T(8,128)(2,1)}, u32[]{:S(2)}, u32[]{:S(2)}) collective-permute-start(bf16[512,2048]{1,0:T(8,128)(2,1)} %get-tuple-element.413), channel_id=1, source_target_pairs={{0,4},{4,0},{8,12},{12,8},{16,20},{20,16},{24,28},{28,24},{1,5},{5... | collective-permute-start | bytes 6291464 | tf_op jit(solution)/shard_map/ppermute | solution.py:959
  929.1 125.6 %reduce-scatter.11.cloned.1.call-start = ((), (), s32[]{:S(2)}) async-start(), calls=%async_computation.19 | async-start | bytes 1310720 | tf_op jit(solution)/shard_map/reduce_scatter | solution.py:1410
  966.5 103.6 %reduce-scatter.9.cloned.1.call-start = ((), (), s32[]{:S(2)}) async-start(), calls=%async_computation.18 | async-start | bytes 5242880 | tf_op jit(solution)/shard_map/reduce_scatter | solution.py:1198
  976.6 43.8 %collective-permute-start.74 = (bf16[256,2048]{1,0:T(8,128)(2,1)}, bf16[256,2048]{1,0:T(8,128)(2,1)}, u32[]{:S(2)}, u32[]{:S(2)}) collective-permute-start(bf16[256,2048]{1,0:T(8,128)(2,1)} %add_convert_fusion.12), channel_id=1, source_target_pairs={{0,8},{4,12},{8,0},{12,4},{16,24},{20,28},{24,16},{28,20},{1,9},{5... | collective-permute-start | bytes 3145736 | tf_op jit(solution)/shard_map/ppermute | solution.py:959
  985.2 46.0 %collective-permute-start.72 = (bf16[256,2048]{1,0:T(8,128)(2,1)}, bf16[256,2048]{1,0:T(8,128)(2,1)}, u32[]{:S(2)}, u32[]{:S(2)}) collective-permute-start(bf16[256,2048]{1,0:T(8,128)(2,1)} %slice.333), channel_id=1, source_target_pairs={{0,16},{4,20},{8,24},{12,28},{16,0},{20,4},{24,8},{28,12},{1,17},{... | collective-permute-start | bytes 3145736 | tf_op jit(solution)/shard_map/ppermute | solution.py:959
  (140 other events, 2036.1 us)
Sparse Core Ops, SparseCore 0:
  12.5 83.5 all-gather.7
  99.4 64.8 all-gather.9
  166.5 104.5 all-gather.11
  275.8 62.0 all-gather.13
  651.8 59.9 reduce-scatter.4
  767.3 109.6 reduce-scatter.6
  966.6 24.9 reduce-scatter.10
  994.6 75.4 reduce-scatter.8

commit v5 on v3

--- a/solution.py
+++ b/solution.py
@@ -704,7 +704,7 @@
             dimension_semantics=("arbitrary",), vmem_limit_bytes=40 << 20
         ),
         cost_estimate=pl.CostEstimate(
-            flops=rows * width * columns * 240 // 100, bytes_accessed=rows * width, transcendentals=0
+            flops=rows * width * columns * 150 // 100, bytes_accessed=rows * width, transcendentals=0
         ),
         name="project",
     )(*arrays)
@@ -763,7 +763,7 @@
             dimension_semantics=("arbitrary",), vmem_limit_bytes=40 << 20
         ),
         cost_estimate=pl.CostEstimate(
-            flops=rows * width * columns * 240 // 100, bytes_accessed=rows * width, transcendentals=0
+            flops=rows * width * columns * 150 // 100, bytes_accessed=rows * width, transcendentals=0
         ),
         name="project_back",
     )(left, right, grads, weights)
@@ -812,7 +812,7 @@
             dimension_semantics=("arbitrary",), vmem_limit_bytes=58 << 20
         ),
         cost_estimate=pl.CostEstimate(
-            flops=flops * 60 // 100, bytes_accessed=rows * width, transcendentals=0
+            flops=flops * 38 // 100, bytes_accessed=rows * width, transcendentals=0
         ),
         name="feed",
     )(*two, *cot, w_low, w_high, w_dn)
@@ -842,7 +842,7 @@
             dimension_semantics=("arbitrary",), vmem_limit_bytes=32 << 20
         ),
         cost_estimate=pl.CostEstimate(
-            flops=rows * width * size * 1920 // 100, bytes_accessed=rows * width, transcendentals=0
+            flops=rows * width * size * 1200 // 100, bytes_accessed=rows * width, transcendentals=0
         ),
         name="spread",
     )(grads, weights)
@@ -879,7 +879,7 @@
             dimension_semantics=("arbitrary",), vmem_limit_bytes=32 << 20
         ),
         cost_estimate=pl.CostEstimate(
-            flops=rows * width * size * 1920 // 100, bytes_accessed=rows * width, transcendentals=0
+            flops=rows * width * size * 1200 // 100, bytes_accessed=rows * width, transcendentals=0
         ),
         name="mix_out_grad",
     )(heads, grads)
@@ -947,7 +947,7 @@
             dimension_semantics=("arbitrary",), vmem_limit_bytes=58 << 20
         ),
         cost_estimate=pl.CostEstimate(
-            flops=count * rows * m * n * 120 // 100,
+            flops=count * rows * m * n * 75 // 100,
             bytes_accessed=rows * (m + n),
             transcendentals=0,
         ),
@@ -1144,7 +1144,7 @@
         ins=common + [(projected, "near", fv_block)],
         outs=[(tall_shape, F32, "run", tall_block)],
         scratch=[],
-        flops=27 * unit,
+        flops=17 * unit,
         name="run_states",
     )
     cot, run_state, _ = plane_gather(cot_low, run_state)
@@ -1163,7 +1163,7 @@
             ((steps,) + state_shape, F32, "block", (1,) + state_shape),
         ],
         scratch=[pltpu.VMEM(state_shape, F32)],
-        flops=45 * unit,
+        flops=28 * unit,
         name="mix_forward",
     )
     gu_second, dn_pairs, first_pairs, cot, _ = together(
@@ -1303,7 +1303,7 @@
             (runs_shape, BF16, "run", run_block),
         ],
         scratch=[pltpu.VMEM(state_shape, F32)],
-        flops=35 * unit,
+        flops=22 * unit,
         name="gate_back",
     )
     out_grad = out_grad.reshape(seq_count, all_heads, head_size // seq_count, width)
@@ -1330,7 +1330,7 @@
             ((1, chans), F32, "whole", None),
         ],
         scratch=[pltpu.VMEM(state_shape, F32)],
-        flops=69 * unit,
+        flops=43 * unit,
         name="mix_backward",
     )
     grad_projected = grad_projected.reshape(seq_count, rows, 4 * chans)

time: 1080 us -> 1080 us (level)
    unnamed x171 -> x165, local copies, waits for them, and re-layouts: 50.3 us -> 51.5 us
  transfers between devices with their start and end apart: 95 -> 95, of which waited for: 28 -> 29; matrix products, arithmetic and copies ran while one was open for 23% -> 23% of each run, Pallas kernels for 36% -> 36%
where the time goes in v5:
time: 1080 us; the launch traced here: 1070 us
  Pallas kernels  382 us (35%)
  waiting for transfers between devices  280 us (26%)
  local copies, waits for them, and re-layouts  143 us (13%)
  other arithmetic  136 us (13%)
  starting transfers between devices  98.4 us (9%)
  between operations  16 us (1%)
  matrix products  11.9 us (1%)
    pallas_call x4, Pallas kernels, feed_call(): pl.pallas_call(feed_kernel, grid=(rows // tile,), in_specs=[cut(width)] *...  115 us
    pallas_call x4, Pallas kernels, recur_call(): pl.pallas_call(kernel, grid_spec=pltpu.PrefetchScalarGridSpec(num_scalar_...  102 us
    ppermute x74, waiting for transfers between devices, swap(): lax.ppermute(value, 'seq', [(i, i ^ across) for i in range(lax.axis_size(...  90 us
    pallas_call x3, Pallas kernels, outer_call(): pl.pallas_call(functools.partial(outer_kernel, count, place), grid=(count...  77.3 us
    all_to_all x2, waiting for transfers between devices, to_scan(): return lax.all_to_all(array, 'mp', split_axis=0, concat_axis=0, tiled=True)  70.6 us
    convert_element_type x21, other arithmetic, add_low(): return (a.astype(F32) + b.astype(F32)).astype(BF16)  60.4 us
    unnamed x165, local copies, waits for them, and re-layouts  51.5 us
    ppermute x74, starting transfers between devices, swap(): lax.ppermute(value, 'seq', [(i, i ^ across) for i in range(lax.axis_size(...  50.9 us
  transfers between devices with their start and end apart: 95, of which 29 were waited for; matrix products, arithmetic and copies ran while one was open for 23% of the time, Pallas kernels for 36%

profile of v5, /device:TPU:0, one launch (start us, length us, event | category | flops | bytes accessed | tf_op | source)
XLA Modules:
  0.0 1068.3 jit_solution(12664984064015513588)
XLA Ops:
  31.3 9.0 constant_dynamic-slice_fusion.4
  43.7 25.8 %collective-permute-done.1.left.refs_2_ = bf16[512,2048]{1,0:T(8,128)(2,1)} collective-permute-done((bf16[512,2048]{1,0:T(8,128)(2,1)S(1)}, bf16[512,2048]{1,0:T(8,128)(2,1)}, u32[]{:S(2)}, u32[]{:S(2)}) %collective-permute-start.1) | collective-permute-done | bytes 2097184 | tf_op jit(solution)/shard_map/ppermute | solution.py:959
  86.6 12.6 %collective-permute-done.5 = bf16[256,2048]{1,0:T(8,128)(2,1)} collective-permute-done((bf16[256,2048]{1,0:T(8,128)(2,1)S(1)}, bf16[256,2048]{1,0:T(8,128)(2,1)}, u32[]{:S(2)}, u32[]{:S(2)}) %collective-permute-start.5) | collective-permute-done | bytes 1048608 | tf_op jit(solution)/shard_map/ppermute | solution.py:959
  118.4 8.7 project.4.rest_0_
  127.1 8.0 project.5.rest_0_
  135.1 8.0 project.6.rest_0_
  149.2 16.2 %run_states.1 = f32[2,8,2,136,128]{4,3,2,1,0:T(8,128)S(1)} custom-call(s32[4]{0:T(128)S(1)} %pad_add_fusion.where, s32[2,4]{1,0:T(2,128)S(1)} %copy-done.18, f32[1,256]{1,0:T(1,128)S(1)} %get-tuple-element.578.gap, f32[8,2,256,1024]{3,2,1,0:T(8,128)} %bitcast.245), custom_call_target="tpu_custom_call" | custom-call | flops 4563402752 | bytes 838913 | tf_op jit(solution)/shard_map/run_states/pallas_call | solution.py:640
  177.8 50.4 %all-to-all-done.decays.states = bf16[4,8,136,128]{3,2,1,0:T(8,128)(2,1)S(1)} async-done(((bf16[4,8,136,128]{3,2,1,0:T(8,128)(2,1)}), bf16[4,8,136,128]{3,2,1,0:T(8,128)(2,1)S(1)}, u32[]{:S(2)}, u32[]{:S(2)}) %all-to-all-start) | async-done | bytes 1114144 | tf_op jit(solution)/shard_map/all_to_all | solution.py:1134
  243.1 29.3 %all-to-all-done.1 = bf16[4,8,128,128]{3,2,1,0:T(8,128)(2,1)S(1)} async-done(((bf16[4,8,128,128]{3,2,1,0:T(8,128)(2,1)}), bf16[4,8,128,128]{3,2,1,0:T(8,128)(2,1)S(1)}, u32[]{:S(2)}, u32[]{:S(2)}) %all-to-all-start.1) | async-done | bytes 1048608 | tf_op jit(solution)/shard_map/all_to_all | solution.py:1137
  275.4 26.2 %mix_forward.1 = (bf16[8,2,256,256]{3,2,1,0:T(8,128)(2,1)S(1)}, f32[8,2,256,256]{3,2,1,0:T(8,128)}, f32[16,2,2,128,128]{4,3,2,1,0:T(8,128)}) custom-call(s32[4]{0:T(128)S(1)} %pad_add_fusion.where, s32[2,4]{1,0:T(2,128)S(1)} %copy-done.18, f32[1,256]{1,0:T(1,128)S(1)} %get-tuple-element.578.gap, f32[1,256]{1,0:T(1,128)S(1)} %get-tuple-element.577.gain, ...), custom_call_target="tpu_custom_call" | custom-call | flops 7516192768 | bytes 891393 | tf_op jit(solution)/shard_map/mix_forward/pallas_call | solution.py:640
  313.5 19.9 %all-to-all-done.2.heads = bf16[8,512,256]{2,1,0:T(8,128)(2,1)S(1)} async-done(((bf16[8,512,256]{2,1,0:T(8,128)(2,1)}), bf16[8,512,256]{2,1,0:T(8,128)(2,1)S(1)}, u32[]{:S(2)}, u32[]{:S(2)}) %all-to-all-start.2) | async-done | bytes 2097184 | tf_op jit(solution)/shard_map/all_to_all | solution.py:1182
  341.6 11.9 %multiply_reduce_fusion.2 = (f32[512]{0:T(512)S(1)}, f32[512,2048]{1,0:T(8,128)}) fusion(bf16[512,2048]{0,1:T(8,128)(2,1)} %bitcast.257, bf16[2048,2048]{1,0:T(8,128)(2,1)} %bitcast.232, f32[256,2,2048]{2,0,1:T(8,128)} %copy-done.24), kind=kOutput, calls=%fused_computation.36 | convolution fusion | flops 4298112512 | bytes 18876416 | tf_op jit(solution)/shard_map/dot_general | solution.py:364
  371.6 28.8 %feed.4 = (bf16[512,768]{1,0:T(8,128)(2,1)}, bf16[512,1536]{1,0:T(8,128)(2,1)}, bf16[512,2048]{1,0:T(8,128)(2,1)}, bf16[512,2048]{1,0:T(8,128)(2,1)}, bf16[512,7...) custom-call(bf16[512,2048]{1,0:T(8,128)(2,1)} %copy-done.55, ...), custom_call_target="tpu_custom_call" | custom-call | flops 7344394240 | bytes 1048576 | tf_op jit(solution)/shard_map/feed/pallas_call | solution.py:805
  400.5 11.2 %collective-permute-done.15.refs_0_.refs_2_ = bf16[512,2048]{1,0:T(8,128)(2,1)} collective-permute-done((bf16[512,2048]{1,0:T(8,128)(2,1)S(1)}, bf16[512,2048]{1,0:T(8,128)(2,1)}, u32[]{:S(2)}, u32[]{:S(2)}) %collective-permute-start.15) | collective-permute-done | bytes 2097184 | tf_op jit(solution)/shard_map/ppermute | solution.py:959
  420.2 28.8 %feed.5 = (bf16[512,768]{1,0:T(8,128)(2,1)}, bf16[512,1536]{1,0:T(8,128)(2,1)}, bf16[512,2048]{1,0:T(8,128)(2,1)}, bf16[512,2048]{1,0:T(8,128)(2,1)}, bf16[512,7...) custom-call(bf16[512,2048]{1,0:T(8,128)(2,1)} %collective-permute-done.15.ref, ...), custom_call_target="tpu_custom_call" | custom-call | flops 7344394240 | bytes 1048576 | tf_op jit(solution)/shard_map/feed/pallas_call | solution.py:805
  456.0 29.0 %feed.6 = (bf16[512,768]{1,0:T(8,128)(2,1)}, bf16[512,1536]{1,0:T(8,128)(2,1)}, bf16[512,2048]{1,0:T(8,128)(2,1)}, bf16[512,2048]{1,0:T(8,128)(2,1)}, bf16[512,7...) custom-call(bf16[512,2048]{1,0:T(8,128)(2,1)} %collective-permute-done.16.ref, ...), custom_call_target="tpu_custom_call" | custom-call | flops 7344394240 | bytes 1048576 | tf_op jit(solution)/shard_map/feed/pallas_call | solution.py:805
  496.9 28.8 %feed.7 = (bf16[512,768]{1,0:T(8,128)(2,1)}, bf16[512,1536]{1,0:T(8,128)(2,1)}, bf16[512,2048]{1,0:T(8,128)(2,1)}, bf16[512,2048]{1,0:T(8,128)(2,1)}, bf16[512,7...) custom-call(bf16[512,2048]{1,0:T(8,128)(2,1)} %copy-done.61, ...), custom_call_target="tpu_custom_call" | custom-call | flops 7344394240 | bytes 1048576 | tf_op jit(solution)/shard_map/feed/pallas_call | solution.py:805
  540.8 33.8 %gate_up_grad.1 = bf16[2,2,4,2,256,384]{5,4,3,2,1,0:T(8,128)(2,1)} custom-call(bf16[512,2048]{1,0:T(8,128)(2,1)} %copy-done.55, bf16[512,2048]{1,0:T(8,128)(2,1)} %copy-done.69, bf16[512,2048]{1,0:T(8,128)(2,1)} %collective-permute-done.15.refs_0_.refs_2_, bf16[512,2048]{1,0:T(8,128)(2,1)} %copy-done.70, ...), custom_call_target="tpu_custom_call" | custom-call | flops 9663676416 | bytes 1835008 | tf_op jit(solution)/shard_map/gate_up_grad/pallas_call | solution.py:934
  592.8 19.3 %down_grad.1 = bf16[2,2,4,384,256]{4,3,2,1,0:T(8,128)(2,1)} custom-call(bf16[512,768]{1,0:T(8,128)(2,1)} %get-tuple-element.335.refs_0_, bf16[512,768]{1,0:T(8,128)(2,1)} %get-tuple-element.336.refs_1_, bf16[512,768]{1,0:T(8,128)(2,1)} %get-tuple-element.337.refs_2_, bf16[512,768]{1,0:T(8,128)(2,1)} %get-tuple-element.338.refs_3_, ...), custom_call_target="tpu_custom_call" | custom-call | flops 4831838208 | bytes 1441792 | tf_op jit(solution)/shard_map/down_grad/pallas_call | solution.py:934
  625.0 7.4 spread.1
  667.5 10.0 all-to-all-done.3
  682.6 20.0 %gate_back.1 = (f32[8,2,256,256]{3,2,1,0:T(8,128)}, bf16[8,2,256,256]{3,2,1,0:T(8,128)(2,1)S(1)}, f32[1,256]{1,0:T(1,128)S(1)}, bf16[2,8,2,128,128]{4,3,2,1,0:T(8,128)(2,1)S(1)}) custom-call(s32[4]{0:T(128)S(1)} %pad_add_fusion.where, s32[2,4]{1,0:T(2,128)S(1)} %copy-done.18, f32[1,256]{1,0:T(1,128)S(1)} %get-tuple-element.578.gap, ...), custom_call_target="tpu_custom_call" | custom-call | flops 5905580032 | bytes 1153537 | tf_op jit(solution)/shard_map/gate_back/pallas_call | solution.py:640
  715.2 20.2 %all-to-all-done.4.states = bf16[4,8,128,128]{3,2,1,0:T(8,128)(2,1)S(1)} async-done(((bf16[4,8,128,128]{3,2,1,0:T(8,128)(2,1)}), bf16[4,8,128,128]{3,2,1,0:T(8,128)(2,1)S(1)}, u32[]{:S(2)}, u32[]{:S(2)}) %all-to-all-start.4) | async-done | bytes 1048608 | tf_op jit(solution)/shard_map/all_to_all | solution.py:1134
  749.7 19.3 %all-to-all-done.5 = bf16[4,8,128,128]{3,2,1,0:T(8,128)(2,1)S(1)} async-done(((bf16[4,8,128,128]{3,2,1,0:T(8,128)(2,1)}), bf16[4,8,128,128]{3,2,1,0:T(8,128)(2,1)S(1)}, u32[]{:S(2)}, u32[]{:S(2)}) %all-to-all-start.5) | async-done | bytes 1048608 | tf_op jit(solution)/shard_map/all_to_all | solution.py:1137
  775.5 39.7 %mix_backward.1 = (bf16[8,2,256,1024]{3,2,1,0:T(8,128)(2,1)}, f32[1,256]{1,0:T(1,128)S(1)}) custom-call(s32[4]{0:T(128)S(1)} %pad_add_fusion.where, s32[2,4]{1,0:T(2,128)S(1)} %copy-done.18, f32[1,256]{1,0:T(1,128)S(1)} %get-tuple-element.578.gap, f32[8,2,256,1024]{3,2,1,0:T(8,128)} %bitcast.248, f32[8,2,256,256]{3,2,1,0:T(8,128)} %get-tuple-element.366.grad_out, ...), custom_call_target="tpu_custom_call" | custom-call | flops 11542724608 | bytes 1415630 | tf_op jit(solution)/shard_map/mix_backward/pallas_call | solution.py:640
  830.2 24.2 %mix_in_grad.1 = bf16[2,2,4,256,512]{4,3,2,1,0:T(8,128)(2,1)} custom-call(bf16[512,2048]{1,0:T(8,128)(2,1)} %copy-done.4, bf16[512,2048]{1,0:T(8,128)(2,1)} %collective-permute-done.right.refs_1_, bf16[512,2048]{1,0:T(8,128)(2,1)} %collective-permute-done.1.left.refs_2_, bf16[512,2048]{1,0:T(8,128)(2,1)} %collective-permute-done.7.right.refs_3_, ...), custom_call_target="tpu_custom_call" | custom-call | flops 6442450944 | bytes 1572864 | tf_op jit(solution)/shard_map/mix_in_grad/pallas_call | solution.py:934
  864.3 9.1 project_back.4
  876.3 9.4 collective-permute-done.60
  890.1 9.7 project_back.5
  930.6 9.8 project_back.6
  945.5 8.4 project_back.7
  986.6 36.7 %all-to-all-done.8 = f32[8,4,256]{2,1,0:T(4,128)S(1)} async-done(((f32[8,4,256]{2,1,0:T(4,128)}), f32[8,4,256]{2,1,0:T(4,128)S(1)}, u32[]{:S(2)}, u32[]{:S(2)}) %all-to-all-start.8) | async-done | bytes 32800 | tf_op jit(solution)/shard_map/all_to_all | solution.py:1420
  (510 shorter events, 423.0 us)
Async XLA Ops:
  7.2 92.1 %all-gather.8.cloned.1.call-start = ((), (), s32[]{:S(2)}) async-start(), calls=%async_computation.15 | async-start | bytes 5242880 | tf_op jit(solution)/shard_map/all_gather | solution.py:1054
  12.4 260.2 %all-gather.10.cloned.1.call-start = ((), (), s32[]{:S(2)}) async-start(), calls=%async_computation.20 | async-start | bytes 3932160 | tf_op jit(solution)/shard_map/all_gather | solution.py:1054
  20.6 48.9 %collective-permute-start.1 = (bf16[512,2048]{1,0:T(8,128)(2,1)S(1)}, bf16[512,2048]{1,0:T(8,128)(2,1)}, u32[]{:S(2)}, u32[]{:S(2)}) collective-permute-start(bf16[512,2048]{1,0:T(8,128)(2,1)S(1)} %fusion.1.left.refs_0_), channel_id=1, source_target_pairs={{0,8},{4,12},{8,0},{12,4},{16,24},{20,28},{24,16},{28,20},{1,9},{5... | collective-permute-start | bytes 6291464 | tf_op jit(solution)/shard_map/ppermute | solution.py:959
  23.1 47.8 %collective-permute-start.2 = (bf16[512,2048]{1,0:T(8,128)(2,1)S(1)}, bf16[512,2048]{1,0:T(8,128)(2,1)}, u32[]{:S(2)}, u32[]{:S(2)}) collective-permute-start(bf16[512,2048]{1,0:T(8,128)(2,1)S(1)} %fusion.1.left.refs_0_), channel_id=1, source_target_pairs={{0,16},{4,20},{8,24},{12,28},{16,0},{20,4},{24,8},{28,12},{1,17},{... | collective-permute-start | bytes 6291464 | tf_op jit(solution)/shard_map/ppermute | solution.py:959
  99.3 173.3 %all-gather.12.cloned.1.call-start = ((), (), s32[]{:S(2)}) async-start(), calls=%async_computation.21 | async-start | bytes 3932160 | tf_op jit(solution)/shard_map/all_gather | solution.py:1054
  103.1 62.3 %collective-permute-start.12 = (bf16[512,2048]{1,0:T(8,128)(2,1)}, bf16[512,2048]{1,0:T(8,128)(2,1)}, u32[]{:S(2)}, u32[]{:S(2)}) collective-permute-start(bf16[512,2048]{1,0:T(8,128)(2,1)} %bitcast_convert_fusion.refs_2_.refs_8_), channel_id=1, source_target_pairs={{0,4},{4,0},{8,12},{12,8},{16,20},{20,16},{24,28},{28,24},{1,5},{5... | collective-permute-start | bytes 6291464 | tf_op jit(solution)/shard_map/ppermute | solution.py:959
  103.5 61.8 %collective-permute-start.13 = (bf16[512,2048]{1,0:T(8,128)(2,1)}, bf16[512,2048]{1,0:T(8,128)(2,1)}, u32[]{:S(2)}, u32[]{:S(2)}) collective-permute-start(bf16[512,2048]{1,0:T(8,128)(2,1)} %bitcast_convert_fusion.refs_2_.refs_8_), channel_id=1, source_target_pairs={{0,8},{4,12},{8,0},{12,4},{16,24},{20,28},{24,16},{28,20},{1,9},{5... | collective-permute-start | bytes 6291464 | tf_op jit(solution)/shard_map/ppermute | solution.py:959
  109.9 55.5 %collective-permute-start.14 = (bf16[512,2048]{1,0:T(8,128)(2,1)S(1)}, bf16[512,2048]{1,0:T(8,128)(2,1)}, u32[]{:S(2)}, u32[]{:S(2)}) collective-permute-start(bf16[512,2048]{1,0:T(8,128)(2,1)S(1)} %copy-done.32), channel_id=1, source_target_pairs={{0,16},{4,20},{8,24},{12,28},{16,0},{20,4},{24,8},{28,12},{1,17},{... | collective-permute-start | bytes 6291464 | tf_op jit(solution)/shard_map/ppermute | solution.py:959
  165.4 71.7 %collective-permute-start.20 = (bf16[512,2048]{1,0:T(8,128)(2,1)}, bf16[512,2048]{1,0:T(8,128)(2,1)}, u32[]{:S(2)}, u32[]{:S(2)}) collective-permute-start(bf16[512,2048]{1,0:T(8,128)(2,1)} %collective-permute-done.13.refs_2_.refs_10_), channel_id=1, source_target_pairs={{0,4},{4,0},{8,12},{12,8},{16,20},{20,16},{24,28},{28,24},{1,5},{5... | collective-permute-start | bytes 6291464 | tf_op jit(solution)/shard_map/ppermute | solution.py:959
  165.5 71.6 %collective-permute-start.21 = (bf16[512,2048]{1,0:T(8,128)(2,1)}, bf16[512,2048]{1,0:T(8,128)(2,1)}, u32[]{:S(2)}, u32[]{:S(2)}) collective-permute-start(bf16[512,2048]{1,0:T(8,128)(2,1)} %collective-permute-done.14.refs_2_.refs_12_), channel_id=1, source_target_pairs={{0,4},{4,0},{8,12},{12,8},{16,20},{20,16},{24,28},{28,24},{1,5},{5... | collective-permute-start | bytes 6291464 | tf_op jit(solution)/shard_map/ppermute | solution.py:959
  167.2 61.0 %all-to-all-start = ((bf16[4,8,136,128]{3,2,1,0:T(8,128)(2,1)}), bf16[4,8,136,128]{3,2,1,0:T(8,128)(2,1)S(1)}, u32[]{:S(2)}, u32[]{:S(2)}) async-start(bf16[4,8,136,128]{3,2,1,0:T(8,128)(2,1)} %bitcast.28), calls=%async_computation | async-start | bytes 2228224 | tf_op jit(solution)/shard_map/all_to_all | solution.py:1134
  175.8 61.3 %collective-permute-start.18 = (bf16[256,2048]{1,0:T(8,128)(2,1)}, bf16[256,2048]{1,0:T(8,128)(2,1)}, u32[]{:S(2)}, u32[]{:S(2)}) collective-permute-start(bf16[256,2048]{1,0:T(8,128)(2,1)} %slice.250), channel_id=1, source_target_pairs={{0,8},{4,12},{8,0},{12,4},{16,24},{20,28},{24,16},{28,20},{1,9},{5... | collective-permute-start | bytes 3145736 | tf_op jit(solution)/shard_map/ppermute | solution.py:959
  177.4 59.6 %collective-permute-start.19 = (bf16[256,2048]{1,0:T(8,128)(2,1)S(1)}, bf16[256,2048]{1,0:T(8,128)(2,1)}, u32[]{:S(2)}, u32[]{:S(2)}) collective-permute-start(bf16[256,2048]{1,0:T(8,128)(2,1)S(1)} %slice.251), channel_id=1, source_target_pairs={{0,16},{4,20},{8,24},{12,28},{16,0},{20,4},{24,8},{28,12},{1,17},{... | collective-permute-start | bytes 3145736 | tf_op jit(solution)/shard_map/ppermute | solution.py:959
  237.1 116.4 %all-gather.14.cloned.1.call-start = ((), (), s32[]{:S(2)}) async-start(), calls=%async_computation.22 | async-start | bytes 3932160 | tf_op jit(solution)/shard_map/all_gather | solution.py:1054
  309.8 48.7 %collective-permute-start.24 = (bf16[2,1024,384]{2,1,0:T(8,128)(2,1)}, bf16[2,1024,384]{2,1,0:T(8,128)(2,1)}, u32[]{:S(2)}, u32[]{:S(2)}) collective-permute-start(bf16[2,1024,384]{2,1,0:T(8,128)(2,1)} %dynamic-slice_bitcast_fusion.8), channel_id=1, source_target_pairs={{0,4},{4,0},{8,12},{12,8},{16,20},{20,16},{24,28},{28,24},{1,5},{5... | collective-permute-start | bytes 4718600 | tf_op jit(solution)/shard_map/ppermute | solution.py:959
  363.6 48.1 %collective-permute-start.15 = (bf16[512,2048]{1,0:T(8,128)(2,1)S(1)}, bf16[512,2048]{1,0:T(8,128)(2,1)}, u32[]{:S(2)}, u32[]{:S(2)}) collective-permute-start(bf16[512,2048]{1,0:T(8,128)(2,1)S(1)} %multiply_convert_fusion.refs_0_), channel_id=1, source_target_pairs={{0,8},{4,12},{8,0},{12,4},{16,24},{20,28},{24,16},{28,20},{1,9},{5... | collective-permute-start | bytes 6291464 | tf_op jit(solution)/shard_map/ppermute | solution.py:959
  364.2 47.7 %collective-permute-start.16 = (bf16[512,2048]{1,0:T(8,128)(2,1)S(1)}, bf16[512,2048]{1,0:T(8,128)(2,1)}, u32[]{:S(2)}, u32[]{:S(2)}) collective-permute-start(bf16[512,2048]{1,0:T(8,128)(2,1)S(1)} %multiply_convert_fusion.refs_0_), channel_id=1, source_target_pairs={{0,16},{4,20},{8,24},{12,28},{16,0},{20,4},{24,8},{28,12},{1,17},{... | collective-permute-start | bytes 6291464 | tf_op jit(solution)/shard_map/ppermute | solution.py:959
  411.9 44.1 %collective-permute-start.31 = (bf16[512,2048]{1,0:T(8,128)(2,1)}, bf16[512,2048]{1,0:T(8,128)(2,1)}, u32[]{:S(2)}, u32[]{:S(2)}) collective-permute-start(bf16[512,2048]{1,0:T(8,128)(2,1)} %collective-permute-done.16.refs_0_.refs_4_), channel_id=1, source_target_pairs={{0,4},{4,0},{8,12},{12,8},{16,20},{20,16},{24,28},{28,24},{1,5},{5... | collective-permute-start | bytes 6291464 | tf_op jit(solution)/shard_map/ppermute | solution.py:959
  535.6 44.8 %collective-permute-start.36 = (bf16[256,2048]{1,0:T(8,128)(2,1)}, bf16[256,2048]{1,0:T(8,128)(2,1)S(1)}, u32[]{:S(2)}, u32[]{:S(2)}) collective-permute-start(bf16[256,2048]{1,0:T(8,128)(2,1)} %slice.262), channel_id=1, source_target_pairs={{0,8},{4,12},{8,0},{12,4},{16,24},{20,28},{24,16},{28,20},{1,9},{5... | collective-permute-start | bytes 3145736 | tf_op jit(solution)/shard_map/ppermute | solution.py:959
  592.8 149.9 %collective-permute-start.52 = (bf16[2,4,2,256,384]{4,3,2,1,0:T(8,128)(2,1)}, bf16[2,4,2,256,384]{4,3,2,1,0:T(8,128)(2,1)}, u32[]{:S(2)}, u32[]{:S(2)}) collective-permute-start(bf16[2,4,2,256,384]{4,3,2,1,0:T(8,128)(2,1)} %dynamic-slice_bitcast_fusion.1), channel_id=1, source_target_pairs={{0,4},{4,0},{8,12},{12,8},{16,20},{20,16},{24,28},{28,24},{1,5},{5... | collective-permute-start | bytes 9437192 | tf_op jit(solution)/shard_map/ppermute | solution.py:959
  650.9 168.2 %reduce-scatter.5.cloned.1.call-start = ((), (), s32[]{:S(2)}) async-start(), calls=%async_computation.16 | async-start | bytes 3932160 | tf_op jit(solution)/shard_map/reduce_scatter | solution.py:1198
  742.7 160.2 %reduce-scatter.7.cloned.1.call-start = ((), (), s32[]{:S(2)}) async-start(), calls=%async_computation.17 | async-start | bytes 7864320 | tf_op jit(solution)/shard_map/reduce_scatter | solution.py:1198
  770.9 44.3 %collective-permute-start.55 = (bf16[256,2048]{1,0:T(8,128)(2,1)S(1)}, bf16[256,2048]{1,0:T(8,128)(2,1)}, u32[]{:S(2)}, u32[]{:S(2)}) collective-permute-start(bf16[256,2048]{1,0:T(8,128)(2,1)S(1)} %get-tuple-element.541), channel_id=1, source_target_pairs={{0,8},{4,12},{8,0},{12,4},{16,24},{20,28},{24,16},{28,20},{1,9},{5... | collective-permute-start | bytes 3145736 | tf_op jit(solution)/shard_map/ppermute | solution.py:959
  774.8 44.3 %collective-permute-start.54 = (bf16[256,2048]{1,0:T(8,128)(2,1)S(1)}, bf16[256,2048]{1,0:T(8,128)(2,1)}, u32[]{:S(2)}, u32[]{:S(2)}) collective-permute-start(bf16[256,2048]{1,0:T(8,128)(2,1)S(1)} %slice.271), channel_id=1, source_target_pairs={{0,16},{4,20},{8,24},{12,28},{16,0},{20,4},{24,8},{28,12},{1,17},{... | collective-permute-start | bytes 3145736 | tf_op jit(solution)/shard_map/ppermute | solution.py:959
  830.1 210.2 %reduce-scatter.9.cloned.1.call-start = ((), (), s32[]{:S(2)}) async-start(), calls=%async_computation.18 | async-start | bytes 5242880 | tf_op jit(solution)/shard_map/reduce_scatter | solution.py:1198
  961.5 65.6 %collective-permute-start.68 = (bf16[256,2048]{1,0:T(8,128)(2,1)}, bf16[256,2048]{1,0:T(8,128)(2,1)S(1)}, u32[]{:S(2)}, u32[]{:S(2)}) collective-permute-start(bf16[256,2048]{1,0:T(8,128)(2,1)} %slice.330), channel_id=1, source_target_pairs={{0,8},{4,12},{8,0},{12,4},{16,24},{20,28},{24,16},{28,20},{1,9},{5... | collective-permute-start | bytes 3145736 | tf_op jit(solution)/shard_map/ppermute | solution.py:959
  964.8 58.5 %collective-permute-start.75 = (bf16[512,2048]{1,0:T(8,128)(2,1)}, bf16[512,2048]{1,0:T(8,128)(2,1)}, u32[]{:S(2)}, u32[]{:S(2)}) collective-permute-start(bf16[512,2048]{1,0:T(8,128)(2,1)} %copy-done.21), channel_id=1, source_target_pairs={{0,4},{4,0},{8,12},{12,8},{16,20},{20,16},{24,28},{28,24},{1,5},{5... | collective-permute-start | bytes 6291464 | tf_op jit(solution)/shard_map/ppermute | solution.py:959
  967.8 59.3 %collective-permute-start.74 = (bf16[256,2048]{1,0:T(8,128)(2,1)}, bf16[256,2048]{1,0:T(8,128)(2,1)}, u32[]{:S(2)}, u32[]{:S(2)}) collective-permute-start(bf16[256,2048]{1,0:T(8,128)(2,1)} %add_convert_fusion.12), channel_id=1, source_target_pairs={{0,8},{4,12},{8,0},{12,4},{16,24},{20,28},{24,16},{28,20},{1,9},{5... | collective-permute-start | bytes 3145736 | tf_op jit(solution)/shard_map/ppermute | solution.py:959
  974.9 52.1 %collective-permute-start.73 = (bf16[256,2048]{1,0:T(8,128)(2,1)}, bf16[256,2048]{1,0:T(8,128)(2,1)}, u32[]{:S(2)}, u32[]{:S(2)}) collective-permute-start(bf16[256,2048]{1,0:T(8,128)(2,1)} %add_convert_fusion.13), channel_id=1, source_target_pairs={{0,16},{4,20},{8,24},{12,28},{16,0},{20,4},{24,8},{28,12},{1,17},{... | collective-permute-start | bytes 3145736 | tf_op jit(solution)/shard_map/ppermute | solution.py:959
  975.9 51.1 %collective-permute-start.72 = (bf16[256,2048]{1,0:T(8,128)(2,1)}, bf16[256,2048]{1,0:T(8,128)(2,1)}, u32[]{:S(2)}, u32[]{:S(2)}) collective-permute-start(bf16[256,2048]{1,0:T(8,128)(2,1)} %slice.333), channel_id=1, source_target_pairs={{0,16},{4,20},{8,24},{12,28},{16,0},{20,4},{24,8},{28,12},{1,17},{... | collective-permute-start | bytes 3145736 | tf_op jit(solution)/shard_map/ppermute | solution.py:959
  979.1 44.1 %all-to-all-start.8 = ((f32[8,4,256]{2,1,0:T(4,128)}), f32[8,4,256]{2,1,0:T(4,128)S(1)}, u32[]{:S(2)}, u32[]{:S(2)}) async-start(f32[8,4,256]{2,1,0:T(4,128)} %copy.125), calls=%async_computation.10 | async-start | bytes 65536 | tf_op jit(solution)/shard_map/all_to_all | solution.py:1420
  982.5 71.6 %reduce-scatter.11.cloned.1.call-start = ((), (), s32[]{:S(2)}) async-start(), calls=%async_computation.19 | async-start | bytes 1310720 | tf_op jit(solution)/shard_map/reduce_scatter | solution.py:1415
  (136 other events, 2088.1 us)
Sparse Core Ops, SparseCore 0:
  12.5 83.5 all-gather.7
  99.4 64.8 all-gather.9
  166.5 105.1 all-gather.11
  273.2 61.5 all-gather.13
  653.8 59.9 reduce-scatter.4
  769.2 109.7 reduce-scatter.6
  903.1 75.4 reduce-scatter.8
  986.7 26.4 reduce-scatter.10
